TPU v7x, 128 devices: a whole 4x4x4 slice. The times are simulated.
128 devices in a mesh: node: 8 (over y, core), local: 16 (over z, x).
Axes of the slice: x: 4, y: 4, z: 4, core: 2. Of those that a mesh axis runs over, the one named last changes fastest.
Arguments:
- tokens: bfloat16 [98304, 8192], P(('node', 'local')), may hold values from -24 to 24
- out_grads: bfloat16 [98304, 1024], P(('node', 'local')), may hold values from -0.21582031 to 0.21582031
- master: float32 [8192, 1024], P(('node', 'local')), may hold values from -6 to 6
- moment: float32 [8192, 1024], P(('node', 'local')), may hold values from -18 to 18
- second: float32 [8192, 1024], P(('node', 'local')), may hold values from 0.1 to 100
Outputs:
- new_master: float32 [8192, 1024], P(('node', 'local'))
- new_moment: float32 [8192, 1024], P(('node', 'local'))
- new_second: float32 [8192, 1024], P(('node', 'local'))
- weight_copy: bfloat16 [8, 1024, 1024], P(None, 'local')
All inputs are finite; a program needn't handle non-finite values. Where the computation divides by a largest or mean magnitude, that divisor is 1e-20 or more.
Results may differ from a plain program's by a relative error of at most 0.001.
Values may be sent and summed in bfloat16 or wider, within the bound.
No kernel may reach another device: no remote copies, remote signals or barrier semaphores. Data moves between devices by JAX's collectives and lax.ppermute only.
A program may use at most 256 MiB of HBM per device.

v0:
```python
import jax
import jax.numpy as jnp
from jax import lax
from jax.sharding import PartitionSpec as P

KV = 1024
QBLOCK = 128


def quantize(values):
    shape = values.shape
    blocks = values.reshape(shape[:-1] + (shape[-1] // QBLOCK, QBLOCK))
    scale = (jnp.max(jnp.abs(blocks), axis=-1) + 1e-06).astype(jnp.bfloat16)
    codes = (blocks / scale.astype(jnp.float32)[..., None]).astype(jnp.bfloat16)
    return (codes.reshape(shape), scale)


def restore(codes, scale):
    shape = codes.shape
    blocks = codes.astype(jnp.float32).reshape(shape[:-1] + (shape[-1] // QBLOCK, QBLOCK))
    return (blocks * scale.astype(jnp.float32)[..., None]).reshape(shape)


def local(tokens, out_grads, master, moment, second):
    groups = lax.axis_size("node")
    members = lax.axis_size("local")
    rows = master.shape[0]
    grad_full = lax.dot_general(
        tokens, out_grads, (((0,), (0,)), ((), ())), preferred_element_type=jnp.float32
    )
    codes, scale = quantize(grad_full)
    codes = codes.reshape(groups, members, rows, KV)
    scale = scale.reshape(groups, members, rows, KV // QBLOCK)
    codes, scale = (
        lax.all_to_all(codes, "local", split_axis=1, concat_axis=1, tiled=True),
        lax.all_to_all(scale, "local", split_axis=1, concat_axis=1, tiled=True),
    )
    partial_sum = jnp.sum(restore(codes, scale), axis=1)
    codes_two, scale_two = quantize(partial_sum)
    codes_two, scale_two = (
        lax.all_to_all(codes_two, "node", split_axis=0, concat_axis=0, tiled=True),
        lax.all_to_all(scale_two, "node", split_axis=0, concat_axis=0, tiled=True),
    )
    grad_rows = jnp.sum(restore(codes_two, scale_two), axis=0)
    new_moment = 0.9 * moment + 0.1 * grad_rows
    new_second = 0.95 * second + 0.05 * grad_rows * grad_rows
    first_fix = 1.0 - 0.9**10
    second_fix = 1.0 - 0.95**10
    update = new_moment / first_fix / (jnp.sqrt(new_second / second_fix) + 1e-08) + 0.1 * master
    new_master = master - 0.05 * update
    weight_copy = lax.all_gather(new_master.astype(jnp.bfloat16)[None], "node", axis=0, tiled=True)
    return (new_master, new_moment, new_second, weight_copy)


def solution(mesh):
    return jax.shard_map(
        local,
        mesh=mesh,
        in_specs=(
            P(("node", "local"), None),
            P(("node", "local"), None),
            P(("node", "local"), None),
            P(("node", "local"), None),
            P(("node", "local"), None),
        ),
        out_specs=(
            P(("node", "local"), None),
            P(("node", "local"), None),
            P(("node", "local"), None),
            P(None, "local", None),
        ),
        check_vma=False,
    )
```

profile of v0, /device:TPU:1, one launch (start us, length us, event | category | flops | bytes accessed | tf_op | source)
XLA Modules:
  0.0 530.4 jit_solution(13034215371942390461)
XLA Ops:
  7.2 0.0 copy-start
  7.2 1.4 copy-done
  8.6 21.9 %fusion.3 = f32[8192,1024]{1,0:T(8,128)} fusion(bf16[768,8192]{1,0:T(8,128)(2,1)} %param.5, bf16[768,1024]{1,0:T(8,128)(2,1)S(1)} %copy-done), kind=kOutput, calls=%fused_computation.14 | convolution fusion | flops 12884901888 | bytes 47710208 | tf_op jit(solution)/shard_map/dot_general | solution.py:28
  30.5 12.8 %abs_bitcast_fusion = f32[1024,8,8,128]{3,1,2,0:T(8,128)S(1)} fusion(f32[8192,1024]{1,0:T(8,128)} %fusion.3), kind=kLoop, calls=%fused_computation.2 | loop fusion | flops 8388608 | bytes 67108864
  43.3 14.8 %copy.39 = f32[1024,8,8,128]{3,2,1,0:T(8,128)} copy(f32[1024,8,8,128]{3,1,2,0:T(8,128)S(1)} %abs_bitcast_fusion) | data formatting | bytes 67108864
  58.1 19.7 %reduce_max.18 = f32[8192,8]{1,0:T(8,128)} reduce(f32[8192,8,128]{2,1,0:T(8,128)} %bitcast.31, f32[]{:T(128)} %constant.2.clone.1), dimensions={2}, to_apply=%region_0.0 | reduce | flops 8323072 | bytes 33816580 | tf_op jit(solution)/shard_map/reduce_max | solution.py:13
  77.9 2.8 copy.31
  80.7 0.2 convert_element_type.59
  80.9 0.2 copy.42
  81.1 0.9 reshape.43
  82.0 8.4 %all-to-all-start.1 = ((bf16[16,2,2048]{2,1,0:T(2,128)(2,1)}), bf16[16,2,2048]{2,1,0:T(2,128)(2,1)S(1)}, u32[]{:S(2)}, u32[]{:S(2)}) async-start(bf16[16,2,2048]{2,1,0:T(2,128)(2,1)} %reshape.43), calls=%async_computation.1 | async-start | bytes 262144 | tf_op jit(solution)/shard_map/all_to_all | solution.py:36
  90.5 2.4 copy.32
  92.9 17.1 %div.37 = f32[8192,8,128]{2,1,0:T(8,128)} broadcast(f32[8192,8]{1,0:T(8,128)} %copy.32), dimensions={0,1} | broadcast | bytes 33816576 | tf_op jit(solution)/shard_map/div | solution.py:14
  110.0 35.4 %div.38 = f32[8,16,64,1024]{3,2,1,0:T(8,128)} reshape(f32[8192,8,128]{2,1,0:T(8,128)} %div.37) | data formatting | bytes 67108864 | tf_op jit(solution)/shard_map/div | solution.py:14
  145.4 27.7 %divide_convert_fusion = bf16[8,16,64,1024]{3,2,1,0:T(8,128)(2,1)} fusion(f32[8,16,64,1024]{3,2,1,0:T(8,128)} %bitcast.30, f32[8,16,64,1024]{3,2,1,0:T(8,128)} %div.38), kind=kLoop, calls=%fused_computation.1 | loop fusion | flops 16777216 | bytes 83886080 | tf_op jit(solution)/shard_map/convert_element_type | solution.py:14
  173.1 14.1 %copy.33 = bf16[8,16,64,1024]{3,2,0,1:T(8,128)(2,1)} copy(bf16[8,16,64,1024]{3,2,1,0:T(8,128)(2,1)} %divide_convert_fusion) | data formatting | bytes 33554432 | tf_op jit(solution)/shard_map/convert_element_type | solution.py:14
  187.2 0.0 all-to-all-done.1
  187.2 6.7 %all-to-all-start = ((bf16[8,16,64,1024]{3,2,0,1:T(8,128)(2,1)}), bf16[8,16,64,1024]{3,2,0,1:T(8,128)(2,1)}, u32[]{:S(2)}, u32[]{:S(2)}) async-start(bf16[8,16,64,1024]{3,2,0,1:T(8,128)(2,1)} %copy.33), calls=%async_computation | async-start | bytes 33554432 | tf_op jit(solution)/shard_map/all_to_all | solution.py:35
  193.9 0.2 reshape.44
  194.1 2.3 copy.35
  196.5 12.8 %mul.51 = f32[8,16,64,8,128]{4,3,2,0,1:T(8,128)} broadcast(f32[8,16,64,8]{3,2,0,1:T(8,128)} %copy.35), dimensions={0,1,2,3} | broadcast | bytes 33816576 | tf_op jit(solution)/shard_map/mul | solution.py:21
  209.2 35.5 %mul.52 = f32[8,16,64,1024]{3,2,0,1:T(8,128)} reshape(f32[8,16,64,8,128]{4,3,2,0,1:T(8,128)} %mul.51) | data formatting | bytes 67108864 | tf_op jit(solution)/shard_map/mul | solution.py:21
  244.7 194.9 %all-to-all-done = bf16[8,16,64,1024]{3,2,0,1:T(8,128)(2,1)} async-done(((bf16[8,16,64,1024]{3,2,0,1:T(8,128)(2,1)}), bf16[8,16,64,1024]{3,2,0,1:T(8,128)(2,1)}, u32[]{:S(2)}, u32[]{:S(2)}) %all-to-all-start) | async-done | bytes 16777248 | tf_op jit(solution)/shard_map/all_to_all | solution.py:35
  439.6 16.8 %multiply_reduce_fusion = f32[8,64,1024]{2,1,0:T(8,128)S(1)} fusion(f32[8,16,64,1024]{3,2,0,1:T(8,128)} %mul.52, bf16[8,16,64,1024]{3,2,0,1:T(8,128)(2,1)} %all-to-all-done), kind=kLoop, calls=%fused_computation | loop fusion | flops 24641536 | bytes 52428800 | tf_op jit(solution)/shard_map/reduce_sum | solution.py:38
  456.5 0.0 copy-start.2
  456.5 1.3 copy-done.2
  457.8 0.2 abs.14
  458.0 0.5 copy.40
  458.5 0.6 bitcast_reduce_fusion
  459.1 0.0 copy-start.3
  459.1 0.0 copy-start.4
  459.2 0.1 copy.36
  459.3 0.1 copy.37
  459.4 0.0 copy-start.1
  459.4 1.9 div.40
  461.3 2.7 div.41
  464.0 0.7 reshape.45
  464.7 6.8 %all-to-all-start.3 = ((bf16[8,2,256]{2,1,0:T(2,128)(2,1)}), bf16[8,2,256]{2,1,0:T(2,128)(2,1)S(1)}, u32[]{:S(2)}, u32[]{:S(2)}) async-start(bf16[8,2,256]{2,1,0:T(2,128)(2,1)} %reshape.45), calls=%async_computation.3 | async-start | bytes 16384 | tf_op jit(solution)/shard_map/all_to_all | solution.py:42
  471.5 3.6 divide_convert_fusion.1
  475.1 1.0 all-to-all-done.3
  476.1 4.2 all-to-all-start.2
  480.3 0.0 all-gather.3.cloned.1.call-start
  480.3 0.1 reshape.46
  480.3 0.1 copy.38
  480.5 1.9 mul.54
  482.4 2.7 mul.55
  485.1 10.3 %all-to-all-done.2 = bf16[8,64,1024]{2,1,0:T(8,128)(2,1)S(1)} async-done(((bf16[8,64,1024]{2,1,0:T(8,128)(2,1)}), bf16[8,64,1024]{2,1,0:T(8,128)(2,1)S(1)}, u32[]{:S(2)}, u32[]{:S(2)}) %all-to-all-start.2) | async-done | bytes 1048608 | tf_op jit(solution)/shard_map/all_to_all | solution.py:41
  495.4 1.9 multiply_reduce_fusion.1
  497.3 0.0 copy-done.3
  497.3 0.0 copy-done.4
  497.3 2.0 fusion.1
  499.3 0.0 all-gather.3.cloned.1.call-update
  499.3 22.0 %all-gather.3.cloned.1.call-done = bf16[512,1024]{1,0:T(8,128)(2,1)} async-done(((bf16[64,1024]{1,0:T(8,128)(2,1)}), bf16[512,1024]{1,0:T(8,128)(2,1)}) %all-gather.3.cloned.1.call-update) | async-done | bytes 1048592 | tf_op jit(solution)/shard_map/all_gather | solution.py:51
  521.3 2.3 copy.44
  523.6 0.0 copy-done.1
  (3 shorter events, 0.1 us)
Async XLA Ops:
  7.2 1.4 copy-start
  82.0 105.2 %all-to-all-start.1 = ((bf16[16,2,2048]{2,1,0:T(2,128)(2,1)}), bf16[16,2,2048]{2,1,0:T(2,128)(2,1)S(1)}, u32[]{:S(2)}, u32[]{:S(2)}) async-start(bf16[16,2,2048]{2,1,0:T(2,128)(2,1)} %reshape.43), calls=%async_computation.1 | async-start | bytes 262144 | tf_op jit(solution)/shard_map/all_to_all | solution.py:36
  187.2 252.4 %all-to-all-start = ((bf16[8,16,64,1024]{3,2,0,1:T(8,128)(2,1)}), bf16[8,16,64,1024]{3,2,0,1:T(8,128)(2,1)}, u32[]{:S(2)}, u32[]{:S(2)}) async-start(bf16[8,16,64,1024]{3,2,0,1:T(8,128)(2,1)} %copy.33), calls=%async_computation | async-start | bytes 33554432 | tf_op jit(solution)/shard_map/all_to_all | solution.py:35
  456.5 1.3 copy-start.2
  459.1 38.2 %copy-start.3 = (f32[64,1024]{1,0:T(8,128)S(1)}, f32[64,1024]{1,0:T(8,128)}, u32[]{:S(2)}) copy-start(f32[64,1024]{1,0:T(8,128)} %param.7) | copy-start | bytes 786436
  459.1 38.2 %copy-start.4 = (f32[64,1024]{1,0:T(8,128)S(1)}, f32[64,1024]{1,0:T(8,128)}, u32[]{:S(2)}) copy-start(f32[64,1024]{1,0:T(8,128)} %param.8) | copy-start | bytes 786436
  459.4 64.2 %copy-start.1 = (bf16[768,1024]{1,0:T(8,128)(2,1)S(1)}, bf16[768,1024]{1,0:T(8,128)(2,1)}, u32[]{:S(2)}) copy-start(bf16[768,1024]{1,0:T(8,128)(2,1)} %param.6) | copy-start | bytes 4718596
  464.7 11.4 %all-to-all-start.3 = ((bf16[8,2,256]{2,1,0:T(2,128)(2,1)}), bf16[8,2,256]{2,1,0:T(2,128)(2,1)S(1)}, u32[]{:S(2)}, u32[]{:S(2)}) async-start(bf16[8,2,256]{2,1,0:T(2,128)(2,1)} %reshape.45), calls=%async_computation.3 | async-start | bytes 16384 | tf_op jit(solution)/shard_map/all_to_all | solution.py:42
  476.1 19.3 %all-to-all-start.2 = ((bf16[8,64,1024]{2,1,0:T(8,128)(2,1)}), bf16[8,64,1024]{2,1,0:T(8,128)(2,1)S(1)}, u32[]{:S(2)}, u32[]{:S(2)}) async-start(bf16[8,64,1024]{2,1,0:T(8,128)(2,1)} %divide_convert_fusion.1), calls=%async_computation.2 | async-start | bytes 2097152 | tf_op jit(solution)/shard_map/all_to_all | solution.py:41
  480.3 41.1 %all-gather.3.cloned.1.call-start = ((), (), s32[]{:S(2)}) async-start(), calls=%async_computation.4 | async-start | bytes 1179648 | tf_op jit(solution)/shard_map/all_gather | solution.py:51
Sparse Core Ops, SparseCore 0:
  499.5 21.8 all-gather.2
where the time goes:
time: 533 us; the launch traced here: 530 us
  waiting for transfers between devices  228 us (43%)
  local copies, waits for them, and re-layouts  155 us (29%)
  other arithmetic  85.4 us (16%)
  starting transfers between devices  26.1 us (5%)
  matrix products  21.9 us (4%)
  between operations  14.2 us (3%)
    all_to_all x1, waiting for transfers between devices, local(): lax.all_to_all(codes, 'local', split_axis=1, concat_axis=1, tiled=True)  195 us
    div x4, local copies, waits for them, and re-layouts, quantize(): codes = (blocks / scale.astype(jnp.float32)[..., None]).astype(jnp.bfloat16)  57.1 us
    mul x4, local copies, waits for them, and re-layouts, restore(): return (blocks * scale.astype(jnp.float32)[..., None]).reshape(shape)  52.9 us
    convert_element_type x2, other arithmetic, quantize(): codes = (blocks / scale.astype(jnp.float32)[..., None]).astype(jnp.bfloat16)  31.3 us
    unnamed x17, local copies, waits for them, and re-layouts  22.2 us
    all_gather x1, waiting for transfers between devices, local(): lax.all_gather(new_master.astype(jnp.bfloat16)[None], 'node', axis=0, til...  22 us
    dot_general x1, matrix products, local(): lax.dot_general(tokens, out_grads, (((0,), (0,)), ((), ())), preferred_el...  21.9 us
    reduce_max x2, other arithmetic, quantize(): scale = (jnp.max(jnp.abs(blocks), axis=-1) + 1e-06).astype(jnp.bfloat16)  20.3 us
  transfers between devices with their start and end apart: 5, of which 4 were waited for; matrix products, arithmetic and copies ran while one was open for 29% of the time, Pallas kernels for 0%

commit v1 on v0

v1 whole, which is shorter than its diff:
```python
import functools

import jax
import jax.numpy as jnp
from jax import lax
from jax.experimental import pallas as pl
from jax.experimental.pallas import tpu as pltpu
from jax.sharding import PartitionSpec as P

D = 8192
KV = 1024
TOK = 768
CHUNKS = 2
KVC = KV // CHUNKS
KB = KVC // 128
F32 = jnp.float32
BF16 = jnp.bfloat16
MIB = 1 << 20

MATCH = ((1, 0, 3, 2), (3, 2, 1, 0))


def bits(v):
    b = lax.shift_right_logical(v, 1)
    return (v ^ b) & 1, b


def local_perm(dim):
    m = MATCH[dim % 2]
    if dim < 2:
        return [(z * 4 + x, z * 4 + m[x]) for z in range(4) for x in range(4)]
    return [(z * 4 + x, m[z] * 4 + x) for z in range(4) for x in range(4)]


def y_perm(k):
    return [(n, ((n // 2 + k) % 4) * 2 + n % 2) for n in range(8)]


CORE_PERM = [(n, n ^ 1) for n in range(8)]


def pad16(n):
    return -(-n // 16) * 16


def code_rows(tiles):
    return tiles * KVC


def msg_rows(tiles):
    return tiles * KVC + pad16(tiles * KB)


def params(mib):
    return pltpu.CompilerParams(vmem_limit_bytes=mib * MIB)


def vmem():
    return pl.BlockSpec(memory_space=pltpu.VMEM)


def quantize(m):
    top = jnp.max(jnp.abs(m), axis=0, keepdims=True) + 1e-06
    scale = top.astype(BF16).astype(F32)
    return (m * (1.0 / scale)).astype(BF16), scale


def encode(m):
    top = jnp.max(jnp.abs(m), axis=0, keepdims=True) + 1e-30
    scale = top.astype(BF16).astype(F32)
    e = jnp.exp2(jnp.abs(m) * (250.0 / scale) - 125.0)
    return jnp.where(m < 0, -e, e).astype(BF16), scale


def decode(code, scale):
    y = code.astype(F32)
    m = (jnp.log2(jnp.abs(y)) + 125.0) * (scale * (1.0 / 250.0))
    return jnp.where(y < 0, -m, m)


def first_kernel(part, tok, og, send, keep, tokv, ogt, sc_send, sc_keep, sem):
    order = [(part + s) % 4 for s in range(4)]
    me_l = lax.axis_index("local")
    me_n = lax.axis_index("node")
    yp = (lax.shift_right_logical(me_n, 1) + part) & 3
    ax, bx = bits(me_l & 3)
    az, bz = bits(lax.shift_right_logical(me_l, 2))
    copies = []
    for q in range(4):
        b = (q >> 1) ^ bz
        z = 2 * b + ((q & 1) ^ az ^ b)
        for c in range(2):
            start = pl.multiple_of((yp * 2 + c) * 1024 + z * 256, 256)
            cp = pltpu.make_async_copy(tok.at[:, pl.ds(start, 256)], tokv.at[q, c], sem.at[q, c])
            cp.start()
            copies.append(cp)
    ogt[...] = og[...].T
    for q in range(4):
        copies[2 * q].wait()
        copies[2 * q + 1].wait()

    def pair(rel):
        xh = rel[1] ^ bx
        q = rel[2] + 2 * rel[3]
        lanes = pl.ds(pl.multiple_of(xh * 128, 128), 128)
        t0 = tokv[q, 0, :, lanes]
        t1 = tokv[q, 1, :, lanes]
        swap = (xh ^ ax) == 1
        even = jnp.concatenate([t0[:, :64], t1[:, :64]], axis=1)
        odd = jnp.concatenate([t0[:, 64:], t1[:, 64:]], axis=1)
        both = jnp.concatenate([jnp.where(swap, odd, even), jnp.where(swap, even, odd)], axis=1)
        g = jnp.dot(ogt[...], both, preferred_element_type=F32)
        for k in range(KB):
            code, scale = quantize(g[k * 128:(k + 1) * 128])
            for a in range(2):
                bit = {0: a, 1: rel[1], 2: rel[2], 3: rel[3]}
                out, sc = (send, sc_send) if bit[order[0]] is ONE or (order[0] == 0 and a == 1) else (keep, sc_keep)
                pos = bit[order[1]] * 4 + bit[order[2]] * 2 + bit[order[3]]
                row = pl.multiple_of(pos * KVC + k * 128, 128)
                out[pl.ds(row, 128), :] = code[:, a * 128:(a + 1) * 128]
                sc[pl.ds(pos * KB + k, 1), :] = scale[:, a * 128:(a + 1) * 128]

    if order[0] == 0:
        def body(t, _):
            pair({1: t & 1, 2: lax.shift_right_logical(t, 1) & 1, 3: lax.shift_right_logical(t, 2)})
            return 0
        lax.fori_loop(0, 8, body, 0)
    else:
        rest = [d for d in (1, 2, 3) if d != order[0]]

        def body(t, _):
            for v in (ONE, ZERO):
                pair({order[0]: v, rest[0]: t & 1, rest[1]: lax.shift_right_logical(t, 1)})
            return 0
        lax.fori_loop(0, 4, body, 0)
    send[code_rows(8):, :] = sc_send[...].astype(BF16)
    keep[code_rows(8):, :] = sc_keep[...].astype(BF16)


class Bit(int):
    pass


ZERO, ONE = Bit(0), Bit(1)


def first_stage(tokens, og, part):
    out = jax.ShapeDtypeStruct((msg_rows(8), 128), BF16)
    return pl.pallas_call(
        functools.partial(first_kernel, part),
        out_shape=(out, out),
        in_specs=[pl.BlockSpec(memory_space=pl.ANY), vmem()],
        out_specs=(vmem(), vmem()),
        scratch_shapes=[
            pltpu.VMEM((4, 2, TOK, 256), BF16),
            pltpu.VMEM((KVC, TOK), BF16),
            pltpu.VMEM((pad16(8 * KB), 128), F32),
            pltpu.VMEM((pad16(8 * KB), 128), F32),
            pltpu.SemaphoreType.DMA((4, 2)),
        ],
        compiler_params=params(24),
        cost_estimate=pl.CostEstimate(flops=2 * KVC * TOK * 2048, bytes_accessed=8 * MIB, transcendentals=0),
        name=f"grad_quantize_{part}",
    )(tokens, og)


def sum_kernel(tiles, coded, keep, recv, keep_out, send_out, sc_out):
    half = tiles // 2
    sc0 = code_rows(tiles)

    def total(block):
        rows = pl.ds(pl.multiple_of(block * 128, 128), 128)
        r_sc = recv[sc0:sc0 + pad16(tiles * KB), :].astype(F32)
        del r_sc
        return rows

    def body(block, _):
        rows = pl.ds(pl.multiple_of(block * 128, 128), 128)
        rs = sc_out[1, pl.ds(block, 1), :]
        if coded:
            m = keep[rows, :] + decode(recv[rows, :], rs)
        else:
            ks = sc_out[0, pl.ds(block, 1), :]
            m = keep[rows, :].astype(F32) * ks + recv[rows, :].astype(F32) * rs
        return m

    n = pad16(tiles * KB)
    sc_out[1, :n, :] = recv[sc0:sc0 + n, :].astype(F32)
    if not coded:
        sc_out[0, :n, :] = keep[sc0:sc0 + n, :].astype(F32)

    def keep_body(block, _):
        keep_out[pl.ds(pl.multiple_of(block * 128, 128), 128), :] = body(block, 0)
        return 0

    def send_body(block, _):
        code, scale = encode(body(block + half * KB, 0))
        send_out[pl.ds(pl.multiple_of(block * 128, 128), 128), :] = code
        sc_out[2, pl.ds(block, 1), :] = scale
        return 0

    lax.fori_loop(0, half * KB, send_body, 0, unroll=2)
    m = pad16(half * KB)
    send_out[code_rows(half):, :] = sc_out[2, :m, :].astype(BF16)
    lax.fori_loop(0, half * KB, keep_body, 0, unroll=2)


def sum_stage(keep, recv, tiles):
    half = tiles // 2
    n = pad16(tiles * KB)
    return pl.pallas_call(
        functools.partial(sum_kernel, tiles, tiles < 8),
        out_shape=(
            jax.ShapeDtypeStruct((code_rows(half), 128), F32),
            jax.ShapeDtypeStruct((msg_rows(half), 128), BF16),
        ),
        in_specs=[vmem(), vmem()],
        out_specs=(vmem(), vmem()),
        scratch_shapes=[pltpu.VMEM((3, n, 128), F32)],
        compiler_params=params(16),
        cost_estimate=pl.CostEstimate(flops=tiles * KVC * 128 * 10, bytes_accessed=tiles * KVC * 128 * 8, transcendentals=0),
        name=f"sum_{tiles}",
    )(keep, recv)


def requantize_kernel(keep, recv, out, sc):
    n = pad16(KB)
    sc[0] = recv[KVC:KVC + n, :].astype(F32)
    for k in range(KB):
        rows = slice(k * 128, (k + 1) * 128)
        m = keep[rows, :] + decode(recv[rows, :], sc[0, k:k + 1, :])
        code, scale = quantize(m)
        out[rows, :] = code
        sc[1, k:k + 1, :] = scale
    out[KVC:, :] = sc[1].astype(BF16)


def requantize_stage(keep, recv):
    return pl.pallas_call(
        requantize_kernel,
        out_shape=jax.ShapeDtypeStruct((msg_rows(1), 128), BF16),
        in_specs=[vmem(), vmem()],
        out_specs=vmem(),
        scratch_shapes=[pltpu.VMEM((2, pad16(KB), 128), F32)],
        compiler_params=params(8),
        cost_estimate=pl.CostEstimate(flops=KVC * 128 * 10, bytes_accessed=KVC * 128 * 8, transcendentals=0),
        name="requantize",
    )(keep, recv)


def node_sum_kernel(a, b, c, d, mine, other, sc, g):
    core = lax.axis_index("node") & 1
    n = pad16(KB)
    for i, r in enumerate((a, b, c, d)):
        sc[i] = r[KVC:KVC + n, :].astype(F32)
    for k in range(KB):
        rows = slice(k * 128, (k + 1) * 128)
        m = a[rows, :].astype(F32) * sc[0, k:k + 1, :]
        for i, r in ((1, b), (2, c), (3, d)):
            m = m + r[rows, :].astype(F32) * sc[i, k:k + 1, :]
        g[rows, :] = m
    h = KVC // 2
    lo = g[:h, :]
    hi = g[h:, :]
    first = jnp.concatenate([lo[:, :64], hi[:, :64]], axis=1)
    second = jnp.concatenate([lo[:, 64:], hi[:, 64:]], axis=1)
    mine[...] = jnp.where(core == 0, first, second)
    other[...] = jnp.where(core == 0, second, first)


def node_sum_stage(parts):
    out = jax.ShapeDtypeStruct((KVC // 2, 128), F32)
    return pl.pallas_call(
        node_sum_kernel,
        out_shape=(out, out),
        in_specs=[vmem()] * 4,
        out_specs=(vmem(), vmem()),
        scratch_shapes=[pltpu.VMEM((4, pad16(KB), 128), F32), pltpu.VMEM((KVC, 128), F32)],
        compiler_params=params(8),
        cost_estimate=pl.CostEstimate(flops=KVC * 128 * 10, bytes_accessed=KVC * 128 * 12, transcendentals=0),
        name="node_sum",
    )(*parts)


def adam_kernel(mine, recv, master, moment, second, new_master, new_moment, new_second, weight):
    t = (mine[...] + recv[...]).T
    grad = jnp.concatenate([t[:64], t[64:]], axis=1)
    m = 0.9 * moment[...] + 0.1 * grad
    s = 0.95 * second[...] + 0.05 * grad * grad
    update = m / (1.0 - 0.9**10) / (jnp.sqrt(s / (1.0 - 0.95**10)) + 1e-08) + 0.1 * master[...]
    w = master[...] - 0.05 * update
    new_master[...] = w
    new_moment[...] = m
    new_second[...] = s
    weight[...] = w.astype(BF16)


def adam_stage(mine, recv, master, moment, second, chunk):
    block = pl.BlockSpec((64, KVC), lambda i: (0, chunk))
    whole = pl.BlockSpec((KVC // 2, 128), lambda i: (0, 0))
    out = pl.BlockSpec((64, KVC), lambda i: (0, 0))
    f = jax.ShapeDtypeStruct((64, KVC), F32)
    return pl.pallas_call(
        adam_kernel,
        grid=(1,),
        out_shape=(f, f, f, jax.ShapeDtypeStruct((64, KVC), BF16)),
        in_specs=[whole, whole, block, block, block],
        out_specs=(out,) * 4,
        compiler_params=params(8),
        cost_estimate=pl.CostEstimate(flops=64 * KVC * 20, bytes_accessed=64 * KVC * 32, transcendentals=0),
        name="adam",
    )(mine, recv, master, moment, second)


def gather_kernel(*refs):
    me_n = lax.axis_index("node")
    y = lax.shift_right_logical(me_n, 1)
    core = me_n & 1
    pieces = refs[:CHUNKS * 11]
    new_master, new_moment, new_second, weight = refs[CHUNKS * 11:]
    for c in range(CHUNKS):
        p = pieces[c * 11:(c + 1) * 11]
        cols = slice(c * KVC, (c + 1) * KVC)
        new_master[:, cols] = p[0][...]
        new_moment[:, cols] = p[1][...]
        new_second[:, cols] = p[2][...]
        for k in range(4):
            src = ((y - k) & 3) * 2
            weight[src + core, :, cols] = p[3 + k][...]
            weight[src + 1 - core, :, cols] = p[7 + k][...]


def gather_stage(pieces):
    f = jax.ShapeDtypeStruct((64, KV), F32)
    return pl.pallas_call(
        gather_kernel,
        out_shape=(f, f, f, jax.ShapeDtypeStruct((8, 64, KV), BF16)),
        in_specs=[vmem()] * len(pieces),
        out_specs=(vmem(),) * 4,
        compiler_params=params(16),
        cost_estimate=pl.CostEstimate(flops=0, bytes_accessed=6 * MIB, transcendentals=0),
        name="gather_outputs",
    )(*pieces)


def local(tokens, out_grads, master, moment, second):
    og = [out_grads[:, c * KVC:(c + 1) * KVC] for c in range(CHUNKS)]
    units = [(c, p) for c in range(CHUNKS) for p in range(4)]
    keep, recv = {}, {}
    for u in units:
        c, p = u
        send, keep[u] = first_stage(tokens, og[c], p)
        recv[u] = lax.ppermute(send, "local", local_perm(p % 4))
    for s, tiles in ((1, 8), (2, 4), (3, 2)):
        for u in units:
            keep[u], send = sum_stage(keep[u], recv[u], tiles)
            recv[u] = lax.ppermute(send, "local", local_perm((u[1] + s) % 4))
    pieces = []
    for c in range(CHUNKS):
        parts = []
        for p in range(4):
            q = requantize_stage(keep[c, p], recv[c, p])
            parts.append(lax.ppermute(q, "node", y_perm(p)) if p else q)
        mine, other = node_sum_stage(parts)
        other = lax.ppermute(other, "node", CORE_PERM)
        a, b, d, w = adam_stage(mine, other, master, moment, second, c)
        own = [w] + [lax.ppermute(w, "node", y_perm(k)) for k in (1, 2, 3)]
        pieces += [a, b, d] + own + [lax.ppermute(v, "node", CORE_PERM) for v in own]
    return gather_stage(pieces)


def solution(mesh):
    rows = P(("node", "local"), None)
    return jax.shard_map(
        local,
        mesh=mesh,
        in_specs=(rows,) * 5,
        out_specs=(rows, rows, rows, P(None, "local", None)),
        check_vma=False,
    )
```

time: 533 us -> 165 us (0.31)
  waiting for transfers between devices: 228 us -> 42.4 us
  local copies, waits for them, and re-layouts: 155 us -> 6.06 us
  other arithmetic: 85.4 us -> 0 us
  Pallas kernels: 0 us -> 47.8 us
  starting transfers between devices: 26.1 us -> 67.8 us
  matrix products: 21.9 us -> 0 us
  between operations: 14.2 us -> 1.15 us
    all_to_all x4 -> x0, waiting for transfers between devices: 206 us -> none  [the longest x1 195 us: local(): lax.all_to_all(codes, 'local', split_axis=1, concat_axis=1, tiled=True)]
    ppermute x0 -> x54, starting transfers between devices: none -> 67.8 us  [the longest x24 19.7 us: local(): recv[u] = lax.ppermute(send, 'local', local_perm((u[1] + s) % 4))]
    div x4 -> x0, local copies, waits for them, and re-layouts: 57.1 us -> none  [quantize(): codes = (blocks / scale.astype(jnp.float32)[..., None]).astype(jnp.bfloat16)]
    mul x4 -> x0, local copies, waits for them, and re-layouts: 52.9 us -> none  [restore(): return (blocks * scale.astype(jnp.float32)[..., None]).reshape(shape)]
    pallas_call x0 -> x45, Pallas kernels: none -> 47.8 us  [the longest x8 31.7 us: first_stage(): pl.pallas_call(functools.partial(first_kernel, part), out_shape=(out, out...]
    ppermute x0 -> x54, waiting for transfers between devices: none -> 42.4 us  [the longest x24 20.4 us: local(): recv[u] = lax.ppermute(send, 'local', local_perm((u[1] + s) % 4))]
    convert_element_type x5 -> x0, other arithmetic: 33.3 us -> none  [the longest x2 31.3 us: quantize(): codes = (blocks / scale.astype(jnp.float32)[..., None]).astype(jnp.bfloat16)]
    all_to_all x4 -> x0, starting transfers between devices: 26.1 us -> none  [the longest x1 8.44 us: local(): lax.all_to_all(scale, 'local', split_axis=1, concat_axis=1, tiled=True)]
  transfers between devices with their start and end apart: 5 -> 54, of which waited for: 4 -> 17; matrix products, arithmetic and copies ran while one was open for 29% -> 0% of each run, Pallas kernels for 0% -> 26%
where the time goes in v1:
time: 165 us
  starting transfers between devices  67.8 us (41%)
  Pallas kernels  47.8 us (29%)
  waiting for transfers between devices  42.4 us (26%)
  local copies, waits for them, and re-layouts  6.06 us (4%)
    pallas_call x8, Pallas kernels, first_stage(): pl.pallas_call(functools.partial(first_kernel, part), out_shape=(out, out...  31.7 us
    ppermute x24, waiting for transfers between devices, local(): recv[u] = lax.ppermute(send, 'local', local_perm((u[1] + s) % 4))  20.4 us
    ppermute x24, starting transfers between devices, local(): recv[u] = lax.ppermute(send, 'local', local_perm((u[1] + s) % 4))  19.7 us
    ppermute x8, waiting for transfers between devices, local(): recv[u] = lax.ppermute(send, 'local', local_perm(p % 4))  19.1 us
    ppermute x2, starting transfers between devices, local(): other = lax.ppermute(other, 'node', CORE_PERM)  17.7 us
    pallas_call x24, Pallas kernels, sum_stage(): pl.pallas_call(functools.partial(sum_kernel, tiles, tiles < 8), out_shape...  13 us
    ppermute x8, starting transfers between devices, local(): recv[u] = lax.ppermute(send, 'local', local_perm(p % 4))  10.4 us
    ppermute x6, starting transfers between devices, local(): parts.append(lax.ppermute(q, 'node', y_perm(p)) if p else q)  8.35 us
  transfers between devices with their start and end apart: 54, of which 17 were waited for; matrix products, arithmetic and copies ran while one was open for 0% of the time, Pallas kernels for 26%

profile of v1, /device:TPU:1, one launch (start us, length us, event | category | flops | bytes accessed | tf_op | source)
XLA Modules:
  0.0 165.2 jit_solution(17283590157210334)
XLA Ops:
  0.6 1.5 fusion
  2.1 4.6 %copy-done = bf16[768,8192]{1,0:T(8,128)(2,1)S(1)} copy-done((bf16[768,8192]{1,0:T(8,128)(2,1)S(1)}, bf16[768,8192]{1,0:T(8,128)(2,1)}, u32[]{:S(2)}) %copy-start) | copy-done | bytes 12582936
  6.7 3.7 %grad_quantize_3.3 = (bf16[4128,128]{1,0:T(8,128)(2,1)S(1)}, bf16[4128,128]{1,0:T(8,128)(2,1)S(1)}) custom-call(bf16[768,8192]{1,0:T(8,128)(2,1)S(1)} %copy-done, bf16[768,512]{1,0:T(8,128)(2,1)S(1)} %get-tuple-element.156.og), custom_call_target="tpu_custom_call" | custom-call | flops 1610612736 | bytes 8388608 | tf_op jit(solution)/shard_map/grad_quantize_3/pallas_call | solution.py:149
  10.4 4.7 %collective-permute-start.41 = (bf16[4128,128]{1,0:T(8,128)(2,1)S(1)}, bf16[4128,128]{1,0:T(8,128)(2,1)S(1)}, u32[]{:S(2)}, u32[]{:S(2)}) collective-permute-start(bf16[4128,128]{1,0:T(8,128)(2,1)S(1)} %get-tuple-element.143), channel_id=1, source_target_pairs={{0,12},{1,13},{2,14},{3,15},{4,8},{5,9},{6,10},{7,11},{8,4},{9,5},... | collective-permute-start | bytes 3170312 | tf_op jit(solution)/shard_map/ppermute | solution.py:353
  15.0 3.7 %grad_quantize_2.3 = (bf16[4128,128]{1,0:T(8,128)(2,1)S(1)}, bf16[4128,128]{1,0:T(8,128)(2,1)S(1)}) custom-call(bf16[768,8192]{1,0:T(8,128)(2,1)S(1)} %copy-done, bf16[768,512]{1,0:T(8,128)(2,1)S(1)} %get-tuple-element.156.og), custom_call_target="tpu_custom_call" | custom-call | flops 1610612736 | bytes 8388608 | tf_op jit(solution)/shard_map/grad_quantize_2/pallas_call | solution.py:149
  18.8 3.7 %grad_quantize_1.3 = (bf16[4128,128]{1,0:T(8,128)(2,1)S(1)}, bf16[4128,128]{1,0:T(8,128)(2,1)S(1)}) custom-call(bf16[768,8192]{1,0:T(8,128)(2,1)S(1)} %copy-done, bf16[768,512]{1,0:T(8,128)(2,1)S(1)} %get-tuple-element.156.og), custom_call_target="tpu_custom_call" | custom-call | flops 1610612736 | bytes 8388608 | tf_op jit(solution)/shard_map/grad_quantize_1/pallas_call | solution.py:149
  22.5 2.6 %collective-permute-start.31 = (bf16[4128,128]{1,0:T(8,128)(2,1)S(1)}, bf16[4128,128]{1,0:T(8,128)(2,1)S(1)}, u32[]{:S(2)}, u32[]{:S(2)}) collective-permute-start(bf16[4128,128]{1,0:T(8,128)(2,1)S(1)} %get-tuple-element.127), channel_id=1, source_target_pairs={{0,3},{1,2},{2,1},{3,0},{4,7},{5,6},{6,5},{7,4},{8,11},{9,10},{10,... | collective-permute-start | bytes 3170312 | tf_op jit(solution)/shard_map/ppermute | solution.py:353
  25.1 4.8 %grad_quantize_0.3 = (bf16[4128,128]{1,0:T(8,128)(2,1)S(1)}, bf16[4128,128]{1,0:T(8,128)(2,1)S(1)}) custom-call(bf16[768,8192]{1,0:T(8,128)(2,1)S(1)} %copy-done, bf16[768,512]{1,0:T(8,128)(2,1)S(1)} %get-tuple-element.156.og), custom_call_target="tpu_custom_call" | custom-call | flops 1610612736 | bytes 8388608 | tf_op jit(solution)/shard_map/grad_quantize_0/pallas_call | solution.py:149
  30.0 3.7 %grad_quantize_3.2 = (bf16[4128,128]{1,0:T(8,128)(2,1)S(1)}, bf16[4128,128]{1,0:T(8,128)(2,1)S(1)}) custom-call(bf16[768,8192]{1,0:T(8,128)(2,1)S(1)} %copy-done, bf16[768,512]{1,0:T(8,128)(2,1)S(1)} %get-tuple-element.157.og), custom_call_target="tpu_custom_call" | custom-call | flops 1610612736 | bytes 8388608 | tf_op jit(solution)/shard_map/grad_quantize_3/pallas_call | solution.py:149
  33.9 3.7 %grad_quantize_2.2 = (bf16[4128,128]{1,0:T(8,128)(2,1)S(1)}, bf16[4128,128]{1,0:T(8,128)(2,1)S(1)}) custom-call(bf16[768,8192]{1,0:T(8,128)(2,1)S(1)} %copy-done, bf16[768,512]{1,0:T(8,128)(2,1)S(1)} %get-tuple-element.157.og), custom_call_target="tpu_custom_call" | custom-call | flops 1610612736 | bytes 8388608 | tf_op jit(solution)/shard_map/grad_quantize_2/pallas_call | solution.py:149
  38.1 0.9 collective-permute-start.9
  39.0 3.7 %grad_quantize_1.2 = (bf16[4128,128]{1,0:T(8,128)(2,1)S(1)}, bf16[4128,128]{1,0:T(8,128)(2,1)S(1)}) custom-call(bf16[768,8192]{1,0:T(8,128)(2,1)S(1)} %copy-done, bf16[768,512]{1,0:T(8,128)(2,1)S(1)} %get-tuple-element.157.og), custom_call_target="tpu_custom_call" | custom-call | flops 1610612736 | bytes 8388608 | tf_op jit(solution)/shard_map/grad_quantize_1/pallas_call | solution.py:149
  42.7 4.8 %grad_quantize_0.2 = (bf16[4128,128]{1,0:T(8,128)(2,1)S(1)}, bf16[4128,128]{1,0:T(8,128)(2,1)S(1)}) custom-call(bf16[768,8192]{1,0:T(8,128)(2,1)S(1)} %copy-done, bf16[768,512]{1,0:T(8,128)(2,1)S(1)} %get-tuple-element.157.og), custom_call_target="tpu_custom_call" | custom-call | flops 1610612736 | bytes 8388608 | tf_op jit(solution)/shard_map/grad_quantize_0/pallas_call | solution.py:149
  47.6 1.6 collective-permute-start.4
  49.4 0.8 sum_8.15
  50.2 3.4 %collective-permute-done.27.recv = bf16[4128,128]{1,0:T(8,128)(2,1)S(1)} collective-permute-done((bf16[4128,128]{1,0:T(8,128)(2,1)S(1)}, bf16[4128,128]{1,0:T(8,128)(2,1)S(1)}, u32[]{:S(2)}, u32[]{:S(2)}) %collective-permute-start.27) | collective-permute-done | bytes 1056800 | tf_op jit(solution)/shard_map/ppermute | solution.py:353
  53.6 0.8 sum_8.14
  54.4 6.3 %collective-permute-done.14.recv = bf16[4128,128]{1,0:T(8,128)(2,1)S(1)} collective-permute-done((bf16[4128,128]{1,0:T(8,128)(2,1)S(1)}, bf16[4128,128]{1,0:T(8,128)(2,1)S(1)}, u32[]{:S(2)}, u32[]{:S(2)}) %collective-permute-start.14) | collective-permute-done | bytes 1056800 | tf_op jit(solution)/shard_map/ppermute | solution.py:353
  60.8 2.4 %collective-permute-start.37 = (bf16[2064,128]{1,0:T(8,128)(2,1)S(1)}, bf16[2064,128]{1,0:T(8,128)(2,1)S(1)}, u32[]{:S(2)}, u32[]{:S(2)}) collective-permute-start(bf16[2064,128]{1,0:T(8,128)(2,1)S(1)} %get-tuple-element.137), channel_id=1, source_target_pairs={{0,12},{1,13},{2,14},{3,15},{4,8},{5,9},{6,10},{7,11},{8,4},{9,5},... | collective-permute-start | bytes 1585160 | tf_op jit(solution)/shard_map/ppermute | solution.py:357
  63.1 0.8 sum_8.13
  63.9 1.4 collective-permute-done.9.recv
  65.7 0.8 sum_8.12
  66.5 0.8 sum_8.11
  67.3 4.4 %collective-permute-done.4.recv = bf16[4128,128]{1,0:T(8,128)(2,1)S(1)} collective-permute-done((bf16[4128,128]{1,0:T(8,128)(2,1)S(1)}, bf16[4128,128]{1,0:T(8,128)(2,1)S(1)}, u32[]{:S(2)}, u32[]{:S(2)}) %collective-permute-start.4) | collective-permute-done | bytes 1056800 | tf_op jit(solution)/shard_map/ppermute | solution.py:353
  71.7 1.5 collective-permute-start.28
  73.2 3.0 %collective-permute-done.recv = bf16[4128,128]{1,0:T(8,128)(2,1)S(1)} collective-permute-done((bf16[4128,128]{1,0:T(8,128)(2,1)S(1)}, bf16[4128,128]{1,0:T(8,128)(2,1)S(1)}, u32[]{:S(2)}, u32[]{:S(2)}) %collective-permute-start) | collective-permute-done | bytes 1056800 | tf_op jit(solution)/shard_map/ppermute | solution.py:353
  76.3 0.8 sum_8.10
  77.1 10.4 %collective-permute-done.42.recv = bf16[2064,128]{1,0:T(8,128)(2,1)S(1)} collective-permute-done((bf16[2064,128]{1,0:T(8,128)(2,1)S(1)}, bf16[2064,128]{1,0:T(8,128)(2,1)S(1)}, u32[]{:S(2)}, u32[]{:S(2)}) %collective-permute-start.42) | collective-permute-done | bytes 528416 | tf_op jit(solution)/shard_map/ppermute | solution.py:357
  87.5 0.8 sum_8.9
  88.4 1.3 collective-permute-start.5
  89.6 0.8 sum_8.8
  91.8 2.6 %collective-permute-start.43 = (bf16[1040,128]{1,0:T(8,128)(2,1)S(1)}, bf16[1040,128]{1,0:T(8,128)(2,1)S(1)}, u32[]{:S(2)}, u32[]{:S(2)}) collective-permute-start(bf16[1040,128]{1,0:T(8,128)(2,1)S(1)} %get-tuple-element.147), channel_id=1, source_target_pairs={{0,3},{1,2},{2,1},{3,0},{4,7},{5,6},{6,5},{7,4},{8,11},{9,10},{10,... | collective-permute-start | bytes 798728 | tf_op jit(solution)/shard_map/ppermute | solution.py:357
  94.4 4.5 %collective-permute-done.15.recv = bf16[2064,128]{1,0:T(8,128)(2,1)S(1)} collective-permute-done((bf16[2064,128]{1,0:T(8,128)(2,1)S(1)}, bf16[2064,128]{1,0:T(8,128)(2,1)S(1)}, u32[]{:S(2)}, u32[]{:S(2)}) %collective-permute-start.15) | collective-permute-done | bytes 528416 | tf_op jit(solution)/shard_map/ppermute | solution.py:357
  100.2 1.3 collective-permute-start.29
  102.0 0.8 collective-permute-start.16
  103.9 2.0 %collective-permute-done.43.recv = bf16[1040,128]{1,0:T(8,128)(2,1)S(1)} collective-permute-done((bf16[1040,128]{1,0:T(8,128)(2,1)S(1)}, bf16[1040,128]{1,0:T(8,128)(2,1)S(1)}, u32[]{:S(2)}, u32[]{:S(2)}) %collective-permute-start.43) | collective-permute-done | bytes 266272 | tf_op jit(solution)/shard_map/ppermute | solution.py:357
  105.9 2.1 %collective-permute-start.6 = (bf16[1040,128]{1,0:T(8,128)(2,1)S(1)}, bf16[1040,128]{1,0:T(8,128)(2,1)S(1)}, u32[]{:S(2)}, u32[]{:S(2)}) collective-permute-start(bf16[1040,128]{1,0:T(8,128)(2,1)S(1)} %get-tuple-element.93), channel_id=1, source_target_pairs={{0,12},{1,13},{2,14},{3,15},{4,8},{5,9},{6,10},{7,11},{8,4},{9,5},... | collective-permute-start | bytes 798728 | tf_op jit(solution)/shard_map/ppermute | solution.py:357
  108.6 0.9 collective-permute-start.2
  109.8 0.7 collective-permute-start.44
  110.8 1.0 collective-permute-done.16.recv
  111.7 0.7 collective-permute-start.39
  114.1 1.3 collective-permute-done.44.recv
  115.4 1.1 collective-permute-start.12
  117.1 1.1 collective-permute-done.39.recv
  118.4 2.3 %collective-permute-start.30 = (bf16[528,128]{1,0:T(8,128)(2,1)S(1)}, bf16[528,128]{1,0:T(8,128)(2,1)S(1)}, u32[]{:S(2)}, u32[]{:S(2)}) collective-permute-start(bf16[528,128]{1,0:T(8,128)(2,1)S(1)} %get-tuple-element.125), channel_id=1, source_target_pairs={{0,12},{1,13},{2,14},{3,15},{4,8},{5,9},{6,10},{7,11},{8,4},{9,5},... | collective-permute-start | bytes 405512 | tf_op jit(solution)/shard_map/ppermute | solution.py:357
  120.7 2.7 %collective-permute-start.45 = (bf16[528,128]{1,0:T(8,128)(2,1)S(1)}, bf16[528,128]{1,0:T(8,128)(2,1)S(1)}, u32[]{:S(2)}, u32[]{:S(2)}) collective-permute-start(bf16[528,128]{1,0:T(8,128)(2,1)S(1)} %requantize.15), channel_id=1, source_target_pairs={{0,96},{16,112},{32,0},{48,16},{64,32},{80,48},{96,64},{112,80},{1... | collective-permute-start | bytes 405512 | tf_op jit(solution)/shard_map/ppermute | solution.py:363
  123.9 0.7 collective-permute-start.35
  125.2 0.6 collective-permute-start.3
  125.9 2.3 %collective-permute-start.18 = (bf16[528,128]{1,0:T(8,128)(2,1)S(1)}, bf16[528,128]{1,0:T(8,128)(2,1)S(1)}, u32[]{:S(2)}, u32[]{:S(2)}) collective-permute-start(bf16[528,128]{1,0:T(8,128)(2,1)S(1)} %requantize.11), channel_id=1, source_target_pairs={{0,96},{16,112},{32,0},{48,16},{64,32},{80,48},{96,64},{112,80},{1... | collective-permute-start | bytes 405512 | tf_op jit(solution)/shard_map/ppermute | solution.py:363
  128.2 1.4 collective-permute-start.13
  129.6 0.9 collective-permute-start.8
  130.8 12.6 %collective-permute-start.46 = (f32[256,128]{1,0:T(8,128)S(1)}, f32[256,128]{1,0:T(8,128)S(1)}, u32[]{:S(2)}, u32[]{:S(2)}) collective-permute-start(f32[256,128]{1,0:T(8,128)S(1)} %get-tuple-element.151), channel_id=1, source_target_pairs={{0,16},{16,0},{32,48},{48,32},{64,80},{80,64},{96,112},{112,96},{1... | collective-permute-start | bytes 393224 | tf_op jit(solution)/shard_map/ppermute | solution.py:365
  143.7 5.2 %collective-permute-start.19 = (f32[256,128]{1,0:T(8,128)S(1)}, f32[256,128]{1,0:T(8,128)S(1)}, u32[]{:S(2)}, u32[]{:S(2)}) collective-permute-start(f32[256,128]{1,0:T(8,128)S(1)} %get-tuple-element.113), channel_id=1, source_target_pairs={{0,16},{16,0},{32,48},{48,32},{64,80},{80,64},{96,112},{112,96},{1... | collective-permute-start | bytes 393224 | tf_op jit(solution)/shard_map/ppermute | solution.py:365
  149.5 1.4 collective-permute-start.48
  151.7 1.3 collective-permute-start.23
  153.1 2.1 %collective-permute-start.22 = (bf16[64,512]{1,0:T(8,128)(2,1)S(1)}, bf16[64,512]{1,0:T(8,128)(2,1)S(1)}, u32[]{:S(2)}, u32[]{:S(2)}) collective-permute-start(bf16[64,512]{1,0:T(8,128)(2,1)S(1)} %get-tuple-element.117.refs_3_), channel_id=1, source_target_pairs={{0,96},{16,112},{32,0},{48,16},{64,32},{80,48},{96,64},{112,80},{1... | collective-permute-start | bytes 196616 | tf_op jit(solution)/shard_map/ppermute | solution.py:367
  155.2 0.8 collective-permute-start.21
  156.0 0.8 collective-permute-start.20
  156.7 0.9 collective-permute-start.53
  158.2 1.7 %collective-permute-done.21.refs_5_ = bf16[64,512]{1,0:T(8,128)(2,1)S(1)} collective-permute-done((bf16[64,512]{1,0:T(8,128)(2,1)S(1)}, bf16[64,512]{1,0:T(8,128)(2,1)S(1)}, u32[]{:S(2)}, u32[]{:S(2)}) %collective-permute-start.21) | collective-permute-done | bytes 65568 | tf_op jit(solution)/shard_map/ppermute | solution.py:367
  159.8 2.1 %collective-permute-start.26 = (bf16[64,512]{1,0:T(8,128)(2,1)S(1)}, bf16[64,512]{1,0:T(8,128)(2,1)S(1)}, u32[]{:S(2)}, u32[]{:S(2)}) collective-permute-start(bf16[64,512]{1,0:T(8,128)(2,1)S(1)} %collective-permute-done.22.refs_6_), channel_id=1, source_target_pairs={{0,16},{16,0},{32,48},{48,32},{64,80},{80,64},{96,112},{112,96},{1... | collective-permute-start | bytes 196616 | tf_op jit(solution)/shard_map/ppermute | solution.py:368
  161.9 0.7 collective-permute-start.25
  162.8 0.7 collective-permute-done.25.refs_9_
  163.9 1.4 gather_outputs.1
  (98 shorter events, 13.6 us)
Async XLA Ops:
  2.1 4.6 %copy-start = (bf16[768,8192]{1,0:T(8,128)(2,1)S(1)}, bf16[768,8192]{1,0:T(8,128)(2,1)}, u32[]{:S(2)}) copy-start(bf16[768,8192]{1,0:T(8,128)(2,1)} %tok.15) | copy-start | bytes 37748740
  10.4 27.7 %collective-permute-start.41 = (bf16[4128,128]{1,0:T(8,128)(2,1)S(1)}, bf16[4128,128]{1,0:T(8,128)(2,1)S(1)}, u32[]{:S(2)}, u32[]{:S(2)}) collective-permute-start(bf16[4128,128]{1,0:T(8,128)(2,1)S(1)} %get-tuple-element.143), channel_id=1, source_target_pairs={{0,12},{1,13},{2,14},{3,15},{4,8},{5,9},{6,10},{7,11},{8,4},{9,5},... | collective-permute-start | bytes 3170312 | tf_op jit(solution)/shard_map/ppermute | solution.py:353
  18.7 28.8 %collective-permute-start.36 = (bf16[4128,128]{1,0:T(8,128)(2,1)S(1)}, bf16[4128,128]{1,0:T(8,128)(2,1)S(1)}, u32[]{:S(2)}, u32[]{:S(2)}) collective-permute-start(bf16[4128,128]{1,0:T(8,128)(2,1)S(1)} %get-tuple-element.135), channel_id=1, source_target_pairs={{0,4},{1,5},{2,6},{3,7},{4,0},{5,1},{6,2},{7,3},{8,12},{9,13},{10,... | collective-permute-start | bytes 3170312 | tf_op jit(solution)/shard_map/ppermute | solution.py:353
  22.5 26.7 %collective-permute-start.31 = (bf16[4128,128]{1,0:T(8,128)(2,1)S(1)}, bf16[4128,128]{1,0:T(8,128)(2,1)S(1)}, u32[]{:S(2)}, u32[]{:S(2)}) collective-permute-start(bf16[4128,128]{1,0:T(8,128)(2,1)S(1)} %get-tuple-element.127), channel_id=1, source_target_pairs={{0,3},{1,2},{2,1},{3,0},{4,7},{5,6},{6,5},{7,4},{8,11},{9,10},{10,... | collective-permute-start | bytes 3170312 | tf_op jit(solution)/shard_map/ppermute | solution.py:353
  29.9 23.7 %collective-permute-start.27 = (bf16[4128,128]{1,0:T(8,128)(2,1)S(1)}, bf16[4128,128]{1,0:T(8,128)(2,1)S(1)}, u32[]{:S(2)}, u32[]{:S(2)}) collective-permute-start(bf16[4128,128]{1,0:T(8,128)(2,1)S(1)} %get-tuple-element.119), channel_id=1, source_target_pairs={{0,1},{1,0},{2,3},{3,2},{4,5},{5,4},{6,7},{7,6},{8,9},{9,8},{10,11... | collective-permute-start | bytes 3170312 | tf_op jit(solution)/shard_map/ppermute | solution.py:353
  33.7 27.1 %collective-permute-start.14 = (bf16[4128,128]{1,0:T(8,128)(2,1)S(1)}, bf16[4128,128]{1,0:T(8,128)(2,1)S(1)}, u32[]{:S(2)}, u32[]{:S(2)}) collective-permute-start(bf16[4128,128]{1,0:T(8,128)(2,1)S(1)} %get-tuple-element.105), channel_id=1, source_target_pairs={{0,12},{1,13},{2,14},{3,15},{4,8},{5,9},{6,10},{7,11},{8,4},{9,5},... | collective-permute-start | bytes 3170312 | tf_op jit(solution)/shard_map/ppermute | solution.py:353
  38.1 27.2 %collective-permute-start.9 = (bf16[4128,128]{1,0:T(8,128)(2,1)S(1)}, bf16[4128,128]{1,0:T(8,128)(2,1)S(1)}, u32[]{:S(2)}, u32[]{:S(2)}) collective-permute-start(bf16[4128,128]{1,0:T(8,128)(2,1)S(1)} %get-tuple-element.97), channel_id=1, source_target_pairs={{0,4},{1,5},{2,6},{3,7},{4,0},{5,1},{6,2},{7,3},{8,12},{9,13},{10,... | collective-permute-start | bytes 3170312 | tf_op jit(solution)/shard_map/ppermute | solution.py:353
  47.6 24.1 %collective-permute-start.4 = (bf16[4128,128]{1,0:T(8,128)(2,1)S(1)}, bf16[4128,128]{1,0:T(8,128)(2,1)S(1)}, u32[]{:S(2)}, u32[]{:S(2)}) collective-permute-start(bf16[4128,128]{1,0:T(8,128)(2,1)S(1)} %get-tuple-element.89), channel_id=1, source_target_pairs={{0,3},{1,2},{2,1},{3,0},{4,7},{5,6},{6,5},{7,4},{8,11},{9,10},{10,... | collective-permute-start | bytes 3170312 | tf_op jit(solution)/shard_map/ppermute | solution.py:353
  49.2 27.0 %collective-permute-start = (bf16[4128,128]{1,0:T(8,128)(2,1)S(1)}, bf16[4128,128]{1,0:T(8,128)(2,1)S(1)}, u32[]{:S(2)}, u32[]{:S(2)}) collective-permute-start(bf16[4128,128]{1,0:T(8,128)(2,1)S(1)} %get-tuple-element.81), channel_id=1, source_target_pairs={{0,1},{1,0},{2,3},{3,2},{4,5},{5,4},{6,7},{7,6},{8,9},{9,8},{10,11... | collective-permute-start | bytes 3170312 | tf_op jit(solution)/shard_map/ppermute | solution.py:353
  53.6 34.0 %collective-permute-start.42 = (bf16[2064,128]{1,0:T(8,128)(2,1)S(1)}, bf16[2064,128]{1,0:T(8,128)(2,1)S(1)}, u32[]{:S(2)}, u32[]{:S(2)}) collective-permute-start(bf16[2064,128]{1,0:T(8,128)(2,1)S(1)} %get-tuple-element.145), channel_id=1, source_target_pairs={{0,1},{1,0},{2,3},{3,2},{4,5},{5,4},{6,7},{7,6},{8,9},{9,8},{10,11... | collective-permute-start | bytes 1585160 | tf_op jit(solution)/shard_map/ppermute | solution.py:357
  60.8 27.6 %collective-permute-start.37 = (bf16[2064,128]{1,0:T(8,128)(2,1)S(1)}, bf16[2064,128]{1,0:T(8,128)(2,1)S(1)}, u32[]{:S(2)}, u32[]{:S(2)}) collective-permute-start(bf16[2064,128]{1,0:T(8,128)(2,1)S(1)} %get-tuple-element.137), channel_id=1, source_target_pairs={{0,12},{1,13},{2,14},{3,15},{4,8},{5,9},{6,10},{7,11},{8,4},{9,5},... | collective-permute-start | bytes 1585160 | tf_op jit(solution)/shard_map/ppermute | solution.py:357
  65.3 25.1 %collective-permute-start.32 = (bf16[2064,128]{1,0:T(8,128)(2,1)S(1)}, bf16[2064,128]{1,0:T(8,128)(2,1)S(1)}, u32[]{:S(2)}, u32[]{:S(2)}) collective-permute-start(bf16[2064,128]{1,0:T(8,128)(2,1)S(1)} %get-tuple-element.129), channel_id=1, source_target_pairs={{0,4},{1,5},{2,6},{3,7},{4,0},{5,1},{6,2},{7,3},{8,12},{9,13},{10,... | collective-permute-start | bytes 1585160 | tf_op jit(solution)/shard_map/ppermute | solution.py:357
  71.7 20.1 %collective-permute-start.28 = (bf16[2064,128]{1,0:T(8,128)(2,1)S(1)}, bf16[2064,128]{1,0:T(8,128)(2,1)S(1)}, u32[]{:S(2)}, u32[]{:S(2)}) collective-permute-start(bf16[2064,128]{1,0:T(8,128)(2,1)S(1)} %get-tuple-element.121), channel_id=1, source_target_pairs={{0,3},{1,2},{2,1},{3,0},{4,7},{5,6},{6,5},{7,4},{8,11},{9,10},{10,... | collective-permute-start | bytes 1585160 | tf_op jit(solution)/shard_map/ppermute | solution.py:357
  76.2 22.6 %collective-permute-start.15 = (bf16[2064,128]{1,0:T(8,128)(2,1)S(1)}, bf16[2064,128]{1,0:T(8,128)(2,1)S(1)}, u32[]{:S(2)}, u32[]{:S(2)}) collective-permute-start(bf16[2064,128]{1,0:T(8,128)(2,1)S(1)} %get-tuple-element.107), channel_id=1, source_target_pairs={{0,1},{1,0},{2,3},{3,2},{4,5},{5,4},{6,7},{7,6},{8,9},{9,8},{10,11... | collective-permute-start | bytes 1585160 | tf_op jit(solution)/shard_map/ppermute | solution.py:357
  87.5 12.0 %collective-permute-start.10 = (bf16[2064,128]{1,0:T(8,128)(2,1)S(1)}, bf16[2064,128]{1,0:T(8,128)(2,1)S(1)}, u32[]{:S(2)}, u32[]{:S(2)}) collective-permute-start(bf16[2064,128]{1,0:T(8,128)(2,1)S(1)} %get-tuple-element.99), channel_id=1, source_target_pairs={{0,12},{1,13},{2,14},{3,15},{4,8},{5,9},{6,10},{7,11},{8,4},{9,5},... | collective-permute-start | bytes 1585160 | tf_op jit(solution)/shard_map/ppermute | solution.py:357
  88.4 11.8 %collective-permute-start.5 = (bf16[2064,128]{1,0:T(8,128)(2,1)S(1)}, bf16[2064,128]{1,0:T(8,128)(2,1)S(1)}, u32[]{:S(2)}, u32[]{:S(2)}) collective-permute-start(bf16[2064,128]{1,0:T(8,128)(2,1)S(1)} %get-tuple-element.91), channel_id=1, source_target_pairs={{0,4},{1,5},{2,6},{3,7},{4,0},{5,1},{6,2},{7,3},{8,12},{9,13},{10,... | collective-permute-start | bytes 1585160 | tf_op jit(solution)/shard_map/ppermute | solution.py:357
  90.4 11.5 %collective-permute-start.1 = (bf16[2064,128]{1,0:T(8,128)(2,1)S(1)}, bf16[2064,128]{1,0:T(8,128)(2,1)S(1)}, u32[]{:S(2)}, u32[]{:S(2)}) collective-permute-start(bf16[2064,128]{1,0:T(8,128)(2,1)S(1)} %get-tuple-element.83), channel_id=1, source_target_pairs={{0,3},{1,2},{2,1},{3,0},{4,7},{5,6},{6,5},{7,4},{8,11},{9,10},{10,... | collective-permute-start | bytes 1585160 | tf_op jit(solution)/shard_map/ppermute | solution.py:357
  91.8 14.0 %collective-permute-start.43 = (bf16[1040,128]{1,0:T(8,128)(2,1)S(1)}, bf16[1040,128]{1,0:T(8,128)(2,1)S(1)}, u32[]{:S(2)}, u32[]{:S(2)}) collective-permute-start(bf16[1040,128]{1,0:T(8,128)(2,1)S(1)} %get-tuple-element.147), channel_id=1, source_target_pairs={{0,3},{1,2},{2,1},{3,0},{4,7},{5,6},{6,5},{7,4},{8,11},{9,10},{10,... | collective-permute-start | bytes 798728 | tf_op jit(solution)/shard_map/ppermute | solution.py:357
  98.9 7.0 %collective-permute-start.38 = (bf16[1040,128]{1,0:T(8,128)(2,1)S(1)}, bf16[1040,128]{1,0:T(8,128)(2,1)S(1)}, u32[]{:S(2)}, u32[]{:S(2)}) collective-permute-start(bf16[1040,128]{1,0:T(8,128)(2,1)S(1)} %get-tuple-element.139), channel_id=1, source_target_pairs={{0,1},{1,0},{2,3},{3,2},{4,5},{5,4},{6,7},{7,6},{8,9},{9,8},{10,11... | collective-permute-start | bytes 798728 | tf_op jit(solution)/shard_map/ppermute | solution.py:357
  99.5 9.1 %collective-permute-start.33 = (bf16[1040,128]{1,0:T(8,128)(2,1)S(1)}, bf16[1040,128]{1,0:T(8,128)(2,1)S(1)}, u32[]{:S(2)}, u32[]{:S(2)}) collective-permute-start(bf16[1040,128]{1,0:T(8,128)(2,1)S(1)} %get-tuple-element.131), channel_id=1, source_target_pairs={{0,12},{1,13},{2,14},{3,15},{4,8},{5,9},{6,10},{7,11},{8,4},{9,5},... | collective-permute-start | bytes 798728 | tf_op jit(solution)/shard_map/ppermute | solution.py:357
  100.2 9.6 %collective-permute-start.29 = (bf16[1040,128]{1,0:T(8,128)(2,1)S(1)}, bf16[1040,128]{1,0:T(8,128)(2,1)S(1)}, u32[]{:S(2)}, u32[]{:S(2)}) collective-permute-start(bf16[1040,128]{1,0:T(8,128)(2,1)S(1)} %get-tuple-element.123), channel_id=1, source_target_pairs={{0,4},{1,5},{2,6},{3,7},{4,0},{5,1},{6,2},{7,3},{8,12},{9,13},{10,... | collective-permute-start | bytes 798728 | tf_op jit(solution)/shard_map/ppermute | solution.py:357
  102.0 9.8 %collective-permute-start.16 = (bf16[1040,128]{1,0:T(8,128)(2,1)S(1)}, bf16[1040,128]{1,0:T(8,128)(2,1)S(1)}, u32[]{:S(2)}, u32[]{:S(2)}) collective-permute-start(bf16[1040,128]{1,0:T(8,128)(2,1)S(1)} %get-tuple-element.109), channel_id=1, source_target_pairs={{0,3},{1,2},{2,1},{3,0},{4,7},{5,6},{6,5},{7,4},{8,11},{9,10},{10,... | collective-permute-start | bytes 798728 | tf_op jit(solution)/shard_map/ppermute | solution.py:357
  105.9 7.2 %collective-permute-start.11 = (bf16[1040,128]{1,0:T(8,128)(2,1)S(1)}, bf16[1040,128]{1,0:T(8,128)(2,1)S(1)}, u32[]{:S(2)}, u32[]{:S(2)}) collective-permute-start(bf16[1040,128]{1,0:T(8,128)(2,1)S(1)} %get-tuple-element.101), channel_id=1, source_target_pairs={{0,1},{1,0},{2,3},{3,2},{4,5},{5,4},{6,7},{7,6},{8,9},{9,8},{10,11... | collective-permute-start | bytes 798728 | tf_op jit(solution)/shard_map/ppermute | solution.py:357
  105.9 7.4 %collective-permute-start.6 = (bf16[1040,128]{1,0:T(8,128)(2,1)S(1)}, bf16[1040,128]{1,0:T(8,128)(2,1)S(1)}, u32[]{:S(2)}, u32[]{:S(2)}) collective-permute-start(bf16[1040,128]{1,0:T(8,128)(2,1)S(1)} %get-tuple-element.93), channel_id=1, source_target_pairs={{0,12},{1,13},{2,14},{3,15},{4,8},{5,9},{6,10},{7,11},{8,4},{9,5},... | collective-permute-start | bytes 798728 | tf_op jit(solution)/shard_map/ppermute | solution.py:357
  108.6 9.8 %collective-permute-start.2 = (bf16[1040,128]{1,0:T(8,128)(2,1)S(1)}, bf16[1040,128]{1,0:T(8,128)(2,1)S(1)}, u32[]{:S(2)}, u32[]{:S(2)}) collective-permute-start(bf16[1040,128]{1,0:T(8,128)(2,1)S(1)} %get-tuple-element.85), channel_id=1, source_target_pairs={{0,4},{1,5},{2,6},{3,7},{4,0},{5,1},{6,2},{7,3},{8,12},{9,13},{10,... | collective-permute-start | bytes 798728 | tf_op jit(solution)/shard_map/ppermute | solution.py:357
  109.8 5.6 %collective-permute-start.44 = (bf16[528,128]{1,0:T(8,128)(2,1)S(1)}, bf16[528,128]{1,0:T(8,128)(2,1)S(1)}, u32[]{:S(2)}, u32[]{:S(2)}) collective-permute-start(bf16[528,128]{1,0:T(8,128)(2,1)S(1)} %get-tuple-element.149), channel_id=1, source_target_pairs={{0,4},{1,5},{2,6},{3,7},{4,0},{5,1},{6,2},{7,3},{8,12},{9,13},{10,... | collective-permute-start | bytes 405512 | tf_op jit(solution)/shard_map/ppermute | solution.py:357
  111.7 6.5 %collective-permute-start.39 = (bf16[528,128]{1,0:T(8,128)(2,1)S(1)}, bf16[528,128]{1,0:T(8,128)(2,1)S(1)}, u32[]{:S(2)}, u32[]{:S(2)}) collective-permute-start(bf16[528,128]{1,0:T(8,128)(2,1)S(1)} %get-tuple-element.141), channel_id=1, source_target_pairs={{0,3},{1,2},{2,1},{3,0},{4,7},{5,6},{6,5},{7,4},{8,11},{9,10},{10,... | collective-permute-start | bytes 405512 | tf_op jit(solution)/shard_map/ppermute | solution.py:357
  113.0 7.7 %collective-permute-start.34 = (bf16[528,128]{1,0:T(8,128)(2,1)S(1)}, bf16[528,128]{1,0:T(8,128)(2,1)S(1)}, u32[]{:S(2)}, u32[]{:S(2)}) collective-permute-start(bf16[528,128]{1,0:T(8,128)(2,1)S(1)} %get-tuple-element.133), channel_id=1, source_target_pairs={{0,1},{1,0},{2,3},{3,2},{4,5},{5,4},{6,7},{7,6},{8,9},{9,8},{10,11... | collective-permute-start | bytes 405512 | tf_op jit(solution)/shard_map/ppermute | solution.py:357
  113.3 10.1 %collective-permute-start.17 = (bf16[528,128]{1,0:T(8,128)(2,1)S(1)}, bf16[528,128]{1,0:T(8,128)(2,1)S(1)}, u32[]{:S(2)}, u32[]{:S(2)}) collective-permute-start(bf16[528,128]{1,0:T(8,128)(2,1)S(1)} %get-tuple-element.111), channel_id=1, source_target_pairs={{0,4},{1,5},{2,6},{3,7},{4,0},{5,1},{6,2},{7,3},{8,12},{9,13},{10,... | collective-permute-start | bytes 405512 | tf_op jit(solution)/shard_map/ppermute | solution.py:357
  115.4 8.5 %collective-permute-start.12 = (bf16[528,128]{1,0:T(8,128)(2,1)S(1)}, bf16[528,128]{1,0:T(8,128)(2,1)S(1)}, u32[]{:S(2)}, u32[]{:S(2)}) collective-permute-start(bf16[528,128]{1,0:T(8,128)(2,1)S(1)} %get-tuple-element.103), channel_id=1, source_target_pairs={{0,3},{1,2},{2,1},{3,0},{4,7},{5,6},{6,5},{7,4},{8,11},{9,10},{10,... | collective-permute-start | bytes 405512 | tf_op jit(solution)/shard_map/ppermute | solution.py:357
  118.3 6.9 %collective-permute-start.7 = (bf16[528,128]{1,0:T(8,128)(2,1)S(1)}, bf16[528,128]{1,0:T(8,128)(2,1)S(1)}, u32[]{:S(2)}, u32[]{:S(2)}) collective-permute-start(bf16[528,128]{1,0:T(8,128)(2,1)S(1)} %get-tuple-element.95), channel_id=1, source_target_pairs={{0,1},{1,0},{2,3},{3,2},{4,5},{5,4},{6,7},{7,6},{8,9},{9,8},{10,11... | collective-permute-start | bytes 405512 | tf_op jit(solution)/shard_map/ppermute | solution.py:357
  118.4 7.5 %collective-permute-start.30 = (bf16[528,128]{1,0:T(8,128)(2,1)S(1)}, bf16[528,128]{1,0:T(8,128)(2,1)S(1)}, u32[]{:S(2)}, u32[]{:S(2)}) collective-permute-start(bf16[528,128]{1,0:T(8,128)(2,1)S(1)} %get-tuple-element.125), channel_id=1, source_target_pairs={{0,12},{1,13},{2,14},{3,15},{4,8},{5,9},{6,10},{7,11},{8,4},{9,5},... | collective-permute-start | bytes 405512 | tf_op jit(solution)/shard_map/ppermute | solution.py:357
  120.7 7.5 %collective-permute-start.45 = (bf16[528,128]{1,0:T(8,128)(2,1)S(1)}, bf16[528,128]{1,0:T(8,128)(2,1)S(1)}, u32[]{:S(2)}, u32[]{:S(2)}) collective-permute-start(bf16[528,128]{1,0:T(8,128)(2,1)S(1)} %requantize.15), channel_id=1, source_target_pairs={{0,96},{16,112},{32,0},{48,16},{64,32},{80,48},{96,64},{112,80},{1... | collective-permute-start | bytes 405512 | tf_op jit(solution)/shard_map/ppermute | solution.py:363
  123.4 6.2 %collective-permute-start.40 = (bf16[528,128]{1,0:T(8,128)(2,1)S(1)}, bf16[528,128]{1,0:T(8,128)(2,1)S(1)}, u32[]{:S(2)}, u32[]{:S(2)}) collective-permute-start(bf16[528,128]{1,0:T(8,128)(2,1)S(1)} %requantize.14), channel_id=1, source_target_pairs={{0,64},{16,80},{32,96},{48,112},{64,0},{80,16},{96,32},{112,48},{1... | collective-permute-start | bytes 405512 | tf_op jit(solution)/shard_map/ppermute | solution.py:363
  123.9 6.7 %collective-permute-start.35 = (bf16[528,128]{1,0:T(8,128)(2,1)S(1)}, bf16[528,128]{1,0:T(8,128)(2,1)S(1)}, u32[]{:S(2)}, u32[]{:S(2)}) collective-permute-start(bf16[528,128]{1,0:T(8,128)(2,1)S(1)} %requantize.13), channel_id=1, source_target_pairs={{0,32},{16,48},{32,64},{48,80},{64,96},{80,112},{96,0},{112,16},{1... | collective-permute-start | bytes 405512 | tf_op jit(solution)/shard_map/ppermute | solution.py:363
  125.2 18.2 %collective-permute-start.3 = (bf16[528,128]{1,0:T(8,128)(2,1)S(1)}, bf16[528,128]{1,0:T(8,128)(2,1)S(1)}, u32[]{:S(2)}, u32[]{:S(2)}) collective-permute-start(bf16[528,128]{1,0:T(8,128)(2,1)S(1)} %get-tuple-element.87), channel_id=1, source_target_pairs={{0,12},{1,13},{2,14},{3,15},{4,8},{5,9},{6,10},{7,11},{8,4},{9,5},... | collective-permute-start | bytes 405512 | tf_op jit(solution)/shard_map/ppermute | solution.py:357
  125.9 17.6 %collective-permute-start.18 = (bf16[528,128]{1,0:T(8,128)(2,1)S(1)}, bf16[528,128]{1,0:T(8,128)(2,1)S(1)}, u32[]{:S(2)}, u32[]{:S(2)}) collective-permute-start(bf16[528,128]{1,0:T(8,128)(2,1)S(1)} %requantize.11), channel_id=1, source_target_pairs={{0,96},{16,112},{32,0},{48,16},{64,32},{80,48},{96,64},{112,80},{1... | collective-permute-start | bytes 405512 | tf_op jit(solution)/shard_map/ppermute | solution.py:363
  128.2 15.3 %collective-permute-start.13 = (bf16[528,128]{1,0:T(8,128)(2,1)S(1)}, bf16[528,128]{1,0:T(8,128)(2,1)S(1)}, u32[]{:S(2)}, u32[]{:S(2)}) collective-permute-start(bf16[528,128]{1,0:T(8,128)(2,1)S(1)} %requantize.10), channel_id=1, source_target_pairs={{0,64},{16,80},{32,96},{48,112},{64,0},{80,16},{96,32},{112,48},{1... | collective-permute-start | bytes 405512 | tf_op jit(solution)/shard_map/ppermute | solution.py:363
  129.6 13.9 %collective-permute-start.8 = (bf16[528,128]{1,0:T(8,128)(2,1)S(1)}, bf16[528,128]{1,0:T(8,128)(2,1)S(1)}, u32[]{:S(2)}, u32[]{:S(2)}) collective-permute-start(bf16[528,128]{1,0:T(8,128)(2,1)S(1)} %requantize.9), channel_id=1, source_target_pairs={{0,32},{16,48},{32,64},{48,80},{64,96},{80,112},{96,0},{112,16},{1... | collective-permute-start | bytes 405512 | tf_op jit(solution)/shard_map/ppermute | solution.py:363
  130.5 18.4 %copy-start.1 = (f32[64,1024]{1,0:T(8,128)S(1)}, f32[64,1024]{1,0:T(8,128)}, u32[]{:S(2)}) copy-start(f32[64,1024]{1,0:T(8,128)} %master.3) | copy-start | bytes 786436
  130.5 18.4 %copy-start.2 = (f32[64,1024]{1,0:T(8,128)S(1)}, f32[64,1024]{1,0:T(8,128)}, u32[]{:S(2)}) copy-start(f32[64,1024]{1,0:T(8,128)} %moment.3) | copy-start | bytes 786436
  130.5 18.4 %copy-start.3 = (f32[64,1024]{1,0:T(8,128)S(1)}, f32[64,1024]{1,0:T(8,128)}, u32[]{:S(2)}) copy-start(f32[64,1024]{1,0:T(8,128)} %second.3) | copy-start | bytes 786436
  130.8 18.1 %collective-permute-start.46 = (f32[256,128]{1,0:T(8,128)S(1)}, f32[256,128]{1,0:T(8,128)S(1)}, u32[]{:S(2)}, u32[]{:S(2)}) collective-permute-start(f32[256,128]{1,0:T(8,128)S(1)} %get-tuple-element.151), channel_id=1, source_target_pairs={{0,16},{16,0},{32,48},{48,32},{64,80},{80,64},{96,112},{112,96},{1... | collective-permute-start | bytes 393224 | tf_op jit(solution)/shard_map/ppermute | solution.py:365
  143.7 7.8 %collective-permute-start.19 = (f32[256,128]{1,0:T(8,128)S(1)}, f32[256,128]{1,0:T(8,128)S(1)}, u32[]{:S(2)}, u32[]{:S(2)}) collective-permute-start(f32[256,128]{1,0:T(8,128)S(1)} %get-tuple-element.113), channel_id=1, source_target_pairs={{0,16},{16,0},{32,48},{48,32},{64,80},{80,64},{96,112},{112,96},{1... | collective-permute-start | bytes 393224 | tf_op jit(solution)/shard_map/ppermute | solution.py:365
  149.1 4.0 %collective-permute-start.50 = (bf16[64,512]{1,0:T(8,128)(2,1)S(1)}, bf16[64,512]{1,0:T(8,128)(2,1)S(1)}, u32[]{:S(2)}, u32[]{:S(2)}) collective-permute-start(bf16[64,512]{1,0:T(8,128)(2,1)S(1)} %get-tuple-element.155.refs_14_), channel_id=1, source_target_pairs={{0,16},{16,0},{32,48},{48,32},{64,80},{80,64},{96,112},{112,96},{1... | collective-permute-start | bytes 196616 | tf_op jit(solution)/shard_map/ppermute | solution.py:368
  149.2 6.0 %collective-permute-start.49 = (bf16[64,512]{1,0:T(8,128)(2,1)S(1)}, bf16[64,512]{1,0:T(8,128)(2,1)S(1)}, u32[]{:S(2)}, u32[]{:S(2)}) collective-permute-start(bf16[64,512]{1,0:T(8,128)(2,1)S(1)} %get-tuple-element.155.refs_14_), channel_id=1, source_target_pairs={{0,96},{16,112},{32,0},{48,16},{64,32},{80,48},{96,64},{112,80},{1... | collective-permute-start | bytes 196616 | tf_op jit(solution)/shard_map/ppermute | solution.py:367
  149.5 6.4 %collective-permute-start.48 = (bf16[64,512]{1,0:T(8,128)(2,1)S(1)}, bf16[64,512]{1,0:T(8,128)(2,1)S(1)}, u32[]{:S(2)}, u32[]{:S(2)}) collective-permute-start(bf16[64,512]{1,0:T(8,128)(2,1)S(1)} %get-tuple-element.155.refs_14_), channel_id=1, source_target_pairs={{0,64},{16,80},{32,96},{48,112},{64,0},{80,16},{96,32},{112,48},{1... | collective-permute-start | bytes 196616 | tf_op jit(solution)/shard_map/ppermute | solution.py:367
  150.9 5.8 %collective-permute-start.47 = (bf16[64,512]{1,0:T(8,128)(2,1)S(1)}, bf16[64,512]{1,0:T(8,128)(2,1)S(1)}, u32[]{:S(2)}, u32[]{:S(2)}) collective-permute-start(bf16[64,512]{1,0:T(8,128)(2,1)S(1)} %get-tuple-element.155.refs_14_), channel_id=1, source_target_pairs={{0,32},{16,48},{32,64},{48,80},{64,96},{80,112},{96,0},{112,16},{1... | collective-permute-start | bytes 196616 | tf_op jit(solution)/shard_map/ppermute | solution.py:367
  151.7 5.9 %collective-permute-start.23 = (bf16[64,512]{1,0:T(8,128)(2,1)S(1)}, bf16[64,512]{1,0:T(8,128)(2,1)S(1)}, u32[]{:S(2)}, u32[]{:S(2)}) collective-permute-start(bf16[64,512]{1,0:T(8,128)(2,1)S(1)} %get-tuple-element.117.refs_3_), channel_id=1, source_target_pairs={{0,16},{16,0},{32,48},{48,32},{64,80},{80,64},{96,112},{112,96},{1... | collective-permute-start | bytes 196616 | tf_op jit(solution)/shard_map/ppermute | solution.py:368
  153.1 4.7 %collective-permute-start.22 = (bf16[64,512]{1,0:T(8,128)(2,1)S(1)}, bf16[64,512]{1,0:T(8,128)(2,1)S(1)}, u32[]{:S(2)}, u32[]{:S(2)}) collective-permute-start(bf16[64,512]{1,0:T(8,128)(2,1)S(1)} %get-tuple-element.117.refs_3_), channel_id=1, source_target_pairs={{0,96},{16,112},{32,0},{48,16},{64,32},{80,48},{96,64},{112,80},{1... | collective-permute-start | bytes 196616 | tf_op jit(solution)/shard_map/ppermute | solution.py:367
  155.2 4.6 %collective-permute-start.21 = (bf16[64,512]{1,0:T(8,128)(2,1)S(1)}, bf16[64,512]{1,0:T(8,128)(2,1)S(1)}, u32[]{:S(2)}, u32[]{:S(2)}) collective-permute-start(bf16[64,512]{1,0:T(8,128)(2,1)S(1)} %get-tuple-element.117.refs_3_), channel_id=1, source_target_pairs={{0,64},{16,80},{32,96},{48,112},{64,0},{80,16},{96,32},{112,48},{1... | collective-permute-start | bytes 196616 | tf_op jit(solution)/shard_map/ppermute | solution.py:367
  156.0 6.0 %collective-permute-start.20 = (bf16[64,512]{1,0:T(8,128)(2,1)S(1)}, bf16[64,512]{1,0:T(8,128)(2,1)S(1)}, u32[]{:S(2)}, u32[]{:S(2)}) collective-permute-start(bf16[64,512]{1,0:T(8,128)(2,1)S(1)} %get-tuple-element.117.refs_3_), channel_id=1, source_target_pairs={{0,32},{16,48},{32,64},{48,80},{64,96},{80,112},{96,0},{112,16},{1... | collective-permute-start | bytes 196616 | tf_op jit(solution)/shard_map/ppermute | solution.py:367
  156.7 5.9 %collective-permute-start.53 = (bf16[64,512]{1,0:T(8,128)(2,1)S(1)}, bf16[64,512]{1,0:T(8,128)(2,1)S(1)}, u32[]{:S(2)}, u32[]{:S(2)}) collective-permute-start(bf16[64,512]{1,0:T(8,128)(2,1)S(1)} %collective-permute-done.49.refs_17_), channel_id=1, source_target_pairs={{0,16},{16,0},{32,48},{48,32},{64,80},{80,64},{96,112},{112,96},{1... | collective-permute-start | bytes 196616 | tf_op jit(solution)/shard_map/ppermute | solution.py:368
  157.6 5.0 %collective-permute-start.52 = (bf16[64,512]{1,0:T(8,128)(2,1)S(1)}, bf16[64,512]{1,0:T(8,128)(2,1)S(1)}, u32[]{:S(2)}, u32[]{:S(2)}) collective-permute-start(bf16[64,512]{1,0:T(8,128)(2,1)S(1)} %collective-permute-done.48.refs_16_), channel_id=1, source_target_pairs={{0,16},{16,0},{32,48},{48,32},{64,80},{80,64},{96,112},{112,96},{1... | collective-permute-start | bytes 196616 | tf_op jit(solution)/shard_map/ppermute | solution.py:368
  157.7 4.9 %collective-permute-start.51 = (bf16[64,512]{1,0:T(8,128)(2,1)S(1)}, bf16[64,512]{1,0:T(8,128)(2,1)S(1)}, u32[]{:S(2)}, u32[]{:S(2)}) collective-permute-start(bf16[64,512]{1,0:T(8,128)(2,1)S(1)} %collective-permute-done.47.refs_15_), channel_id=1, source_target_pairs={{0,16},{16,0},{32,48},{48,32},{64,80},{80,64},{96,112},{112,96},{1... | collective-permute-start | bytes 196616 | tf_op jit(solution)/shard_map/ppermute | solution.py:368
  159.8 3.0 %collective-permute-start.26 = (bf16[64,512]{1,0:T(8,128)(2,1)S(1)}, bf16[64,512]{1,0:T(8,128)(2,1)S(1)}, u32[]{:S(2)}, u32[]{:S(2)}) collective-permute-start(bf16[64,512]{1,0:T(8,128)(2,1)S(1)} %collective-permute-done.22.refs_6_), channel_id=1, source_target_pairs={{0,16},{16,0},{32,48},{48,32},{64,80},{80,64},{96,112},{112,96},{1... | collective-permute-start | bytes 196616 | tf_op jit(solution)/shard_map/ppermute | solution.py:368
  161.9 1.6 collective-permute-start.25
  162.6 1.3 collective-permute-start.24

commit v2 on v0

v2 whole, which is shorter than its diff:
```python
import functools

import jax
import jax.numpy as jnp
from jax import lax
from jax.experimental import pallas as pl
from jax.experimental.pallas import tpu as pltpu
from jax.sharding import PartitionSpec as P

D = 8192
KV = 1024
TOK = 768
RUNS = KV // 128
HALF = KV // 2
PARTS = (2, 3, 0, 1)
F32 = jnp.float32
BF16 = jnp.bfloat16
MIB = 1 << 20
SMALL = pl.CostEstimate(flops=1, bytes_accessed=1, transcendentals=0)

MATCH = ((1, 0, 3, 2), (3, 2, 1, 0))


def bits(v):
    b = lax.shift_right_logical(v, 1)
    return (v ^ b) & 1, b


def local_perm(dim):
    m = MATCH[dim % 2]
    if dim < 2:
        return [(z * 4 + x, z * 4 + m[x]) for z in range(4) for x in range(4)]
    return [(z * 4 + x, m[z] * 4 + x) for z in range(4) for x in range(4)]


def y_perm(k):
    return [(n, ((n // 2 + k) % 4) * 2 + n % 2) for n in range(8)]


CORE_PERM = [(n, n ^ 1) for n in range(8)]


def pad16(n):
    return -(-n // 16) * 16


def code_rows(tiles):
    return tiles * KV


def msg_rows(tiles):
    return tiles * KV + pad16(tiles * RUNS)


def params(mib):
    return pltpu.CompilerParams(vmem_limit_bytes=mib * MIB)


def vmem():
    return pl.BlockSpec(memory_space=pltpu.VMEM)


def quantize(m):
    top = jnp.max(jnp.abs(m), axis=0, keepdims=True) + 1e-06
    scale = top.astype(BF16).astype(F32)
    return (m * (1.0 / scale)).astype(BF16), scale


def encode(m):
    top = jnp.max(jnp.abs(m), axis=0, keepdims=True) + 1e-30
    scale = top.astype(BF16).astype(F32)
    e = jnp.exp2(jnp.abs(m) * (250.0 / scale) - 125.0)
    return jnp.where(m < 0, -e, e).astype(BF16), scale


def decode(code, scale):
    y = code.astype(F32)
    m = (jnp.log2(jnp.abs(y)) + 125.0) * (scale * (1.0 / 250.0))
    return jnp.where(y < 0, -m, m)


def first_kernel(part, sent, load, first, tok, og_hbm, *refs):
    order = [(part + s) % 4 for s in range(4)]
    refs = list(refs)
    if not first:
        mine, ogt = refs.pop(0), refs.pop(0)
    refs.pop(0)
    out = refs.pop(0)
    if first:
        mine, ogt = refs.pop(0), refs.pop(0)
    if load is not None:
        ahead = refs.pop(0)
    sc, ogv, sem = refs
    me_l = lax.axis_index("local")
    me_n = lax.axis_index("node")
    y = lax.shift_right_logical(me_n, 1)
    ax, bx = bits(me_l & 3)
    az, bz = bits(lax.shift_right_logical(me_l, 2))

    def fetch(p, to, z, c, s):
        source = pl.multiple_of(((y + p) & 3) * 2048 + c * 1024 + z * 256, 256)
        to_lane = pl.multiple_of(c * 1024 + z * 256, 256)
        return pltpu.make_async_copy(tok.at[:, pl.ds(source, 256)], to.at[:, pl.ds(to_lane, 256)], sem.at[s])

    def place_z(a, b):
        zb = b ^ bz
        return 2 * zb + (a ^ az ^ zb)

    def pairs(t):
        lo, hi = t & 1, t >> 1 if isinstance(t, int) else lax.shift_right_logical(t, 1)
        return {0: [(0, lo, hi), (1, lo, hi)], 1: [(sent, lo, hi)], 2: [(lo, sent, hi)], 3: [(lo, hi, sent)]}[order[0]]

    wait, rest = {}, []
    if first:
        ogc = pltpu.make_async_copy(og_hbm, ogv, sem.at[16])
        ogc.start()
        used = []
        for t in range(4):
            for _, a, b in pairs(t):
                if (a, b) not in used:
                    used.append((a, b))
        late = [(a, b) for a in range(2) for b in range(2) if (a, b) not in used]
        for i, (a, b) in enumerate(used + late):
            cs = [fetch(part, mine, place_z(a, b), c, 2 * i + c) for c in range(2)]
            for cp in cs:
                cp.start()
            if i < len(used):
                wait[a, b] = cs
            else:
                rest += cs
    if load is not None:
        for z in range(4):
            for c in range(2):
                rest.append(fetch(load, ahead, z, c, 8 + 2 * z + c))
                rest[-1].start()
    if first:
        ogc.wait()
        ogt[...] = ogv[...].T

    def body(t, _):
        columns, places = [], []
        for x, a, b in pairs(t):
            for cp in wait.pop((a, b), ()) if first else ():
                cp.wait()
            lane = place_z(a, b) * 256 + (x ^ bx) * 128
            t0 = mine[:, pl.ds(pl.multiple_of(lane, 128), 128)]
            t1 = mine[:, pl.ds(pl.multiple_of(lane + 1024, 128), 128)]
            swap = (x ^ bx ^ ax) == 1
            even = jnp.concatenate([t0[:, :64], t1[:, :64]], axis=1)
            odd = jnp.concatenate([t0[:, 64:], t1[:, 64:]], axis=1)
            for d in (sent,) if order[0] == 0 else (0, 1):
                columns.append(jnp.where(swap, even, odd) if d else jnp.where(swap, odd, even))
                bit = (d, x, a, b)
                places.append(bit[order[1]] * 4 + bit[order[2]] * 2 + bit[order[3]])
        both = jnp.concatenate(columns, axis=1)
        grad = jnp.dot(ogt[...], both, preferred_element_type=F32)
        for k in range(RUNS):
            code, scale = quantize(grad[k * 128:(k + 1) * 128])
            for i, place in enumerate(places):
                row = place * KV + k * 128
                row = row if isinstance(row, int) else pl.multiple_of(row, 128)
                out[pl.ds(row, 128), :] = code[:, i * 128:(i + 1) * 128]
                sc[pl.ds(place * RUNS + k, 1), :] = scale[:, i * 128:(i + 1) * 128]
        return 0

    if first:
        for t in range(4):
            body(t, 0)
    else:
        lax.fori_loop(0, 4, body, 0)
    out[code_rows(8):, :] = sc[...].astype(BF16)
    for cp in rest:
        cp.wait()


def first_stage(tokens, out_grads, part, sent, load, mine, ogt, after):
    first = mine is None
    held = jax.ShapeDtypeStruct((TOK, 2048), BF16)
    made = jax.ShapeDtypeStruct((KV, TOK), BF16)
    out = [jax.ShapeDtypeStruct((msg_rows(8), 128), BF16)] + [held, made] * first + [held] * (load is not None)
    args = [] if first else [mine, ogt]
    anywhere = pl.BlockSpec(memory_space=pl.ANY)
    return pl.pallas_call(
        functools.partial(first_kernel, part, sent, load, first),
        out_shape=tuple(out),
        in_specs=[anywhere, anywhere] + [vmem()] * len(args) + [anywhere],
        out_specs=tuple(vmem() for _ in out),
        scratch_shapes=[
            pltpu.VMEM((pad16(8 * RUNS), 128), F32),
            pltpu.VMEM((TOK, KV) if first else (16, 128), BF16),
            pltpu.SemaphoreType.DMA((17,)),
        ],
        compiler_params=params(18),
        cost_estimate=SMALL,
        name=f"grad_{'send' if sent else 'keep'}_{part}",
    )(tokens, out_grads, *args, after)


def sum_kernel(tiles, kb, coded, n, *refs):
    half = tiles // 2
    keeps, recvs = refs[:n], refs[n:2 * n]
    keep_out, send_out, sc_keep, sc_recv, sc_send = refs[2 * n + 1:]
    rows = tiles * kb
    for j in range(n):
        sc_recv[j] = recvs[j][rows * 128:, :].astype(F32)
        if not coded:
            sc_keep[j] = keeps[j][rows * 128:, :].astype(F32)

    def total(j, block):
        r = pl.ds(pl.multiple_of(block * 128, 128), 128)
        scale = sc_recv[j, pl.ds(block, 1), :]
        if coded:
            return keeps[j][r, :] + decode(recvs[j][r, :], scale)
        return keeps[j][r, :].astype(F32) * sc_keep[j, pl.ds(block, 1), :] + recvs[j][r, :].astype(F32) * scale

    def place(j, block):
        if n == 1:
            return block
        return lax.div(block, kb) * (n * kb) + j * kb + lax.rem(block, kb)

    for j in range(n):
        def send_body(block, _):
            code, scale = encode(total(j, block + half * kb))
            to = place(j, block)
            send_out[pl.ds(pl.multiple_of(to * 128, 128), 128), :] = code
            sc_send[pl.ds(to, 1), :] = scale
            return 0

        lax.fori_loop(0, half * kb, send_body, 0, unroll=2)
    send_out[n * half * kb * 128:, :] = sc_send[...].astype(BF16)
    for j in range(n):
        def keep_body(block, _):
            keep_out[pl.ds(pl.multiple_of(place(j, block) * 128, 128), 128), :] = total(j, block)
            return 0

        lax.fori_loop(0, half * kb, keep_body, 0, unroll=2)


def sum_stage(keeps, recvs, tiles, kb, after):
    n = len(keeps)
    half = n * tiles // 2 * kb
    return pl.pallas_call(
        functools.partial(sum_kernel, tiles, kb, tiles < 8, n),
        out_shape=(
            jax.ShapeDtypeStruct((half * 128, 128), F32),
            jax.ShapeDtypeStruct((half * 128 + pad16(half), 128), BF16),
        ),
        in_specs=[vmem()] * (2 * n) + [pl.BlockSpec(memory_space=pl.ANY)],
        out_specs=(vmem(), vmem()),
        scratch_shapes=[
            pltpu.VMEM((n, pad16(tiles * kb), 128), F32),
            pltpu.VMEM((n, pad16(tiles * kb), 128), F32),
            pltpu.VMEM((pad16(half), 128), F32),
        ],
        compiler_params=params(16),
        cost_estimate=SMALL,
        name=f"sum_{tiles}",
    )(*keeps, *recvs, after)


def pack(lo, hi, core):
    first = jnp.concatenate([lo[:, :64], hi[:, :64]], axis=1)
    second = jnp.concatenate([lo[:, 64:], hi[:, 64:]], axis=1)
    return jnp.where(core == 0, first, second), jnp.where(core == 0, second, first)


def requantize_kernel(keep, recv, _, mine, other, sc):
    core = lax.axis_index("node") & 1
    sc[0] = recv[KV:KV + 16, :].astype(F32)
    for k in range(RUNS // 2):
        made = []
        for j in (k, k + RUNS // 2):
            rows = slice(j * 128, (j + 1) * 128)
            made.append(quantize(keep[rows, :] + decode(recv[rows, :], sc[0, j:j + 1, :])))
        codes = pack(made[0][0], made[1][0], core)
        scales = pack(made[0][1], made[1][1], core)
        for i, out in enumerate((mine, other)):
            out[k * 128:(k + 1) * 128, :] = codes[i]
            sc[1 + i, k:k + 1, :] = scales[i]
    mine[HALF:, :] = sc[1].astype(BF16)
    other[HALF:, :] = sc[2].astype(BF16)


def requantize_stage(keep, recv, after):
    out = jax.ShapeDtypeStruct((HALF + 16, 128), BF16)
    return pl.pallas_call(
        requantize_kernel,
        out_shape=(out, out),
        in_specs=[vmem(), vmem(), pl.BlockSpec(memory_space=pl.ANY)],
        out_specs=(vmem(), vmem()),
        scratch_shapes=[pltpu.VMEM((3, 16, 128), F32)],
        compiler_params=params(8),
        cost_estimate=SMALL,
        name="requantize",
    )(keep, recv, after)


def core_sum_kernel(coded, mine, recv, _, out, sc):
    sc[0] = mine[HALF:, :].astype(F32)
    sc[1] = recv[HALF:, :].astype(F32)
    for k in range(RUNS // 2):
        rows = slice(k * 128, (k + 1) * 128)
        m = mine[rows, :].astype(F32) * sc[0, k:k + 1, :] + recv[rows, :].astype(F32) * sc[1, k:k + 1, :]
        if coded:
            m, sc[2, k:k + 1, :] = encode(m)
        out[rows, :] = m
    if coded:
        out[HALF:, :] = sc[2].astype(BF16)


def core_sum_stage(mine, recv, coded, after):
    out = jax.ShapeDtypeStruct((HALF + 16, 128), BF16) if coded else jax.ShapeDtypeStruct((HALF, 128), F32)
    return pl.pallas_call(
        functools.partial(core_sum_kernel, coded),
        out_shape=out,
        in_specs=[vmem(), vmem(), pl.BlockSpec(memory_space=pl.ANY)],
        out_specs=vmem(),
        scratch_shapes=[pltpu.VMEM((3, 16, 128), F32)],
        compiler_params=params(8),
        cost_estimate=SMALL,
        name="core_sum",
    )(mine, recv, after)


def adam_rule(grad, master, moment, second):
    m = 0.9 * moment + 0.1 * grad
    s = 0.95 * second + 0.05 * grad * grad
    update = m / (1.0 - 0.9**10) / (jnp.sqrt(s / (1.0 - 0.95**10)) + 1e-08) + 0.1 * master
    return master - 0.05 * update, m, s


def weight_kernel(own, a, b, c, master, moment, second, weight, grad, sc, g):
    for i, r in enumerate((a, b, c)):
        sc[i] = r[HALF:, :].astype(F32)
    for k in range(RUNS // 2):
        rows = slice(k * 128, (k + 1) * 128)
        m = own[rows, :]
        for i, r in enumerate((a, b, c)):
            m = m + decode(r[rows, :], sc[i, k:k + 1, :])
        g[rows, :] = m
    t = g[...].T
    whole = jnp.concatenate([t[:64], t[64:]], axis=1)
    grad[...] = whole
    weight[...] = adam_rule(whole, master[...], moment[...], second[...])[0].astype(BF16)


def weight_stage(own, others, master, moment, second):
    return pl.pallas_call(
        weight_kernel,
        out_shape=(jax.ShapeDtypeStruct((64, KV), BF16), jax.ShapeDtypeStruct((64, KV), F32)),
        in_specs=[vmem()] * 7,
        out_specs=(vmem(),) * 2,
        scratch_shapes=[pltpu.VMEM((3, 16, 128), F32), pltpu.VMEM((HALF, 128), F32)],
        compiler_params=params(8),
        cost_estimate=SMALL,
        name="adam_weight",
    )(own, *others, master, moment, second)


def adam_kernel(grad, master, moment, second, _, new_master, new_moment, new_second):
    new_master[...], new_moment[...], new_second[...] = adam_rule(grad[...], master[...], moment[...], second[...])


def adam_stage(grad, master, moment, second, after):
    f = jax.ShapeDtypeStruct((64, KV), F32)
    return pl.pallas_call(
        adam_kernel,
        out_shape=(f, f, f),
        in_specs=[vmem()] * 4 + [pl.BlockSpec(memory_space=pl.ANY)],
        out_specs=(vmem(),) * 3,
        compiler_params=params(8),
        cost_estimate=pl.CostEstimate(flops=64 * KV * 20, bytes_accessed=64 * KV * 32, transcendentals=0),
        name="adam",
    )(grad, master, moment, second, after)


def gather_kernel(*refs):
    me_n = lax.axis_index("node")
    y = lax.shift_right_logical(me_n, 1)
    core = me_n & 1
    weight = refs[8]
    for k in range(4):
        src = ((y - k) & 3) * 2
        weight[src + core] = refs[k][...]
        weight[src + 1 - core] = refs[4 + k][...]


def gather_stage(pieces):
    return pl.pallas_call(
        gather_kernel,
        out_shape=jax.ShapeDtypeStruct((8, 64, KV), BF16),
        in_specs=[vmem()] * 8,
        out_specs=vmem(),
        compiler_params=params(16),
        cost_estimate=SMALL,
        name="gather_weights",
    )(*pieces)


def local(tokens, out_grads, master, moment, second):
    tokens = pltpu.with_memory_space_constraint(tokens, pltpu.HBM)
    out_grads = pltpu.with_memory_space_constraint(out_grads, pltpu.HBM)
    keep, recv, held = {}, {}, {}
    after, ogt = out_grads, None
    for i, p in enumerate(PARTS):
        load = PARTS[i + 1] if i < 3 else None
        send, *more = first_stage(tokens, out_grads, p, 1, load, held.get(p), ogt, after)
        if i == 0:
            held[p], ogt = more.pop(0), more.pop(0)
        if load is not None:
            held[load], = more
        after = send
        recv[p] = lax.ppermute(send, "local", local_perm(p))
    for p in PARTS:
        keep[p], = first_stage(tokens, out_grads, p, 0, None, held[p], ogt, after)
        after = keep[p]
    for step, tiles in ((1, 8), (2, 4), (3, 2)):
        for p in PARTS:
            keep[p], send = sum_stage([keep[p]], [recv[p]], tiles, RUNS, after)
            after = send
            recv[p] = lax.ppermute(send, "local", local_perm((p + step) % 4))
    mine, other = {}, {}
    for p in PARTS:
        mine[p], other[p] = requantize_stage(keep[p], recv[p], after)
        after = mine[p]
        other[p] = lax.ppermute(other[p], "node", CORE_PERM)
    parts = {}
    for p in PARTS:
        after = core_sum_stage(mine[p], other[p], p > 0, after)
        parts[p] = lax.ppermute(after, "node", y_perm(p)) if p else after
    w, grad = weight_stage(parts[0], [parts[p] for p in (1, 2, 3)], master, moment, second)
    own = [w] + [lax.ppermute(w, "node", y_perm(k)) for k in (1, 2, 3)]
    a, b, d = adam_stage(grad, master, moment, second, w)
    weight = gather_stage(own + [lax.ppermute(v, "node", CORE_PERM) for v in own])
    return a, b, d, weight


def solution(mesh):
    rows = P(("node", "local"), None)
    return jax.shard_map(
        local,
        mesh=mesh,
        in_specs=(rows,) * 5,
        out_specs=(rows, rows, rows, P(None, "local", None)),
        check_vma=False,
    )
```

time: 533 us -> 143 us (0.27)
  waiting for transfers between devices: 228 us -> 49.4 us
  local copies, waits for them, and re-layouts: 155 us -> 0.01 us
  other arithmetic: 85.4 us -> 0 us
  Pallas kernels: 0 us -> 43.4 us
  starting transfers between devices: 26.1 us -> 49.1 us
  matrix products: 21.9 us -> 0 us
  between operations: 14.2 us -> 0.91 us
    all_to_all x4 -> x0, waiting for transfers between devices: 206 us -> none  [the longest x1 195 us: local(): lax.all_to_all(codes, 'local', split_axis=1, concat_axis=1, tiled=True)]
    div x4 -> x0, local copies, waits for them, and re-layouts: 57.1 us -> none  [quantize(): codes = (blocks / scale.astype(jnp.float32)[..., None]).astype(jnp.bfloat16)]
    mul x4 -> x0, local copies, waits for them, and re-layouts: 52.9 us -> none  [restore(): return (blocks * scale.astype(jnp.float32)[..., None]).reshape(shape)]
    ppermute x0 -> x30, waiting for transfers between devices: none -> 49.4 us  [the longest x12 21.3 us: local(): recv[p] = lax.ppermute(send, 'local', local_perm((p + step) % 4))]
    ppermute x0 -> x30, starting transfers between devices: none -> 49.1 us  [the longest x12 18.6 us: local(): recv[p] = lax.ppermute(send, 'local', local_perm((p + step) % 4))]
    pallas_call x0 -> x31, Pallas kernels: none -> 43.4 us  [the longest x8 26 us: first_stage(): pl.pallas_call(functools.partial(first_kernel, part, sent, load, first),...]
    convert_element_type x5 -> x0, other arithmetic: 33.3 us -> none  [the longest x2 31.3 us: quantize(): codes = (blocks / scale.astype(jnp.float32)[..., None]).astype(jnp.bfloat16)]
    all_to_all x4 -> x0, starting transfers between devices: 26.1 us -> none  [the longest x1 8.44 us: local(): lax.all_to_all(scale, 'local', split_axis=1, concat_axis=1, tiled=True)]
  transfers between devices with their start and end apart: 5 -> 30, of which waited for: 4 -> 14; matrix products, arithmetic and copies ran while one was open for 29% -> 0% of each run, Pallas kernels for 0% -> 26%
where the time goes in v2:
time: 143 us
  waiting for transfers between devices  49.4 us (35%)
  starting transfers between devices  49.1 us (34%)
  Pallas kernels  43.4 us (30%)
    pallas_call x8, Pallas kernels, first_stage(): pl.pallas_call(functools.partial(first_kernel, part, sent, load, first),...  26 us
    ppermute x12, waiting for transfers between devices, local(): recv[p] = lax.ppermute(send, 'local', local_perm((p + step) % 4))  21.3 us
    ppermute x4, waiting for transfers between devices, local(): recv[p] = lax.ppermute(send, 'local', local_perm(p))  20.9 us
    ppermute x12, starting transfers between devices, local(): recv[p] = lax.ppermute(send, 'local', local_perm((p + step) % 4))  18.6 us
    pallas_call x12, Pallas kernels, sum_stage(): pl.pallas_call(functools.partial(sum_kernel, tiles, kb, tiles < 8, n), ou...  13 us
    ppermute x4, starting transfers between devices, local(): recv[p] = lax.ppermute(send, 'local', local_perm(p))  8.06 us
    ppermute x4, starting transfers between devices, local(): other[p] = lax.ppermute(other[p], 'node', CORE_PERM)  6.99 us
    ppermute x4, starting transfers between devices, local(): lax.ppermute(v, 'node', CORE_PERM)  6.92 us
  transfers between devices with their start and end apart: 30, of which 14 were waited for; matrix products, arithmetic and copies ran while one was open for 0% of the time, Pallas kernels for 26%

profile of v2, /device:TPU:1, one launch (start us, length us, event | category | flops | bytes accessed | tf_op | source)
XLA Modules:
  0.0 142.8 jit_solution(9530474815918377035)
XLA Ops:
  0.6 4.4 %grad_send_2.1 = (bf16[8256,128]{1,0:T(8,128)(2,1)S(1)}, bf16[768,2048]{1,0:T(8,128)(2,1)S(1)}, bf16[1024,768]{1,0:T(8,128)(2,1)S(1)}, bf16[768,2048]{1,0:T(8,128)(2,1)S(1)}) custom-call(bf16[768,8192]{1,0:T(8,128)(2,1)} %tok.15, bf16[768,1024]{1,0:T(8,128)(2,1)} %og_hbm.15, bf16[768,1024]{1,0:T(8,128)(2,1)} %og_hbm.15), custom_call_target="tpu_custom_call" | custom-call | flops 1 | bytes 1 | tf_op jit(solution)/shard_map/grad_send_2/pallas_call | solution.py:183
  5.0 2.5 %collective-permute-start.2 = (bf16[8256,128]{1,0:T(8,128)(2,1)S(1)}, bf16[8256,128]{1,0:T(8,128)(2,1)S(1)}, u32[]{:S(2)}, u32[]{:S(2)}) collective-permute-start(bf16[8256,128]{1,0:T(8,128)(2,1)S(1)} %get-tuple-element.51.refs_2_), channel_id=1, source_target_pairs={{0,4},{1,5},{2,6},{3,7},{4,0},{5,1},{6,2},{7,3},{8,12},{9,13},{10,... | collective-permute-start | bytes 6340616 | tf_op jit(solution)/shard_map/ppermute | solution.py:413
  7.6 3.0 %grad_send_3.1 = (bf16[8256,128]{1,0:T(8,128)(2,1)S(1)}, bf16[768,2048]{1,0:T(8,128)(2,1)S(1)}) custom-call(bf16[768,8192]{1,0:T(8,128)(2,1)} %tok.15, bf16[768,1024]{1,0:T(8,128)(2,1)} %og_hbm.15, bf16[768,2048]{1,0:T(8,128)(2,1)S(1)} %get-tuple-element.49.refs_0_, bf16[1024,768]{1,0:T(8,128)(2,1)S(1)} %get-tuple-element.50.refs_1_, ...), custom_call_target="tpu_custom_call" | custom-call | flops 1 | bytes 1 | tf_op jit(solution)/shard_map/grad_send_3/pallas_call | solution.py:183
  10.6 2.3 %collective-permute-start.1 = (bf16[8256,128]{1,0:T(8,128)(2,1)S(1)}, bf16[8256,128]{1,0:T(8,128)(2,1)S(1)}, u32[]{:S(2)}, u32[]{:S(2)}) collective-permute-start(bf16[8256,128]{1,0:T(8,128)(2,1)S(1)} %get-tuple-element.54.refs_2_), channel_id=1, source_target_pairs={{0,12},{1,13},{2,14},{3,15},{4,8},{5,9},{6,10},{7,11},{8,4},{9,5},... | collective-permute-start | bytes 6340616 | tf_op jit(solution)/shard_map/ppermute | solution.py:413
  12.9 3.3 %grad_send_0.1 = (bf16[8256,128]{1,0:T(8,128)(2,1)S(1)}, bf16[768,2048]{1,0:T(8,128)(2,1)S(1)}) custom-call(bf16[768,8192]{1,0:T(8,128)(2,1)} %tok.15, bf16[768,1024]{1,0:T(8,128)(2,1)} %og_hbm.15, bf16[768,2048]{1,0:T(8,128)(2,1)S(1)} %get-tuple-element.52.refs_0_, bf16[1024,768]{1,0:T(8,128)(2,1)S(1)} %get-tuple-element.50.refs_1_, ...), custom_call_target="tpu_custom_call" | custom-call | flops 1 | bytes 1 | tf_op jit(solution)/shard_map/grad_send_0/pallas_call | solution.py:183
  16.2 1.3 collective-permute-start
  17.5 3.0 %grad_send_1.1.refs_2_ = bf16[8256,128]{1,0:T(8,128)(2,1)S(1)} custom-call(bf16[768,8192]{1,0:T(8,128)(2,1)} %tok.15, bf16[768,1024]{1,0:T(8,128)(2,1)} %og_hbm.15, bf16[768,2048]{1,0:T(8,128)(2,1)S(1)} %get-tuple-element.55.refs_0_, bf16[1024,768]{1,0:T(8,128)(2,1)S(1)} %get-tuple-element.50.refs_1_, bf16[8256,128]{1,0:T(8,128)(2,1)S(1)} %get-tuple-element.56.refs_2_), custom_call_target="tpu_custom_call" | custom-call | flops 1 | bytes 1 | tf_op jit(solution)/shard_map/grad_send_1/pallas_call | solution.py:183
  20.5 1.9 %collective-permute-start.6 = (bf16[8256,128]{1,0:T(8,128)(2,1)S(1)}, bf16[8256,128]{1,0:T(8,128)(2,1)S(1)}, u32[]{:S(2)}, u32[]{:S(2)}) collective-permute-start(bf16[8256,128]{1,0:T(8,128)(2,1)S(1)} %grad_send_1.1.refs_2_), channel_id=1, source_target_pairs={{0,3},{1,2},{2,1},{3,0},{4,7},{5,6},{6,5},{7,4},{8,11},{9,10},{10,... | collective-permute-start | bytes 6340616 | tf_op jit(solution)/shard_map/ppermute | solution.py:413
  22.4 3.0 %grad_keep_2.1.refs_2_.refs_0_ = bf16[8256,128]{1,0:T(8,128)(2,1)S(1)} custom-call(bf16[768,8192]{1,0:T(8,128)(2,1)} %tok.15, bf16[768,1024]{1,0:T(8,128)(2,1)} %og_hbm.15, bf16[768,2048]{1,0:T(8,128)(2,1)S(1)} %get-tuple-element.53.refs_0_, bf16[1024,768]{1,0:T(8,128)(2,1)S(1)} %get-tuple-element.50.refs_1_, bf16[8256,128]{1,0:T(8,128)(2,1)S(1)} %grad_send_1.1.refs_2_), custom_call_target="tpu_custom_call" | custom-call | flops 1 | bytes 1 | tf_op jit(solution)/shard_map/grad_keep_2/pallas_call | solution.py:183
  25.4 3.0 %grad_keep_3.1.refs_2_.refs_0_ = bf16[8256,128]{1,0:T(8,128)(2,1)S(1)} custom-call(bf16[768,8192]{1,0:T(8,128)(2,1)} %tok.15, bf16[768,1024]{1,0:T(8,128)(2,1)} %og_hbm.15, bf16[768,2048]{1,0:T(8,128)(2,1)S(1)} %get-tuple-element.49.refs_0_, bf16[1024,768]{1,0:T(8,128)(2,1)S(1)} %get-tuple-element.50.refs_1_, bf16[8256,128]{1,0:T(8,128)(2,1)S(1)} %grad_keep_2.1.refs_2_.refs_0_), custom_call_target="tpu_custom_call" | custom-call | flops 1 | bytes 1 | tf_op jit(solution)/shard_map/grad_keep_3/pallas_call | solution.py:183
  28.5 3.3 %grad_keep_0.1.refs_2_.refs_0_ = bf16[8256,128]{1,0:T(8,128)(2,1)S(1)} custom-call(bf16[768,8192]{1,0:T(8,128)(2,1)} %tok.15, bf16[768,1024]{1,0:T(8,128)(2,1)} %og_hbm.15, bf16[768,2048]{1,0:T(8,128)(2,1)S(1)} %get-tuple-element.52.refs_0_, bf16[1024,768]{1,0:T(8,128)(2,1)S(1)} %get-tuple-element.50.refs_1_, bf16[8256,128]{1,0:T(8,128)(2,1)S(1)} %grad_keep_3.1.refs_2_.refs_0_), custom_call_target="tpu_custom_call" | custom-call | flops 1 | bytes 1 | tf_op jit(solution)/shard_map/grad_keep_0/pallas_call | solution.py:183
  31.8 3.0 %grad_keep_1.1.refs_2_.refs_0_ = bf16[8256,128]{1,0:T(8,128)(2,1)S(1)} custom-call(bf16[768,8192]{1,0:T(8,128)(2,1)} %tok.15, bf16[768,1024]{1,0:T(8,128)(2,1)} %og_hbm.15, bf16[768,2048]{1,0:T(8,128)(2,1)S(1)} %get-tuple-element.55.refs_0_, bf16[1024,768]{1,0:T(8,128)(2,1)S(1)} %get-tuple-element.50.refs_1_, bf16[8256,128]{1,0:T(8,128)(2,1)S(1)} %grad_keep_0.1.refs_2_.refs_0_), custom_call_target="tpu_custom_call" | custom-call | flops 1 | bytes 1 | tf_op jit(solution)/shard_map/grad_keep_1/pallas_call | solution.py:183
  34.8 18.5 %collective-permute-done.2.refs_1_ = bf16[8256,128]{1,0:T(8,128)(2,1)S(1)} collective-permute-done((bf16[8256,128]{1,0:T(8,128)(2,1)S(1)}, bf16[8256,128]{1,0:T(8,128)(2,1)S(1)}, u32[]{:S(2)}, u32[]{:S(2)}) %collective-permute-start.2) | collective-permute-done | bytes 2113568 | tf_op jit(solution)/shard_map/ppermute | solution.py:413
  53.3 1.6 %sum_8.4 = (f32[4096,128]{1,0:T(8,128)S(1)}, bf16[4128,128]{1,0:T(8,128)(2,1)S(1)}) custom-call(bf16[8256,128]{1,0:T(8,128)(2,1)S(1)} %grad_keep_2.1.refs_2_.refs_0_, bf16[8256,128]{1,0:T(8,128)(2,1)S(1)} %collective-permute-done.2.refs_1_, bf16[8256,128]{1,0:T(8,128)(2,1)S(1)} %grad_keep_1.1.refs_2_.refs_0_), custom_call_target="tpu_custom_call" | custom-call | flops 1 | bytes 1 | tf_op jit(solution)/shard_map/sum_8/pallas_call | solution.py:242
  54.9 3.4 %collective-permute-start.5 = (bf16[4128,128]{1,0:T(8,128)(2,1)S(1)}, bf16[4128,128]{1,0:T(8,128)(2,1)S(1)}, u32[]{:S(2)}, u32[]{:S(2)}) collective-permute-start(bf16[4128,128]{1,0:T(8,128)(2,1)S(1)} %get-tuple-element.57.refs_2_), channel_id=1, source_target_pairs={{0,12},{1,13},{2,14},{3,15},{4,8},{5,9},{6,10},{7,11},{8,4},{9,5},... | collective-permute-start | bytes 3170312 | tf_op jit(solution)/shard_map/ppermute | solution.py:421
  58.4 1.6 %sum_8.5 = (f32[4096,128]{1,0:T(8,128)S(1)}, bf16[4128,128]{1,0:T(8,128)(2,1)S(1)}) custom-call(bf16[8256,128]{1,0:T(8,128)(2,1)S(1)} %grad_keep_3.1.refs_2_.refs_0_, bf16[8256,128]{1,0:T(8,128)(2,1)S(1)} %collective-permute-done.1.refs_1_, bf16[4128,128]{1,0:T(8,128)(2,1)S(1)} %get-tuple-element.57.refs_2_), custom_call_target="tpu_custom_call" | custom-call | flops 1 | bytes 1 | tf_op jit(solution)/shard_map/sum_8/pallas_call | solution.py:242
  60.0 1.3 collective-permute-start.4
  61.3 1.3 collective-permute-done.refs_1_
  62.6 1.6 %sum_8.6 = (f32[4096,128]{1,0:T(8,128)S(1)}, bf16[4128,128]{1,0:T(8,128)(2,1)S(1)}) custom-call(bf16[8256,128]{1,0:T(8,128)(2,1)S(1)} %grad_keep_0.1.refs_2_.refs_0_, bf16[8256,128]{1,0:T(8,128)(2,1)S(1)} %collective-permute-done.refs_1_, bf16[4128,128]{1,0:T(8,128)(2,1)S(1)} %get-tuple-element.58.refs_2_), custom_call_target="tpu_custom_call" | custom-call | flops 1 | bytes 1 | tf_op jit(solution)/shard_map/sum_8/pallas_call | solution.py:242
  64.2 2.6 %collective-permute-start.3 = (bf16[4128,128]{1,0:T(8,128)(2,1)S(1)}, bf16[4128,128]{1,0:T(8,128)(2,1)S(1)}, u32[]{:S(2)}, u32[]{:S(2)}) collective-permute-start(bf16[4128,128]{1,0:T(8,128)(2,1)S(1)} %get-tuple-element.60.refs_2_), channel_id=1, source_target_pairs={{0,3},{1,2},{2,1},{3,0},{4,7},{5,6},{6,5},{7,4},{8,11},{9,10},{10,... | collective-permute-start | bytes 3170312 | tf_op jit(solution)/shard_map/ppermute | solution.py:421
  66.7 1.1 collective-permute-done.6.refs_1_
  67.8 1.6 %sum_8.7 = (f32[4096,128]{1,0:T(8,128)S(1)}, bf16[4128,128]{1,0:T(8,128)(2,1)S(1)}) custom-call(bf16[8256,128]{1,0:T(8,128)(2,1)S(1)} %grad_keep_1.1.refs_2_.refs_0_, bf16[8256,128]{1,0:T(8,128)(2,1)S(1)} %collective-permute-done.6.refs_1_, bf16[4128,128]{1,0:T(8,128)(2,1)S(1)} %get-tuple-element.60.refs_2_), custom_call_target="tpu_custom_call" | custom-call | flops 1 | bytes 1 | tf_op jit(solution)/shard_map/sum_8/pallas_call | solution.py:242
  69.4 0.8 collective-permute-start.10
  70.2 10.9 %collective-permute-done.5.refs_1_ = bf16[4128,128]{1,0:T(8,128)(2,1)S(1)} collective-permute-done((bf16[4128,128]{1,0:T(8,128)(2,1)S(1)}, bf16[4128,128]{1,0:T(8,128)(2,1)S(1)}, u32[]{:S(2)}, u32[]{:S(2)}) %collective-permute-start.5) | collective-permute-done | bytes 1056800 | tf_op jit(solution)/shard_map/ppermute | solution.py:421
  81.1 1.1 sum_4.4
  82.2 1.3 collective-permute-start.9
  83.5 2.0 %collective-permute-done.4.refs_1_ = bf16[4128,128]{1,0:T(8,128)(2,1)S(1)} collective-permute-done((bf16[4128,128]{1,0:T(8,128)(2,1)S(1)}, bf16[4128,128]{1,0:T(8,128)(2,1)S(1)}, u32[]{:S(2)}, u32[]{:S(2)}) %collective-permute-start.4) | collective-permute-done | bytes 1056800 | tf_op jit(solution)/shard_map/ppermute | solution.py:421
  85.5 1.1 sum_4.5
  86.6 2.6 %collective-permute-start.8 = (bf16[2064,128]{1,0:T(8,128)(2,1)S(1)}, bf16[2064,128]{1,0:T(8,128)(2,1)S(1)}, u32[]{:S(2)}, u32[]{:S(2)}) collective-permute-start(bf16[2064,128]{1,0:T(8,128)(2,1)S(1)} %get-tuple-element.65.refs_2_), channel_id=1, source_target_pairs={{0,3},{1,2},{2,1},{3,0},{4,7},{5,6},{6,5},{7,4},{8,11},{9,10},{10,... | collective-permute-start | bytes 1585160 | tf_op jit(solution)/shard_map/ppermute | solution.py:421
  89.2 0.8 collective-permute-done.3.refs_1_
  90.0 1.1 sum_4.6
  91.1 0.7 collective-permute-start.7
  91.9 1.1 sum_4.7
  93.0 1.6 %collective-permute-start.14 = (bf16[2064,128]{1,0:T(8,128)(2,1)S(1)}, bf16[2064,128]{1,0:T(8,128)(2,1)S(1)}, u32[]{:S(2)}, u32[]{:S(2)}) collective-permute-start(bf16[2064,128]{1,0:T(8,128)(2,1)S(1)} %get-tuple-element.71.refs_2_), channel_id=1, source_target_pairs={{0,12},{1,13},{2,14},{3,15},{4,8},{5,9},{6,10},{7,11},{8,4},{9,5},... | collective-permute-start | bytes 1585160 | tf_op jit(solution)/shard_map/ppermute | solution.py:421
  94.5 2.3 %collective-permute-done.9.refs_1_ = bf16[2064,128]{1,0:T(8,128)(2,1)S(1)} collective-permute-done((bf16[2064,128]{1,0:T(8,128)(2,1)S(1)}, bf16[2064,128]{1,0:T(8,128)(2,1)S(1)}, u32[]{:S(2)}, u32[]{:S(2)}) %collective-permute-start.9) | collective-permute-done | bytes 528416 | tf_op jit(solution)/shard_map/ppermute | solution.py:421
  96.8 0.5 sum_2.4
  97.4 2.6 %collective-permute-start.13 = (bf16[1040,128]{1,0:T(8,128)(2,1)S(1)}, bf16[1040,128]{1,0:T(8,128)(2,1)S(1)}, u32[]{:S(2)}, u32[]{:S(2)}) collective-permute-start(bf16[1040,128]{1,0:T(8,128)(2,1)S(1)} %get-tuple-element.72.refs_2_), channel_id=1, source_target_pairs={{0,3},{1,2},{2,1},{3,0},{4,7},{5,6},{6,5},{7,4},{8,11},{9,10},{10,... | collective-permute-start | bytes 798728 | tf_op jit(solution)/shard_map/ppermute | solution.py:421
  100.0 1.9 %collective-permute-done.8.refs_1_ = bf16[2064,128]{1,0:T(8,128)(2,1)S(1)} collective-permute-done((bf16[2064,128]{1,0:T(8,128)(2,1)S(1)}, bf16[2064,128]{1,0:T(8,128)(2,1)S(1)}, u32[]{:S(2)}, u32[]{:S(2)}) %collective-permute-start.8) | collective-permute-done | bytes 528416 | tf_op jit(solution)/shard_map/ppermute | solution.py:421
  101.8 0.5 sum_2.5
  102.4 0.7 collective-permute-start.12
  103.1 0.5 sum_2.6
  103.7 0.9 collective-permute-start.11
  104.6 0.5 sum_2.7
  105.2 2.3 %collective-permute-done.13.recv = bf16[1040,128]{1,0:T(8,128)(2,1)S(1)} collective-permute-done((bf16[1040,128]{1,0:T(8,128)(2,1)S(1)}, bf16[1040,128]{1,0:T(8,128)(2,1)S(1)}, u32[]{:S(2)}, u32[]{:S(2)}) %collective-permute-start.13) | collective-permute-done | bytes 266272 | tf_op jit(solution)/shard_map/ppermute | solution.py:421
  107.9 1.1 collective-permute-done.12.recv
  109.4 4.3 %collective-permute-start.16 = (bf16[528,128]{1,0:T(8,128)(2,1)S(1)}, bf16[528,128]{1,0:T(8,128)(2,1)S(1)}, u32[]{:S(2)}, u32[]{:S(2)}) collective-permute-start(bf16[528,128]{1,0:T(8,128)(2,1)S(1)} %get-tuple-element.84), channel_id=1, source_target_pairs={{0,16},{16,0},{32,48},{48,32},{64,80},{80,64},{96,112},{112,96},{1... | collective-permute-start | bytes 405512 | tf_op jit(solution)/shard_map/ppermute | solution.py:426
  113.8 0.3 requantize.6
  114.1 2.5 %collective-permute-start.15 = (bf16[528,128]{1,0:T(8,128)(2,1)S(1)}, bf16[528,128]{1,0:T(8,128)(2,1)S(1)}, u32[]{:S(2)}, u32[]{:S(2)}) collective-permute-start(bf16[528,128]{1,0:T(8,128)(2,1)S(1)} %get-tuple-element.83), channel_id=1, source_target_pairs={{0,16},{16,0},{32,48},{48,32},{64,80},{80,64},{96,112},{112,96},{1... | collective-permute-start | bytes 405512 | tf_op jit(solution)/shard_map/ppermute | solution.py:426
  117.2 3.0 %collective-permute-start.21 = (bf16[528,128]{1,0:T(8,128)(2,1)S(1)}, bf16[528,128]{1,0:T(8,128)(2,1)S(1)}, u32[]{:S(2)}, u32[]{:S(2)}) collective-permute-start(bf16[528,128]{1,0:T(8,128)(2,1)S(1)} %core_sum.4._), channel_id=1, source_target_pairs={{0,64},{16,80},{32,96},{48,112},{64,0},{80,16},{96,32},{112,48},{1... | collective-permute-start | bytes 405512 | tf_op jit(solution)/shard_map/ppermute | solution.py:430
  120.4 0.8 collective-permute-start.22
  121.4 0.8 collective-permute-start.20
  122.2 4.5 %collective-permute-done.22.c = bf16[528,128]{1,0:T(8,128)(2,1)S(1)} collective-permute-done((bf16[528,128]{1,0:T(8,128)(2,1)S(1)}, bf16[528,128]{1,0:T(8,128)(2,1)S(1)}, u32[]{:S(2)}, u32[]{:S(2)}) %collective-permute-start.22) | collective-permute-done | bytes 135200 | tf_op jit(solution)/shard_map/ppermute | solution.py:430
  126.7 0.5 adam_weight.1
  127.2 3.3 %collective-permute-start.25 = (bf16[64,1024]{1,0:T(8,128)(2,1)S(1)}, bf16[64,1024]{1,0:T(8,128)(2,1)S(1)}, u32[]{:S(2)}, u32[]{:S(2)}) collective-permute-start(bf16[64,1024]{1,0:T(8,128)(2,1)S(1)} %get-tuple-element.90._.refs_0_), channel_id=1, source_target_pairs={{0,96},{16,112},{32,0},{48,16},{64,32},{80,48},{96,64},{112,80},{1... | collective-permute-start | bytes 393224 | tf_op jit(solution)/shard_map/ppermute | solution.py:432
  130.5 0.4 collective-permute-start.24
  130.8 0.3 collective-permute-start.23
  131.2 1.7 %collective-permute-start.26 = (bf16[64,1024]{1,0:T(8,128)(2,1)S(1)}, bf16[64,1024]{1,0:T(8,128)(2,1)S(1)}, u32[]{:S(2)}, u32[]{:S(2)}) collective-permute-start(bf16[64,1024]{1,0:T(8,128)(2,1)S(1)} %get-tuple-element.90._.refs_0_), channel_id=1, source_target_pairs={{0,16},{16,0},{32,48},{48,32},{64,80},{80,64},{96,112},{112,96},{1... | collective-permute-start | bytes 393224 | tf_op jit(solution)/shard_map/ppermute | solution.py:434
  132.9 1.6 %collective-permute-done.25.refs_3_ = bf16[64,1024]{1,0:T(8,128)(2,1)S(1)} collective-permute-done((bf16[64,1024]{1,0:T(8,128)(2,1)S(1)}, bf16[64,1024]{1,0:T(8,128)(2,1)S(1)}, u32[]{:S(2)}, u32[]{:S(2)}) %collective-permute-start.25) | collective-permute-done | bytes 131104 | tf_op jit(solution)/shard_map/ppermute | solution.py:432
  134.4 2.6 %collective-permute-start.29 = (bf16[64,1024]{1,0:T(8,128)(2,1)S(1)}, bf16[64,1024]{1,0:T(8,128)(2,1)S(1)}, u32[]{:S(2)}, u32[]{:S(2)}) collective-permute-start(bf16[64,1024]{1,0:T(8,128)(2,1)S(1)} %collective-permute-done.25.refs_3_), channel_id=1, source_target_pairs={{0,16},{16,0},{32,48},{48,32},{64,80},{80,64},{96,112},{112,96},{1... | collective-permute-start | bytes 393224 | tf_op jit(solution)/shard_map/ppermute | solution.py:434
  137.0 2.1 %collective-permute-start.28 = (bf16[64,1024]{1,0:T(8,128)(2,1)S(1)}, bf16[64,1024]{1,0:T(8,128)(2,1)S(1)}, u32[]{:S(2)}, u32[]{:S(2)}) collective-permute-start(bf16[64,1024]{1,0:T(8,128)(2,1)S(1)} %collective-permute-done.24.refs_2_), channel_id=1, source_target_pairs={{0,16},{16,0},{32,48},{48,32},{64,80},{80,64},{96,112},{112,96},{1... | collective-permute-start | bytes 393224 | tf_op jit(solution)/shard_map/ppermute | solution.py:434
  139.2 1.0 collective-permute-done.23.refs_1_
  140.2 0.5 collective-permute-start.27
  140.7 1.0 adam.1
  141.7 1.1 gather_weights.1
  (33 shorter events, 2.0 us)
Async XLA Ops:
  5.0 48.2 %collective-permute-start.2 = (bf16[8256,128]{1,0:T(8,128)(2,1)S(1)}, bf16[8256,128]{1,0:T(8,128)(2,1)S(1)}, u32[]{:S(2)}, u32[]{:S(2)}) collective-permute-start(bf16[8256,128]{1,0:T(8,128)(2,1)S(1)} %get-tuple-element.51.refs_2_), channel_id=1, source_target_pairs={{0,4},{1,5},{2,6},{3,7},{4,0},{5,1},{6,2},{7,3},{8,12},{9,13},{10,... | collective-permute-start | bytes 6340616 | tf_op jit(solution)/shard_map/ppermute | solution.py:413
  10.6 47.8 %collective-permute-start.1 = (bf16[8256,128]{1,0:T(8,128)(2,1)S(1)}, bf16[8256,128]{1,0:T(8,128)(2,1)S(1)}, u32[]{:S(2)}, u32[]{:S(2)}) collective-permute-start(bf16[8256,128]{1,0:T(8,128)(2,1)S(1)} %get-tuple-element.54.refs_2_), channel_id=1, source_target_pairs={{0,12},{1,13},{2,14},{3,15},{4,8},{5,9},{6,10},{7,11},{8,4},{9,5},... | collective-permute-start | bytes 6340616 | tf_op jit(solution)/shard_map/ppermute | solution.py:413
  16.2 46.3 %collective-permute-start = (bf16[8256,128]{1,0:T(8,128)(2,1)S(1)}, bf16[8256,128]{1,0:T(8,128)(2,1)S(1)}, u32[]{:S(2)}, u32[]{:S(2)}) collective-permute-start(bf16[8256,128]{1,0:T(8,128)(2,1)S(1)} %get-tuple-element.56.refs_2_), channel_id=1, source_target_pairs={{0,1},{1,0},{2,3},{3,2},{4,5},{5,4},{6,7},{7,6},{8,9},{9,8},{10,11... | collective-permute-start | bytes 6340616 | tf_op jit(solution)/shard_map/ppermute | solution.py:413
  20.5 47.2 %collective-permute-start.6 = (bf16[8256,128]{1,0:T(8,128)(2,1)S(1)}, bf16[8256,128]{1,0:T(8,128)(2,1)S(1)}, u32[]{:S(2)}, u32[]{:S(2)}) collective-permute-start(bf16[8256,128]{1,0:T(8,128)(2,1)S(1)} %grad_send_1.1.refs_2_), channel_id=1, source_target_pairs={{0,3},{1,2},{2,1},{3,0},{4,7},{5,6},{6,5},{7,4},{8,11},{9,10},{10,... | collective-permute-start | bytes 6340616 | tf_op jit(solution)/shard_map/ppermute | solution.py:413
  54.9 26.3 %collective-permute-start.5 = (bf16[4128,128]{1,0:T(8,128)(2,1)S(1)}, bf16[4128,128]{1,0:T(8,128)(2,1)S(1)}, u32[]{:S(2)}, u32[]{:S(2)}) collective-permute-start(bf16[4128,128]{1,0:T(8,128)(2,1)S(1)} %get-tuple-element.57.refs_2_), channel_id=1, source_target_pairs={{0,12},{1,13},{2,14},{3,15},{4,8},{5,9},{6,10},{7,11},{8,4},{9,5},... | collective-permute-start | bytes 3170312 | tf_op jit(solution)/shard_map/ppermute | solution.py:421
  60.0 25.5 %collective-permute-start.4 = (bf16[4128,128]{1,0:T(8,128)(2,1)S(1)}, bf16[4128,128]{1,0:T(8,128)(2,1)S(1)}, u32[]{:S(2)}, u32[]{:S(2)}) collective-permute-start(bf16[4128,128]{1,0:T(8,128)(2,1)S(1)} %get-tuple-element.58.refs_2_), channel_id=1, source_target_pairs={{0,1},{1,0},{2,3},{3,2},{4,5},{5,4},{6,7},{7,6},{8,9},{9,8},{10,11... | collective-permute-start | bytes 3170312 | tf_op jit(solution)/shard_map/ppermute | solution.py:421
  64.2 25.8 %collective-permute-start.3 = (bf16[4128,128]{1,0:T(8,128)(2,1)S(1)}, bf16[4128,128]{1,0:T(8,128)(2,1)S(1)}, u32[]{:S(2)}, u32[]{:S(2)}) collective-permute-start(bf16[4128,128]{1,0:T(8,128)(2,1)S(1)} %get-tuple-element.60.refs_2_), channel_id=1, source_target_pairs={{0,3},{1,2},{2,1},{3,0},{4,7},{5,6},{6,5},{7,4},{8,11},{9,10},{10,... | collective-permute-start | bytes 3170312 | tf_op jit(solution)/shard_map/ppermute | solution.py:421
  69.4 22.5 %collective-permute-start.10 = (bf16[4128,128]{1,0:T(8,128)(2,1)S(1)}, bf16[4128,128]{1,0:T(8,128)(2,1)S(1)}, u32[]{:S(2)}, u32[]{:S(2)}) collective-permute-start(bf16[4128,128]{1,0:T(8,128)(2,1)S(1)} %get-tuple-element.63.refs_2_), channel_id=1, source_target_pairs={{0,4},{1,5},{2,6},{3,7},{4,0},{5,1},{6,2},{7,3},{8,12},{9,13},{10,... | collective-permute-start | bytes 3170312 | tf_op jit(solution)/shard_map/ppermute | solution.py:421
  82.2 14.6 %collective-permute-start.9 = (bf16[2064,128]{1,0:T(8,128)(2,1)S(1)}, bf16[2064,128]{1,0:T(8,128)(2,1)S(1)}, u32[]{:S(2)}, u32[]{:S(2)}) collective-permute-start(bf16[2064,128]{1,0:T(8,128)(2,1)S(1)} %get-tuple-element.64.refs_2_), channel_id=1, source_target_pairs={{0,1},{1,0},{2,3},{3,2},{4,5},{5,4},{6,7},{7,6},{8,9},{9,8},{10,11... | collective-permute-start | bytes 1585160 | tf_op jit(solution)/shard_map/ppermute | solution.py:421
  86.6 15.2 %collective-permute-start.8 = (bf16[2064,128]{1,0:T(8,128)(2,1)S(1)}, bf16[2064,128]{1,0:T(8,128)(2,1)S(1)}, u32[]{:S(2)}, u32[]{:S(2)}) collective-permute-start(bf16[2064,128]{1,0:T(8,128)(2,1)S(1)} %get-tuple-element.65.refs_2_), channel_id=1, source_target_pairs={{0,3},{1,2},{2,1},{3,0},{4,7},{5,6},{6,5},{7,4},{8,11},{9,10},{10,... | collective-permute-start | bytes 1585160 | tf_op jit(solution)/shard_map/ppermute | solution.py:421
  91.1 12.0 %collective-permute-start.7 = (bf16[2064,128]{1,0:T(8,128)(2,1)S(1)}, bf16[2064,128]{1,0:T(8,128)(2,1)S(1)}, u32[]{:S(2)}, u32[]{:S(2)}) collective-permute-start(bf16[2064,128]{1,0:T(8,128)(2,1)S(1)} %get-tuple-element.67.refs_2_), channel_id=1, source_target_pairs={{0,4},{1,5},{2,6},{3,7},{4,0},{5,1},{6,2},{7,3},{8,12},{9,13},{10,... | collective-permute-start | bytes 1585160 | tf_op jit(solution)/shard_map/ppermute | solution.py:421
  93.0 11.6 %collective-permute-start.14 = (bf16[2064,128]{1,0:T(8,128)(2,1)S(1)}, bf16[2064,128]{1,0:T(8,128)(2,1)S(1)}, u32[]{:S(2)}, u32[]{:S(2)}) collective-permute-start(bf16[2064,128]{1,0:T(8,128)(2,1)S(1)} %get-tuple-element.71.refs_2_), channel_id=1, source_target_pairs={{0,12},{1,13},{2,14},{3,15},{4,8},{5,9},{6,10},{7,11},{8,4},{9,5},... | collective-permute-start | bytes 1585160 | tf_op jit(solution)/shard_map/ppermute | solution.py:421
  97.4 10.2 %collective-permute-start.13 = (bf16[1040,128]{1,0:T(8,128)(2,1)S(1)}, bf16[1040,128]{1,0:T(8,128)(2,1)S(1)}, u32[]{:S(2)}, u32[]{:S(2)}) collective-permute-start(bf16[1040,128]{1,0:T(8,128)(2,1)S(1)} %get-tuple-element.72.refs_2_), channel_id=1, source_target_pairs={{0,3},{1,2},{2,1},{3,0},{4,7},{5,6},{6,5},{7,4},{8,11},{9,10},{10,... | collective-permute-start | bytes 798728 | tf_op jit(solution)/shard_map/ppermute | solution.py:421
  102.4 6.6 %collective-permute-start.12 = (bf16[1040,128]{1,0:T(8,128)(2,1)S(1)}, bf16[1040,128]{1,0:T(8,128)(2,1)S(1)}, u32[]{:S(2)}, u32[]{:S(2)}) collective-permute-start(bf16[1040,128]{1,0:T(8,128)(2,1)S(1)} %get-tuple-element.73.refs_2_), channel_id=1, source_target_pairs={{0,4},{1,5},{2,6},{3,7},{4,0},{5,1},{6,2},{7,3},{8,12},{9,13},{10,... | collective-permute-start | bytes 798728 | tf_op jit(solution)/shard_map/ppermute | solution.py:421
  103.7 10.0 %collective-permute-start.11 = (bf16[1040,128]{1,0:T(8,128)(2,1)S(1)}, bf16[1040,128]{1,0:T(8,128)(2,1)S(1)}, u32[]{:S(2)}, u32[]{:S(2)}) collective-permute-start(bf16[1040,128]{1,0:T(8,128)(2,1)S(1)} %get-tuple-element.75.refs_2_), channel_id=1, source_target_pairs={{0,12},{1,13},{2,14},{3,15},{4,8},{5,9},{6,10},{7,11},{8,4},{9,5},... | collective-permute-start | bytes 798728 | tf_op jit(solution)/shard_map/ppermute | solution.py:421
  105.1 11.5 %collective-permute-start.18 = (bf16[1040,128]{1,0:T(8,128)(2,1)S(1)}, bf16[1040,128]{1,0:T(8,128)(2,1)S(1)}, u32[]{:S(2)}, u32[]{:S(2)}) collective-permute-start(bf16[1040,128]{1,0:T(8,128)(2,1)S(1)} %get-tuple-element.79._), channel_id=1, source_target_pairs={{0,1},{1,0},{2,3},{3,2},{4,5},{5,4},{6,7},{7,6},{8,9},{9,8},{10,11... | collective-permute-start | bytes 798728 | tf_op jit(solution)/shard_map/ppermute | solution.py:421
  109.4 10.9 %collective-permute-start.16 = (bf16[528,128]{1,0:T(8,128)(2,1)S(1)}, bf16[528,128]{1,0:T(8,128)(2,1)S(1)}, u32[]{:S(2)}, u32[]{:S(2)}) collective-permute-start(bf16[528,128]{1,0:T(8,128)(2,1)S(1)} %get-tuple-element.84), channel_id=1, source_target_pairs={{0,16},{16,0},{32,48},{48,32},{64,80},{80,64},{96,112},{112,96},{1... | collective-permute-start | bytes 405512 | tf_op jit(solution)/shard_map/ppermute | solution.py:426
  113.6 3.4 %collective-permute-start.17 = (bf16[528,128]{1,0:T(8,128)(2,1)S(1)}, bf16[528,128]{1,0:T(8,128)(2,1)S(1)}, u32[]{:S(2)}, u32[]{:S(2)}) collective-permute-start(bf16[528,128]{1,0:T(8,128)(2,1)S(1)} %get-tuple-element.85), channel_id=1, source_target_pairs={{0,16},{16,0},{32,48},{48,32},{64,80},{80,64},{96,112},{112,96},{1... | collective-permute-start | bytes 405512 | tf_op jit(solution)/shard_map/ppermute | solution.py:426
  113.7 13.0 %copy-start = (f32[64,1024]{1,0:T(8,128)S(1)}, f32[64,1024]{1,0:T(8,128)}, u32[]{:S(2)}) copy-start(f32[64,1024]{1,0:T(8,128)} %master.3) | copy-start | bytes 786436
  113.7 13.0 %copy-start.1 = (f32[64,1024]{1,0:T(8,128)S(1)}, f32[64,1024]{1,0:T(8,128)}, u32[]{:S(2)}) copy-start(f32[64,1024]{1,0:T(8,128)} %moment.3) | copy-start | bytes 786436
  113.7 13.0 %copy-start.2 = (f32[64,1024]{1,0:T(8,128)S(1)}, f32[64,1024]{1,0:T(8,128)}, u32[]{:S(2)}) copy-start(f32[64,1024]{1,0:T(8,128)} %second.3) | copy-start | bytes 786436
  114.1 7.1 %collective-permute-start.15 = (bf16[528,128]{1,0:T(8,128)(2,1)S(1)}, bf16[528,128]{1,0:T(8,128)(2,1)S(1)}, u32[]{:S(2)}, u32[]{:S(2)}) collective-permute-start(bf16[528,128]{1,0:T(8,128)(2,1)S(1)} %get-tuple-element.83), channel_id=1, source_target_pairs={{0,16},{16,0},{32,48},{48,32},{64,80},{80,64},{96,112},{112,96},{1... | collective-permute-start | bytes 405512 | tf_op jit(solution)/shard_map/ppermute | solution.py:426
  116.9 4.3 %collective-permute-start.19 = (bf16[528,128]{1,0:T(8,128)(2,1)S(1)}, bf16[528,128]{1,0:T(8,128)(2,1)S(1)}, u32[]{:S(2)}, u32[]{:S(2)}) collective-permute-start(bf16[528,128]{1,0:T(8,128)(2,1)S(1)} %get-tuple-element.88), channel_id=1, source_target_pairs={{0,16},{16,0},{32,48},{48,32},{64,80},{80,64},{96,112},{112,96},{1... | collective-permute-start | bytes 405512 | tf_op jit(solution)/shard_map/ppermute | solution.py:426
  117.2 9.5 %collective-permute-start.21 = (bf16[528,128]{1,0:T(8,128)(2,1)S(1)}, bf16[528,128]{1,0:T(8,128)(2,1)S(1)}, u32[]{:S(2)}, u32[]{:S(2)}) collective-permute-start(bf16[528,128]{1,0:T(8,128)(2,1)S(1)} %core_sum.4._), channel_id=1, source_target_pairs={{0,64},{16,80},{32,96},{48,112},{64,0},{80,16},{96,32},{112,48},{1... | collective-permute-start | bytes 405512 | tf_op jit(solution)/shard_map/ppermute | solution.py:430
  120.4 6.3 %collective-permute-start.22 = (bf16[528,128]{1,0:T(8,128)(2,1)S(1)}, bf16[528,128]{1,0:T(8,128)(2,1)S(1)}, u32[]{:S(2)}, u32[]{:S(2)}) collective-permute-start(bf16[528,128]{1,0:T(8,128)(2,1)S(1)} %core_sum.5._), channel_id=1, source_target_pairs={{0,96},{16,112},{32,0},{48,16},{64,32},{80,48},{96,64},{112,80},{1... | collective-permute-start | bytes 405512 | tf_op jit(solution)/shard_map/ppermute | solution.py:430
  121.4 5.3 %collective-permute-start.20 = (bf16[528,128]{1,0:T(8,128)(2,1)S(1)}, bf16[528,128]{1,0:T(8,128)(2,1)S(1)}, u32[]{:S(2)}, u32[]{:S(2)}) collective-permute-start(bf16[528,128]{1,0:T(8,128)(2,1)S(1)} %core_sum.7), channel_id=1, source_target_pairs={{0,32},{16,48},{32,64},{48,80},{64,96},{80,112},{96,0},{112,16},{1... | collective-permute-start | bytes 405512 | tf_op jit(solution)/shard_map/ppermute | solution.py:430
  127.2 7.2 %collective-permute-start.25 = (bf16[64,1024]{1,0:T(8,128)(2,1)S(1)}, bf16[64,1024]{1,0:T(8,128)(2,1)S(1)}, u32[]{:S(2)}, u32[]{:S(2)}) collective-permute-start(bf16[64,1024]{1,0:T(8,128)(2,1)S(1)} %get-tuple-element.90._.refs_0_), channel_id=1, source_target_pairs={{0,96},{16,112},{32,0},{48,16},{64,32},{80,48},{96,64},{112,80},{1... | collective-permute-start | bytes 393224 | tf_op jit(solution)/shard_map/ppermute | solution.py:432
  130.5 6.6 %collective-permute-start.24 = (bf16[64,1024]{1,0:T(8,128)(2,1)S(1)}, bf16[64,1024]{1,0:T(8,128)(2,1)S(1)}, u32[]{:S(2)}, u32[]{:S(2)}) collective-permute-start(bf16[64,1024]{1,0:T(8,128)(2,1)S(1)} %get-tuple-element.90._.refs_0_), channel_id=1, source_target_pairs={{0,64},{16,80},{32,96},{48,112},{64,0},{80,16},{96,32},{112,48},{1... | collective-permute-start | bytes 393224 | tf_op jit(solution)/shard_map/ppermute | solution.py:432
  130.8 9.4 %collective-permute-start.23 = (bf16[64,1024]{1,0:T(8,128)(2,1)S(1)}, bf16[64,1024]{1,0:T(8,128)(2,1)S(1)}, u32[]{:S(2)}, u32[]{:S(2)}) collective-permute-start(bf16[64,1024]{1,0:T(8,128)(2,1)S(1)} %get-tuple-element.90._.refs_0_), channel_id=1, source_target_pairs={{0,32},{16,48},{32,64},{48,80},{64,96},{80,112},{96,0},{112,16},{1... | collective-permute-start | bytes 393224 | tf_op jit(solution)/shard_map/ppermute | solution.py:432
  131.2 10.5 %collective-permute-start.26 = (bf16[64,1024]{1,0:T(8,128)(2,1)S(1)}, bf16[64,1024]{1,0:T(8,128)(2,1)S(1)}, u32[]{:S(2)}, u32[]{:S(2)}) collective-permute-start(bf16[64,1024]{1,0:T(8,128)(2,1)S(1)} %get-tuple-element.90._.refs_0_), channel_id=1, source_target_pairs={{0,16},{16,0},{32,48},{48,32},{64,80},{80,64},{96,112},{112,96},{1... | collective-permute-start | bytes 393224 | tf_op jit(solution)/shard_map/ppermute | solution.py:434
  134.4 7.3 %collective-permute-start.29 = (bf16[64,1024]{1,0:T(8,128)(2,1)S(1)}, bf16[64,1024]{1,0:T(8,128)(2,1)S(1)}, u32[]{:S(2)}, u32[]{:S(2)}) collective-permute-start(bf16[64,1024]{1,0:T(8,128)(2,1)S(1)} %collective-permute-done.25.refs_3_), channel_id=1, source_target_pairs={{0,16},{16,0},{32,48},{48,32},{64,80},{80,64},{96,112},{112,96},{1... | collective-permute-start | bytes 393224 | tf_op jit(solution)/shard_map/ppermute | solution.py:434
  137.0 4.7 %collective-permute-start.28 = (bf16[64,1024]{1,0:T(8,128)(2,1)S(1)}, bf16[64,1024]{1,0:T(8,128)(2,1)S(1)}, u32[]{:S(2)}, u32[]{:S(2)}) collective-permute-start(bf16[64,1024]{1,0:T(8,128)(2,1)S(1)} %collective-permute-done.24.refs_2_), channel_id=1, source_target_pairs={{0,16},{16,0},{32,48},{48,32},{64,80},{80,64},{96,112},{112,96},{1... | collective-permute-start | bytes 393224 | tf_op jit(solution)/shard_map/ppermute | solution.py:434
  140.2 1.5 %collective-permute-start.27 = (bf16[64,1024]{1,0:T(8,128)(2,1)S(1)}, bf16[64,1024]{1,0:T(8,128)(2,1)S(1)}, u32[]{:S(2)}, u32[]{:S(2)}) collective-permute-start(bf16[64,1024]{1,0:T(8,128)(2,1)S(1)} %collective-permute-done.23.refs_1_), channel_id=1, source_target_pairs={{0,16},{16,0},{32,48},{48,32},{64,80},{80,64},{96,112},{112,96},{1... | collective-permute-start | bytes 393224 | tf_op jit(solution)/shard_map/ppermute | solution.py:434

commit v3 on v2

v3 whole, which is shorter than its diff:
```python
import functools

import jax
import jax.numpy as jnp
from jax import lax
from jax.experimental import pallas as pl
from jax.experimental.pallas import tpu as pltpu
from jax.sharding import PartitionSpec as P

D = 8192
KV = 1024
TOK = 768
RUNS = KV // 128
HALF = KV // 2
PARTS = (1, 2, 3, 0)
EARLY = 2
SENT_AT = {1: 0, 2: 1024, 3: 2048, 0: 3072}
KEPT_AT = {1: 0, 2: 1024, 3: 2048}
HELD = (3072, 5120)
F32 = jnp.float32
BF16 = jnp.bfloat16
MIB = 1 << 20
SMALL = pl.CostEstimate(flops=1, bytes_accessed=1, transcendentals=0)

MATCH = ((1, 0, 3, 2), (3, 2, 1, 0))


def bits(v):
    b = lax.shift_right_logical(v, 1)
    return (v ^ b) & 1, b


def local_perm(dim):
    m = MATCH[dim % 2]
    if dim < 2:
        return [(z * 4 + x, z * 4 + m[x]) for z in range(4) for x in range(4)]
    return [(z * 4 + x, m[z] * 4 + x) for z in range(4) for x in range(4)]


def y_perm(k):
    return [(n, ((n // 2 + k) % 4) * 2 + n % 2) for n in range(8)]


CORE_PERM = [(n, n ^ 1) for n in range(8)]


def pad16(n):
    return -(-n // 16) * 16


def msg_rows(blocks):
    return blocks * 128 + pad16(blocks)


def params(mib):
    return pltpu.CompilerParams(vmem_limit_bytes=mib * MIB)


def vmem():
    return pl.BlockSpec(memory_space=pltpu.VMEM)


def quantize(m):
    top = jnp.max(jnp.abs(m), axis=0, keepdims=True) + 1e-06
    scale = top.astype(BF16).astype(F32)
    return (m * (1.0 / scale)).astype(BF16), scale


def encode(m):
    top = jnp.max(jnp.abs(m), axis=0, keepdims=True) + 1e-30
    scale = top.astype(BF16).astype(F32)
    e = jnp.exp2(jnp.abs(m) * (250.0 / scale) - 125.0)
    return jnp.where(m < 0, -e, e).astype(BF16), scale


def decode(code, scale):
    y = code.astype(F32)
    m = (jnp.log2(jnp.abs(y)) + 125.0) * (scale * (1.0 / 250.0))
    return jnp.where(y < 0, -m, m)


GROUPS = {"early": (0, EARLY), "late": (EARLY, RUNS)}


def aligned(v):
    return v if isinstance(v, int) else pl.multiple_of(v, 128)


def first_kernel(part, sent, group, fetch, *refs):
    order = [(part + s) % 4 for s in range(4)]
    if fetch and sent:
        tok, og, _, out, held, ogt, sc, sem, ogv = refs
    elif fetch:
        tok, ogt, _, out, held, sc, sem = refs
    else:
        held, ogt, _, out, sc = refs
    k0, k1 = GROUPS.get(group, (0, RUNS))
    me_l = lax.axis_index("local")
    ax, bx = bits(me_l & 3)
    az, bz = bits(lax.shift_right_logical(me_l, 2))

    def place_z(a, b):
        zb = b ^ bz
        return 2 * zb + (a ^ az ^ zb)

    if fetch:
        y = lax.shift_right_logical(lax.axis_index("node"), 1)
        copies = []
        if sent:
            copies.append(pltpu.make_async_copy(og, ogv, sem.at[0]))
        for p, at in (SENT_AT if sent else KEPT_AT).items():
            base = ((y + p) & 3) * 2048
            if p == 0:
                for i in range(4):
                    rows = pl.ds(i * TOK // 4, TOK // 4)
                    copies.append(pltpu.make_async_copy(
                        tok.at[rows, pl.ds(pl.multiple_of(base, 2048), 2048)],
                        held.at[rows, at:at + 2048],
                        sem.at[len(copies)],
                    ))
                continue
            for u in range(4 if p == 1 else 2):
                width = 128 if p == 1 else 256
                a, b = {1: (u & 1, u >> 1), 2: (sent, u), 3: (u, sent)}[p]
                lane = place_z(a, b) * 256 + ((sent ^ bx) * 128 if p == 1 else 0)
                for c in range(2):
                    to = at + c * 512 + u * width
                    copies.append(pltpu.make_async_copy(
                        tok.at[:, pl.ds(aligned(base + c * 1024 + lane), width)],
                        held.at[:, to:to + width],
                        sem.at[len(copies)],
                    ))
        for cp in copies:
            cp.start()
        if sent:
            copies.pop(0).wait()
            ogt[...] = ogv[...].T
        for cp in copies[:8]:
            cp.wait()

    for t in range(4):
        columns, places = [], []
        lo, hi = t & 1, t >> 1
        for x, a, b in {
            0: [(0, lo, hi), (1, lo, hi)], 1: [(sent, lo, hi)], 2: [(lo, sent, hi)], 3: [(lo, hi, sent)]
        }[part]:
            half = 512 if part else 1024
            lane = (SENT_AT if sent or not part else KEPT_AT)[part] + {
                0: place_z(a, b) * 256 + (x ^ bx) * 128,
                1: (a + 2 * b) * 128,
                2: b * 256 + (x ^ bx) * 128,
                3: a * 256 + (x ^ bx) * 128,
            }[part]
            t0 = held[:, pl.ds(aligned(lane), 128)]
            t1 = held[:, pl.ds(aligned(lane + half), 128)]
            swap = (x ^ bx ^ ax) == 1
            even = jnp.concatenate([t0[:, :64], t1[:, :64]], axis=1)
            odd = jnp.concatenate([t0[:, 64:], t1[:, 64:]], axis=1)
            for d in (sent,) if part == 0 else (0, 1):
                columns.append(jnp.where(swap, even, odd) if d else jnp.where(swap, odd, even))
                bit = (d, x, a, b)
                places.append(bit[order[1]] * 4 + bit[order[2]] * 2 + bit[order[3]])
        grad = jnp.dot(ogt[k0 * 128:k1 * 128, :], jnp.concatenate(columns, axis=1), preferred_element_type=F32)
        for k in range(k1 - k0):
            code, scale = quantize(grad[k * 128:(k + 1) * 128])
            for i, place in enumerate(places):
                block = place * (k1 - k0) + k
                out[block * 128:(block + 1) * 128, :] = code[:, i * 128:(i + 1) * 128]
                sc[block:block + 1, :] = scale[:, i * 128:(i + 1) * 128]
    out[8 * (k1 - k0) * 128:, :] = sc[...].astype(BF16)
    if fetch:
        for cp in copies[8:]:
            cp.wait()


def first_stage(part, sent, group, args, after, fetch=False):
    k0, k1 = GROUPS.get(group, (0, RUNS))
    blocks = 8 * (k1 - k0)
    out = [jax.ShapeDtypeStruct((msg_rows(blocks), 128), BF16)]
    scratch = [pltpu.VMEM((blocks, 128), F32)]
    anywhere = pl.BlockSpec(memory_space=pl.ANY)
    specs = [vmem()] * 2
    if fetch:
        out.append(jax.ShapeDtypeStruct((TOK, HELD[sent]), BF16))
        scratch.append(pltpu.SemaphoreType.DMA((21,)))
        specs = [anywhere] * 2 if sent else [anywhere, vmem()]
        if sent:
            out.append(jax.ShapeDtypeStruct((KV, TOK), BF16))
            scratch.append(pltpu.VMEM((TOK, KV), BF16))
    return pl.pallas_call(
        functools.partial(first_kernel, part, sent, group, fetch),
        out_shape=tuple(out),
        in_specs=specs + [anywhere],
        out_specs=tuple(vmem() for _ in out),
        scratch_shapes=scratch,
        compiler_params=params(20),
        cost_estimate=SMALL,
        name=f"grad_{'send' if sent else 'keep'}_{part}",
    )(*args, after)


def hold(message, after):
    anywhere = pl.BlockSpec(memory_space=pl.ANY)
    return pl.pallas_call(
        lambda message, _, out: None,
        out_shape=jax.ShapeDtypeStruct(message.shape, message.dtype),
        in_specs=[anywhere, anywhere],
        out_specs=anywhere,
        input_output_aliases={0: 0},
        compiler_params=params(1),
        cost_estimate=SMALL,
        name="hold",
    )(message, after)


def sum_kernel(tiles, send, n, *refs):
    half = tiles // 2
    keep, recvs = refs[0], refs[1:1 + n]
    out, sc_keep, sc_recv, sc_out = refs[2 + n:]
    coded = tiles < 8
    counts = [EARLY, RUNS - EARLY] if n == 2 else [RUNS]
    for j, r in enumerate(recvs):
        rows = pad16(tiles * counts[j])
        sc_recv[j, :rows, :] = r[tiles * counts[j] * 128:, :].astype(F32)
    if not coded:
        sc_keep[...] = keep[tiles * RUNS * 128:, :].astype(F32)

    def body(t, _):
        source = t + half if send else t
        k = 0
        for j, r in enumerate(recvs):
            for i in range(counts[j]):
                block = source * RUNS + k
                kept = keep[pl.ds(aligned(block * 128), 128), :]
                there = source * counts[j] + i
                came = r[pl.ds(aligned(there * 128), 128), :]
                scale = sc_recv[j, pl.ds(there, 1), :]
                if coded:
                    m = kept + decode(came, scale)
                else:
                    m = kept.astype(F32) * sc_keep[pl.ds(block, 1), :] + came.astype(F32) * scale
                to = t * RUNS + k
                if send:
                    m, scale = encode(m)
                    sc_out[pl.ds(to, 1), :] = scale
                out[pl.ds(aligned(to * 128), 128), :] = m
                k += 1
        return 0

    if half == 1:
        body(0, 0)
    else:
        lax.fori_loop(0, half, body, 0)
    if send:
        out[half * RUNS * 128:, :] = sc_out[...].astype(BF16)


def sum_stage(keep, recvs, tiles, send, after):
    n = len(recvs)
    half = tiles // 2 * RUNS
    return pl.pallas_call(
        functools.partial(sum_kernel, tiles, send, n),
        out_shape=jax.ShapeDtypeStruct((msg_rows(half), 128), BF16) if send else jax.ShapeDtypeStruct((half * 128, 128), F32),
        in_specs=[vmem()] * (1 + n) + [pl.BlockSpec(memory_space=pl.ANY)],
        out_specs=vmem(),
        scratch_shapes=[
            pltpu.VMEM((pad16(tiles * RUNS), 128), F32),
            pltpu.VMEM((n, pad16(tiles * RUNS), 128), F32),
            pltpu.VMEM((pad16(half), 128), F32),
        ],
        compiler_params=params(16),
        cost_estimate=SMALL,
        name=f"sum_{'send' if send else 'keep'}_{tiles}",
    )(keep, *recvs, after)


def pack(lo, hi, core):
    first = jnp.concatenate([lo[:, :64], hi[:, :64]], axis=1)
    second = jnp.concatenate([lo[:, 64:], hi[:, 64:]], axis=1)
    return jnp.where(core == 0, first, second), jnp.where(core == 0, second, first)


def requantize_kernel(keep, recv, _, mine, other, sc):
    core = lax.axis_index("node") & 1
    sc[0] = recv[KV:KV + 16, :].astype(F32)
    for k in range(RUNS // 2):
        made = []
        for j in (k, k + RUNS // 2):
            rows = slice(j * 128, (j + 1) * 128)
            made.append(quantize(keep[rows, :] + decode(recv[rows, :], sc[0, j:j + 1, :])))
        codes = pack(made[0][0], made[1][0], core)
        scales = pack(made[0][1], made[1][1], core)
        for i, out in enumerate((mine, other)):
            out[k * 128:(k + 1) * 128, :] = codes[i]
            sc[1 + i, k:k + 1, :] = scales[i]
    mine[HALF:, :] = sc[1].astype(BF16)
    other[HALF:, :] = sc[2].astype(BF16)


def requantize_stage(keep, recv, after):
    out = jax.ShapeDtypeStruct((HALF + 16, 128), BF16)
    return pl.pallas_call(
        requantize_kernel,
        out_shape=(out, out),
        in_specs=[vmem(), vmem(), pl.BlockSpec(memory_space=pl.ANY)],
        out_specs=(vmem(), vmem()),
        scratch_shapes=[pltpu.VMEM((3, 16, 128), F32)],
        compiler_params=params(8),
        cost_estimate=SMALL,
        name="requantize",
    )(keep, recv, after)


def core_sum_kernel(coded, mine, recv, _, out, sc):
    sc[0] = mine[HALF:, :].astype(F32)
    sc[1] = recv[HALF:, :].astype(F32)
    for k in range(RUNS // 2):
        rows = slice(k * 128, (k + 1) * 128)
        m = mine[rows, :].astype(F32) * sc[0, k:k + 1, :] + recv[rows, :].astype(F32) * sc[1, k:k + 1, :]
        if coded:
            m, sc[2, k:k + 1, :] = encode(m)
        out[rows, :] = m
    if coded:
        out[HALF:, :] = sc[2].astype(BF16)


def core_sum_stage(mine, recv, coded, after):
    out = jax.ShapeDtypeStruct((HALF + 16, 128), BF16) if coded else jax.ShapeDtypeStruct((HALF, 128), F32)
    return pl.pallas_call(
        functools.partial(core_sum_kernel, coded),
        out_shape=out,
        in_specs=[vmem(), vmem(), pl.BlockSpec(memory_space=pl.ANY)],
        out_specs=vmem(),
        scratch_shapes=[pltpu.VMEM((3, 16, 128), F32)],
        compiler_params=params(8),
        cost_estimate=SMALL,
        name="core_sum",
    )(mine, recv, after)


def adam_rule(grad, master, moment, second):
    m = 0.9 * moment + 0.1 * grad
    s = 0.95 * second + 0.05 * grad * grad
    update = m / (1.0 - 0.9**10) / (jnp.sqrt(s / (1.0 - 0.95**10)) + 1e-08) + 0.1 * master
    return master - 0.05 * update, m, s


def weight_kernel(own, a, b, c, master, moment, second, weight, grad, sc, g):
    for i, r in enumerate((a, b, c)):
        sc[i] = r[HALF:, :].astype(F32)
    for k in range(RUNS // 2):
        rows = slice(k * 128, (k + 1) * 128)
        m = own[rows, :]
        for i, r in enumerate((a, b, c)):
            m = m + decode(r[rows, :], sc[i, k:k + 1, :])
        g[rows, :] = m
    t = g[...].T
    whole = jnp.concatenate([t[:64], t[64:]], axis=1)
    grad[...] = whole
    weight[...] = adam_rule(whole, master[...], moment[...], second[...])[0].astype(BF16)


def weight_stage(own, others, master, moment, second):
    return pl.pallas_call(
        weight_kernel,
        out_shape=(jax.ShapeDtypeStruct((64, KV), BF16), jax.ShapeDtypeStruct((64, KV), F32)),
        in_specs=[vmem()] * 7,
        out_specs=(vmem(),) * 2,
        scratch_shapes=[pltpu.VMEM((3, 16, 128), F32), pltpu.VMEM((HALF, 128), F32)],
        compiler_params=params(8),
        cost_estimate=SMALL,
        name="adam_weight",
    )(own, *others, master, moment, second)


def adam_kernel(grad, master, moment, second, new_master, new_moment, new_second, mark):
    mark[...] = jnp.zeros_like(mark)
    new_master[...], new_moment[...], new_second[...] = adam_rule(grad[...], master[...], moment[...], second[...])


def adam_stage(*arrays):
    f = jax.ShapeDtypeStruct((64, KV), F32)
    return pl.pallas_call(
        adam_kernel,
        out_shape=(f, f, f, jax.ShapeDtypeStruct((8, 128), F32)),
        in_specs=[vmem()] * 4,
        out_specs=(vmem(),) * 4,
        compiler_params=params(8),
        cost_estimate=SMALL,
        name="adam",
    )(*arrays)


def gather_kernel(*refs):
    me_n = lax.axis_index("node")
    y = lax.shift_right_logical(me_n, 1)
    core = me_n & 1
    weight = refs[8]
    for k in range(4):
        src = ((y - k) & 3) * 2
        weight[src + core] = refs[k][...]
        weight[src + 1 - core] = refs[4 + k][...]


def gather_stage(weights):
    return pl.pallas_call(
        gather_kernel,
        out_shape=jax.ShapeDtypeStruct((8, 64, KV), BF16),
        in_specs=[vmem()] * 8,
        out_specs=vmem(),
        compiler_params=params(8),
        cost_estimate=SMALL,
        name="gather",
    )(*weights)


def local(tokens, out_grads, master, moment, second):
    tokens = pltpu.with_memory_space_constraint(tokens, pltpu.HBM)
    out_grads = pltpu.with_memory_space_constraint(out_grads, pltpu.HBM)
    keep, recv, early, late = {}, {}, {}, {}
    after, args = out_grads, (tokens, out_grads)
    for i, p in enumerate(PARTS):
        after, *more = first_stage(p, 1, "early", args, after, i == 0)
        args = tuple(more) or args
        early[p] = lax.ppermute(after, "local", local_perm(p))
    for p in PARTS:
        after, = first_stage(p, 1, "late", args, after)
        late[p] = after
    for p in PARTS:
        after = hold(late[p], early[p])
        recv[p] = [early[p], lax.ppermute(after, "local", local_perm(p))]
    held, ogt = args
    for i, p in enumerate(PARTS):
        after, *more = first_stage(p, 0, None, (tokens if i == 0 else args[0] if p == 0 else held, ogt), after, i == 0)
        held, = more or [held]
        keep[p] = after
    for step, tiles in ((1, 8), (2, 4), (3, 2)):
        arrived = dict(recv)
        for p in PARTS:
            after = sum_stage(keep[p], arrived[p], tiles, True, after)
            recv[p] = [lax.ppermute(after, "local", local_perm((p + step) % 4))]
        for p in PARTS:
            after = keep[p] = sum_stage(keep[p], arrived[p], tiles, False, after)
    mine, other, parts = {}, {}, {}
    one, two, three, own = PARTS
    for p, summed in ((one, None), (two, one), (three, two), (own, three), (None, own)):
        if p is not None:
            mine[p], other[p] = requantize_stage(keep[p], recv[p][0], after)
            after = mine[p]
            other[p] = lax.ppermute(other[p], "node", CORE_PERM)
        if summed is not None:
            after = core_sum_stage(mine[summed], other[summed], summed > 0, after)
            parts[summed] = lax.ppermute(after, "node", y_perm(summed)) if summed else after
    w, grad = weight_stage(parts[0], [parts[p] for p in (1, 2, 3)], master, moment, second)
    own = [w] + [lax.ppermute(w, "node", y_perm(k)) for k in (1, 2, 3)]
    *new, mark = adam_stage(grad, master, moment, second)
    own[3] = hold(own[3], mark)
    own += [lax.ppermute(v, "node", CORE_PERM) for v in own]
    return (*new, gather_stage(own))


def solution(mesh):
    rows = P(("node", "local"), None)
    return jax.shard_map(
        local,
        mesh=mesh,
        in_specs=(rows,) * 5,
        out_specs=(rows, rows, rows, P(None, "local", None)),
        check_vma=False,
    )
```

time: 143 us -> 138 us (0.965)
  waiting for transfers between devices: 49.4 us -> 45 us
  Pallas kernels: 43.4 us -> 40.3 us
  starting transfers between devices: 49.1 us -> 51.7 us
    pallas_call x21 -> x42, Pallas kernels: 40 us -> 36.9 us  [the longest x12 23.3 us: first_stage(): pl.pallas_call(functools.partial(first_kernel, part, sent, group, fetch),...]
    ppermute x23 -> x27, waiting for transfers between devices: 46.7 us -> 44.3 us  [the longest x12 23.4 us: local(): recv[p] = [lax.ppermute(after, 'local', local_perm((p + step) % 4))]]
    ppermute x23 -> x27, starting transfers between devices: 38.2 us -> 40.4 us  [the longest x12 14.8 us: local(): recv[p] = [lax.ppermute(after, 'local', local_perm((p + step) % 4))]]
    ppermute x3, waiting for transfers between devices: 2.61 us -> 0.67 us  [local(): own = [w] + [lax.ppermute(w, 'node', y_perm(k)) for k in (1, 2, 3)]]
  transfers between devices with their start and end apart: 30 -> 34, of which waited for: 14 -> 13; matrix products, arithmetic and copies ran while one was open for 0% -> 0% of each run, Pallas kernels for 26% -> 25%
where the time goes in v3:
time: 138 us
  starting transfers between devices  51.7 us (37%)
  waiting for transfers between devices  45 us (33%)
  Pallas kernels  40.3 us (29%)
    ppermute x12, waiting for transfers between devices, local(): recv[p] = [lax.ppermute(after, 'local', local_perm((p + step) % 4))]  23.4 us
    pallas_call x12, Pallas kernels, first_stage(): pl.pallas_call(functools.partial(first_kernel, part, sent, group, fetch),...  23.3 us
    ppermute x4, waiting for transfers between devices, local(): recv[p] = [early[p], lax.ppermute(after, 'local', local_perm(p))]  15.9 us
    ppermute x12, starting transfers between devices, local(): recv[p] = [lax.ppermute(after, 'local', local_perm((p + step) % 4))]  14.8 us
    pallas_call x24, Pallas kernels, sum_stage(): pl.pallas_call(functools.partial(sum_kernel, tiles, send, n), out_shape=j...  12.6 us
    ppermute x4, starting transfers between devices, local(): early[p] = lax.ppermute(after, 'local', local_perm(p))  7.51 us
    ppermute x4, starting transfers between devices, local(): recv[p] = [early[p], lax.ppermute(after, 'local', local_perm(p))]  6.83 us
    ppermute x3, starting transfers between devices, local(): lax.ppermute(after, 'node', y_perm(summed))  6.81 us
  transfers between devices with their start and end apart: 34, of which 13 were waited for; matrix products, arithmetic and copies ran while one was open for 0% of the time, Pallas kernels for 25%

profile of v3, /device:TPU:1, one launch (start us, length us, event | category | flops | bytes accessed | tf_op | source)
XLA Modules:
  0.0 138.0 jit_solution(12331038532153828051)
XLA Ops:
  0.6 4.0 %grad_send_1.2 = (bf16[2064,128]{1,0:T(8,128)(2,1)S(1)}, bf16[768,5120]{1,0:T(8,128)(2,1)S(1)}, bf16[1024,768]{1,0:T(8,128)(2,1)S(1)}) custom-call(bf16[768,8192]{1,0:T(8,128)(2,1)} %refs_0_.3, bf16[768,1024]{1,0:T(8,128)(2,1)} %refs_2_.1, bf16[768,1024]{1,0:T(8,128)(2,1)} %refs_2_.1), custom_call_target="tpu_custom_call" | custom-call | flops 1 | bytes 1 | tf_op jit(solution)/shard_map/grad_send_1/pallas_call | solution.py:190
  4.6 3.4 %collective-permute-start.6 = (bf16[2064,128]{1,0:T(8,128)(2,1)S(1)}, bf16[2064,128]{1,0:T(8,128)(2,1)S(1)}, u32[]{:S(2)}, u32[]{:S(2)}) collective-permute-start(bf16[2064,128]{1,0:T(8,128)(2,1)S(1)} %get-tuple-element.25.refs_2_), channel_id=1, source_target_pairs={{0,3},{1,2},{2,1},{3,0},{4,7},{5,6},{6,5},{7,4},{8,11},{9,10},{10,... | collective-permute-start | bytes 1585160 | tf_op jit(solution)/shard_map/ppermute | solution.py:425
  8.0 0.8 grad_send_2.2.refs_2_
  8.8 1.7 %collective-permute-start.4 = (bf16[2064,128]{1,0:T(8,128)(2,1)S(1)}, bf16[2064,128]{1,0:T(8,128)(2,1)S(1)}, u32[]{:S(2)}, u32[]{:S(2)}) collective-permute-start(bf16[2064,128]{1,0:T(8,128)(2,1)S(1)} %grad_send_2.2.refs_2_), channel_id=1, source_target_pairs={{0,4},{1,5},{2,6},{3,7},{4,0},{5,1},{6,2},{7,3},{8,12},{9,13},{10,... | collective-permute-start | bytes 1585160 | tf_op jit(solution)/shard_map/ppermute | solution.py:425
  10.5 0.8 grad_send_3.2.refs_2_
  11.3 2.3 %collective-permute-start.2 = (bf16[2064,128]{1,0:T(8,128)(2,1)S(1)}, bf16[2064,128]{1,0:T(8,128)(2,1)S(1)}, u32[]{:S(2)}, u32[]{:S(2)}) collective-permute-start(bf16[2064,128]{1,0:T(8,128)(2,1)S(1)} %grad_send_3.2.refs_2_), channel_id=1, source_target_pairs={{0,12},{1,13},{2,14},{3,15},{4,8},{5,9},{6,10},{7,11},{8,4},{9,5},... | collective-permute-start | bytes 1585160 | tf_op jit(solution)/shard_map/ppermute | solution.py:425
  13.6 1.3 grad_send_0.2.refs_2_
  15.0 1.6 %grad_send_1.3.refs_2_.message = bf16[6192,128]{1,0:T(8,128)(2,1)S(1)} custom-call(bf16[768,5120]{1,0:T(8,128)(2,1)S(1)} %get-tuple-element.23.refs_0_, bf16[1024,768]{1,0:T(8,128)(2,1)S(1)} %get-tuple-element.24.refs_1_, bf16[2064,128]{1,0:T(8,128)(2,1)S(1)} %grad_send_0.2.refs_2_), custom_call_target="tpu_custom_call" | custom-call | flops 1 | bytes 1 | tf_op jit(solution)/shard_map/grad_send_1/pallas_call | solution.py:190
  16.6 1.6 %grad_send_2.3.refs_2_.message = bf16[6192,128]{1,0:T(8,128)(2,1)S(1)} custom-call(bf16[768,5120]{1,0:T(8,128)(2,1)S(1)} %get-tuple-element.23.refs_0_, bf16[1024,768]{1,0:T(8,128)(2,1)S(1)} %get-tuple-element.24.refs_1_, bf16[6192,128]{1,0:T(8,128)(2,1)S(1)} %grad_send_1.3.refs_2_.message), custom_call_target="tpu_custom_call" | custom-call | flops 1 | bytes 1 | tf_op jit(solution)/shard_map/grad_send_2/pallas_call | solution.py:190
  18.2 1.1 collective-permute-done.6._.refs_1_
  19.3 2.8 %collective-permute-start.7 = (bf16[6192,128]{1,0:T(8,128)(2,1)S(1)}, bf16[6192,128]{1,0:T(8,128)(2,1)S(1)}, u32[]{:S(2)}, u32[]{:S(2)}) collective-permute-start(bf16[6192,128]{1,0:T(8,128)(2,1)S(1)} %hold.8), channel_id=1, source_target_pairs={{0,3},{1,2},{2,1},{3,0},{4,7},{5,6},{6,5},{7,4},{8,11},{9,10},{10,... | collective-permute-start | bytes 4755464 | tf_op jit(solution)/shard_map/ppermute | solution.py:431
  22.1 1.6 %grad_send_3.3.refs_2_.message = bf16[6192,128]{1,0:T(8,128)(2,1)S(1)} custom-call(bf16[768,5120]{1,0:T(8,128)(2,1)S(1)} %get-tuple-element.23.refs_0_, bf16[1024,768]{1,0:T(8,128)(2,1)S(1)} %get-tuple-element.24.refs_1_, bf16[6192,128]{1,0:T(8,128)(2,1)S(1)} %grad_send_2.3.refs_2_.message), custom_call_target="tpu_custom_call" | custom-call | flops 1 | bytes 1 | tf_op jit(solution)/shard_map/grad_send_3/pallas_call | solution.py:190
  23.7 1.7 %collective-permute-start.5 = (bf16[6192,128]{1,0:T(8,128)(2,1)S(1)}, bf16[6192,128]{1,0:T(8,128)(2,1)S(1)}, u32[]{:S(2)}, u32[]{:S(2)}) collective-permute-start(bf16[6192,128]{1,0:T(8,128)(2,1)S(1)} %hold.7), channel_id=1, source_target_pairs={{0,4},{1,5},{2,6},{3,7},{4,0},{5,1},{6,2},{7,3},{8,12},{9,13},{10,... | collective-permute-start | bytes 4755464 | tf_op jit(solution)/shard_map/ppermute | solution.py:431
  25.4 1.7 %grad_send_0.3.message = bf16[6192,128]{1,0:T(8,128)(2,1)S(1)} custom-call(bf16[768,5120]{1,0:T(8,128)(2,1)S(1)} %get-tuple-element.23.refs_0_, bf16[1024,768]{1,0:T(8,128)(2,1)S(1)} %get-tuple-element.24.refs_1_, bf16[6192,128]{1,0:T(8,128)(2,1)S(1)} %grad_send_3.3.refs_2_.message), custom_call_target="tpu_custom_call" | custom-call | flops 1 | bytes 1 | tf_op jit(solution)/shard_map/grad_send_0/pallas_call | solution.py:190
  27.2 2.3 %collective-permute-start.3 = (bf16[6192,128]{1,0:T(8,128)(2,1)S(1)}, bf16[6192,128]{1,0:T(8,128)(2,1)S(1)}, u32[]{:S(2)}, u32[]{:S(2)}) collective-permute-start(bf16[6192,128]{1,0:T(8,128)(2,1)S(1)} %hold.6), channel_id=1, source_target_pairs={{0,12},{1,13},{2,14},{3,15},{4,8},{5,9},{6,10},{7,11},{8,4},{9,5},... | collective-permute-start | bytes 4755464 | tf_op jit(solution)/shard_map/ppermute | solution.py:431
  29.5 3.7 %grad_keep_1.1 = (bf16[8256,128]{1,0:T(8,128)(2,1)S(1)}, bf16[768,3072]{1,0:T(8,128)(2,1)S(1)}) custom-call(bf16[768,8192]{1,0:T(8,128)(2,1)} %refs_0_.3, bf16[1024,768]{1,0:T(8,128)(2,1)S(1)} %get-tuple-element.24.refs_1_, bf16[6192,128]{1,0:T(8,128)(2,1)S(1)} %hold.5.refs_2_), custom_call_target="tpu_custom_call" | custom-call | flops 1 | bytes 1 | tf_op jit(solution)/shard_map/grad_keep_1/pallas_call | solution.py:190
  33.3 2.0 %grad_keep_2.1.refs_2_.refs_0_ = bf16[8256,128]{1,0:T(8,128)(2,1)S(1)} custom-call(bf16[768,3072]{1,0:T(8,128)(2,1)S(1)} %get-tuple-element.26.refs_0_, bf16[1024,768]{1,0:T(8,128)(2,1)S(1)} %get-tuple-element.24.refs_1_, bf16[8256,128]{1,0:T(8,128)(2,1)S(1)} %get-tuple-element.27.refs_2_.refs_0_), custom_call_target="tpu_custom_call" | custom-call | flops 1 | bytes 1 | tf_op jit(solution)/shard_map/grad_keep_2/pallas_call | solution.py:190
  35.3 2.0 %grad_keep_3.1.refs_2_.refs_0_ = bf16[8256,128]{1,0:T(8,128)(2,1)S(1)} custom-call(bf16[768,3072]{1,0:T(8,128)(2,1)S(1)} %get-tuple-element.26.refs_0_, bf16[1024,768]{1,0:T(8,128)(2,1)S(1)} %get-tuple-element.24.refs_1_, bf16[8256,128]{1,0:T(8,128)(2,1)S(1)} %grad_keep_2.1.refs_2_.refs_0_), custom_call_target="tpu_custom_call" | custom-call | flops 1 | bytes 1 | tf_op jit(solution)/shard_map/grad_keep_3/pallas_call | solution.py:190
  37.4 2.2 %grad_keep_0.1.refs_3_.refs_0_ = bf16[8256,128]{1,0:T(8,128)(2,1)S(1)} custom-call(bf16[768,5120]{1,0:T(8,128)(2,1)S(1)} %get-tuple-element.23.refs_0_, bf16[1024,768]{1,0:T(8,128)(2,1)S(1)} %get-tuple-element.24.refs_1_, bf16[8256,128]{1,0:T(8,128)(2,1)S(1)} %grad_keep_3.1.refs_2_.refs_0_), custom_call_target="tpu_custom_call" | custom-call | flops 1 | bytes 1 | tf_op jit(solution)/shard_map/grad_keep_0/pallas_call | solution.py:190
  39.5 15.7 %collective-permute-done.7.refs_2_ = bf16[6192,128]{1,0:T(8,128)(2,1)S(1)} collective-permute-done((bf16[6192,128]{1,0:T(8,128)(2,1)S(1)}, bf16[6192,128]{1,0:T(8,128)(2,1)S(1)}, u32[]{:S(2)}, u32[]{:S(2)}) %collective-permute-start.7) | collective-permute-done | bytes 1585184 | tf_op jit(solution)/shard_map/ppermute | solution.py:431
  55.2 1.2 sum_send_8.4.refs_3_
  56.4 1.9 %collective-permute-start.11 = (bf16[4128,128]{1,0:T(8,128)(2,1)S(1)}, bf16[4128,128]{1,0:T(8,128)(2,1)S(1)}, u32[]{:S(2)}, u32[]{:S(2)}) collective-permute-start(bf16[4128,128]{1,0:T(8,128)(2,1)S(1)} %sum_send_8.4.refs_3_), channel_id=1, source_target_pairs={{0,4},{1,5},{2,6},{3,7},{4,0},{5,1},{6,2},{7,3},{8,12},{9,13},{10,... | collective-permute-start | bytes 3170312 | tf_op jit(solution)/shard_map/ppermute | solution.py:441
  58.5 1.1 sum_send_8.5.refs_3_
  59.6 3.5 %collective-permute-start.10 = (bf16[4128,128]{1,0:T(8,128)(2,1)S(1)}, bf16[4128,128]{1,0:T(8,128)(2,1)S(1)}, u32[]{:S(2)}, u32[]{:S(2)}) collective-permute-start(bf16[4128,128]{1,0:T(8,128)(2,1)S(1)} %sum_send_8.5.refs_3_), channel_id=1, source_target_pairs={{0,12},{1,13},{2,14},{3,15},{4,8},{5,9},{6,10},{7,11},{8,4},{9,5},... | collective-permute-start | bytes 3170312 | tf_op jit(solution)/shard_map/ppermute | solution.py:441
  63.1 1.2 sum_send_8.6.refs_3_
  64.4 1.2 sum_send_8.7.refs_3_
  65.6 1.2 collective-permute-start.8
  67.2 0.4 sum_keep_8.5.refs_3_.refs_0_
  67.6 0.4 sum_keep_8.6.refs_3_.refs_0_
  67.9 0.4 sum_keep_8.7.refs_2_.refs_0_
  68.3 13.4 %collective-permute-done.11.refs_1_ = bf16[4128,128]{1,0:T(8,128)(2,1)S(1)} collective-permute-done((bf16[4128,128]{1,0:T(8,128)(2,1)S(1)}, bf16[4128,128]{1,0:T(8,128)(2,1)S(1)}, u32[]{:S(2)}, u32[]{:S(2)}) %collective-permute-start.11) | collective-permute-done | bytes 1056800 | tf_op jit(solution)/shard_map/ppermute | solution.py:441
  81.7 0.8 sum_send_4.4.refs_2_
  82.5 3.4 %collective-permute-start.15 = (bf16[2064,128]{1,0:T(8,128)(2,1)S(1)}, bf16[2064,128]{1,0:T(8,128)(2,1)S(1)}, u32[]{:S(2)}, u32[]{:S(2)}) collective-permute-start(bf16[2064,128]{1,0:T(8,128)(2,1)S(1)} %sum_send_4.4.refs_2_), channel_id=1, source_target_pairs={{0,12},{1,13},{2,14},{3,15},{4,8},{5,9},{6,10},{7,11},{8,4},{9,5},... | collective-permute-start | bytes 1585160 | tf_op jit(solution)/shard_map/ppermute | solution.py:441
  85.8 0.8 sum_send_4.5.refs_2_
  86.7 0.8 sum_send_4.6.refs_2_
  87.5 0.9 collective-permute-start.13
  88.4 0.8 sum_send_4.7.refs_2_
  89.2 0.8 collective-permute-start.12
  91.3 6.0 %collective-permute-done.15.refs_1_ = bf16[2064,128]{1,0:T(8,128)(2,1)S(1)} collective-permute-done((bf16[2064,128]{1,0:T(8,128)(2,1)S(1)}, bf16[2064,128]{1,0:T(8,128)(2,1)S(1)}, u32[]{:S(2)}, u32[]{:S(2)}) %collective-permute-start.15) | collective-permute-done | bytes 528416 | tf_op jit(solution)/shard_map/ppermute | solution.py:441
  98.2 1.1 collective-permute-start.17
  99.3 0.5 collective-permute-done.13.refs_1_
  101.4 3.2 %collective-permute-done.18.recv = bf16[1040,128]{1,0:T(8,128)(2,1)S(1)} collective-permute-done((bf16[1040,128]{1,0:T(8,128)(2,1)S(1)}, bf16[1040,128]{1,0:T(8,128)(2,1)S(1)}, u32[]{:S(2)}, u32[]{:S(2)}) %collective-permute-start.18) | collective-permute-done | bytes 266272 | tf_op jit(solution)/shard_map/ppermute | solution.py:441
  104.9 2.8 %collective-permute-start.21 = (bf16[528,128]{1,0:T(8,128)(2,1)S(1)}, bf16[528,128]{1,0:T(8,128)(2,1)S(1)}, u32[]{:S(2)}, u32[]{:S(2)}) collective-permute-start(bf16[528,128]{1,0:T(8,128)(2,1)S(1)} %get-tuple-element.31), channel_id=1, source_target_pairs={{0,16},{16,0},{32,48},{48,32},{64,80},{80,64},{96,112},{112,96},{1... | collective-permute-start | bytes 405512 | tf_op jit(solution)/shard_map/ppermute | solution.py:450
  107.8 1.5 %collective-permute-start.16 = (bf16[1040,128]{1,0:T(8,128)(2,1)S(1)}, bf16[1040,128]{1,0:T(8,128)(2,1)S(1)}, u32[]{:S(2)}, u32[]{:S(2)}) collective-permute-start(bf16[1040,128]{1,0:T(8,128)(2,1)S(1)} %sum_send_2.7.refs_2_), channel_id=1, source_target_pairs={{0,12},{1,13},{2,14},{3,15},{4,8},{5,9},{6,10},{7,11},{8,4},{9,5},... | collective-permute-start | bytes 798728 | tf_op jit(solution)/shard_map/ppermute | solution.py:441
  109.6 0.8 collective-permute-start.19
  111.0 1.5 %collective-permute-start.23 = (bf16[528,128]{1,0:T(8,128)(2,1)S(1)}, bf16[528,128]{1,0:T(8,128)(2,1)S(1)}, u32[]{:S(2)}, u32[]{:S(2)}) collective-permute-start(bf16[528,128]{1,0:T(8,128)(2,1)S(1)} %get-tuple-element.35), channel_id=1, source_target_pairs={{0,16},{16,0},{32,48},{48,32},{64,80},{80,64},{96,112},{112,96},{1... | collective-permute-start | bytes 405512 | tf_op jit(solution)/shard_map/ppermute | solution.py:450
  112.5 1.3 collective-permute-start.24
  114.0 2.7 %collective-permute-start.25 = (bf16[528,128]{1,0:T(8,128)(2,1)S(1)}, bf16[528,128]{1,0:T(8,128)(2,1)S(1)}, u32[]{:S(2)}, u32[]{:S(2)}) collective-permute-start(bf16[528,128]{1,0:T(8,128)(2,1)S(1)} %core_sum.5._), channel_id=1, source_target_pairs={{0,64},{16,80},{32,96},{48,112},{64,0},{80,16},{96,32},{112,48},{1... | collective-permute-start | bytes 405512 | tf_op jit(solution)/shard_map/ppermute | solution.py:453
  117.3 1.0 collective-permute-start.22
  118.4 2.8 %collective-permute-start.26 = (bf16[528,128]{1,0:T(8,128)(2,1)S(1)}, bf16[528,128]{1,0:T(8,128)(2,1)S(1)}, u32[]{:S(2)}, u32[]{:S(2)}) collective-permute-start(bf16[528,128]{1,0:T(8,128)(2,1)S(1)} %core_sum.6._), channel_id=1, source_target_pairs={{0,96},{16,112},{32,0},{48,16},{64,32},{80,48},{96,64},{112,80},{1... | collective-permute-start | bytes 405512 | tf_op jit(solution)/shard_map/ppermute | solution.py:453
  121.2 1.8 %collective-permute-done.25.b = bf16[528,128]{1,0:T(8,128)(2,1)S(1)} collective-permute-done((bf16[528,128]{1,0:T(8,128)(2,1)S(1)}, bf16[528,128]{1,0:T(8,128)(2,1)S(1)}, u32[]{:S(2)}, u32[]{:S(2)}) %collective-permute-start.25) | collective-permute-done | bytes 135200 | tf_op jit(solution)/shard_map/ppermute | solution.py:453
  123.0 1.1 collective-permute-done.26.c
  124.2 0.5 adam_weight.1
  124.6 2.5 %collective-permute-start.28 = (bf16[64,1024]{1,0:T(8,128)(2,1)S(1)}, bf16[64,1024]{1,0:T(8,128)(2,1)S(1)}, u32[]{:S(2)}, u32[]{:S(2)}) collective-permute-start(bf16[64,1024]{1,0:T(8,128)(2,1)S(1)} %get-tuple-element.40.refs_0_), channel_id=1, source_target_pairs={{0,64},{16,80},{32,96},{48,112},{64,0},{80,16},{96,32},{112,48},{1... | collective-permute-start | bytes 393224 | tf_op jit(solution)/shard_map/ppermute | solution.py:455
  127.1 1.6 %collective-permute-start.27 = (bf16[64,1024]{1,0:T(8,128)(2,1)S(1)}, bf16[64,1024]{1,0:T(8,128)(2,1)S(1)}, u32[]{:S(2)}, u32[]{:S(2)}) collective-permute-start(bf16[64,1024]{1,0:T(8,128)(2,1)S(1)} %get-tuple-element.40.refs_0_), channel_id=1, source_target_pairs={{0,32},{16,48},{32,64},{48,80},{64,96},{80,112},{96,0},{112,16},{1... | collective-permute-start | bytes 393224 | tf_op jit(solution)/shard_map/ppermute | solution.py:455
  128.7 1.1 collective-permute-start.29
  129.8 1.6 %collective-permute-start.30 = (bf16[64,1024]{1,0:T(8,128)(2,1)S(1)}, bf16[64,1024]{1,0:T(8,128)(2,1)S(1)}, u32[]{:S(2)}, u32[]{:S(2)}) collective-permute-start(bf16[64,1024]{1,0:T(8,128)(2,1)S(1)} %get-tuple-element.40.refs_0_), channel_id=1, source_target_pairs={{0,16},{16,0},{32,48},{48,32},{64,80},{80,64},{96,112},{112,96},{1... | collective-permute-start | bytes 393224 | tf_op jit(solution)/shard_map/ppermute | solution.py:458
  131.4 1.0 adam.1
  132.4 0.8 collective-permute-start.32
  133.2 0.7 collective-permute-done.27.refs_1_
  133.9 1.2 collective-permute-start.31
  135.1 0.8 collective-permute-start.33
  136.1 0.8 collective-permute-done.33.refs_7_
  137.0 1.1 gather.1
  (62 shorter events, 6.7 us)
Async XLA Ops:
  4.6 14.7 %collective-permute-start.6 = (bf16[2064,128]{1,0:T(8,128)(2,1)S(1)}, bf16[2064,128]{1,0:T(8,128)(2,1)S(1)}, u32[]{:S(2)}, u32[]{:S(2)}) collective-permute-start(bf16[2064,128]{1,0:T(8,128)(2,1)S(1)} %get-tuple-element.25.refs_2_), channel_id=1, source_target_pairs={{0,3},{1,2},{2,1},{3,0},{4,7},{5,6},{6,5},{7,4},{8,11},{9,10},{10,... | collective-permute-start | bytes 1585160 | tf_op jit(solution)/shard_map/ppermute | solution.py:425
  8.8 14.9 %collective-permute-start.4 = (bf16[2064,128]{1,0:T(8,128)(2,1)S(1)}, bf16[2064,128]{1,0:T(8,128)(2,1)S(1)}, u32[]{:S(2)}, u32[]{:S(2)}) collective-permute-start(bf16[2064,128]{1,0:T(8,128)(2,1)S(1)} %grad_send_2.2.refs_2_), channel_id=1, source_target_pairs={{0,4},{1,5},{2,6},{3,7},{4,0},{5,1},{6,2},{7,3},{8,12},{9,13},{10,... | collective-permute-start | bytes 1585160 | tf_op jit(solution)/shard_map/ppermute | solution.py:425
  11.3 15.9 %collective-permute-start.2 = (bf16[2064,128]{1,0:T(8,128)(2,1)S(1)}, bf16[2064,128]{1,0:T(8,128)(2,1)S(1)}, u32[]{:S(2)}, u32[]{:S(2)}) collective-permute-start(bf16[2064,128]{1,0:T(8,128)(2,1)S(1)} %grad_send_3.2.refs_2_), channel_id=1, source_target_pairs={{0,12},{1,13},{2,14},{3,15},{4,8},{5,9},{6,10},{7,11},{8,4},{9,5},... | collective-permute-start | bytes 1585160 | tf_op jit(solution)/shard_map/ppermute | solution.py:425
  14.9 14.6 %collective-permute-start = (bf16[2064,128]{1,0:T(8,128)(2,1)S(1)}, bf16[2064,128]{1,0:T(8,128)(2,1)S(1)}, u32[]{:S(2)}, u32[]{:S(2)}) collective-permute-start(bf16[2064,128]{1,0:T(8,128)(2,1)S(1)} %grad_send_0.2.refs_2_), channel_id=1, source_target_pairs={{0,1},{1,0},{2,3},{3,2},{4,5},{5,4},{6,7},{7,6},{8,9},{9,8},{10,11... | collective-permute-start | bytes 1585160 | tf_op jit(solution)/shard_map/ppermute | solution.py:425
  19.3 35.9 %collective-permute-start.7 = (bf16[6192,128]{1,0:T(8,128)(2,1)S(1)}, bf16[6192,128]{1,0:T(8,128)(2,1)S(1)}, u32[]{:S(2)}, u32[]{:S(2)}) collective-permute-start(bf16[6192,128]{1,0:T(8,128)(2,1)S(1)} %hold.8), channel_id=1, source_target_pairs={{0,3},{1,2},{2,1},{3,0},{4,7},{5,6},{6,5},{7,4},{8,11},{9,10},{10,... | collective-permute-start | bytes 4755464 | tf_op jit(solution)/shard_map/ppermute | solution.py:431
  23.7 34.8 %collective-permute-start.5 = (bf16[6192,128]{1,0:T(8,128)(2,1)S(1)}, bf16[6192,128]{1,0:T(8,128)(2,1)S(1)}, u32[]{:S(2)}, u32[]{:S(2)}) collective-permute-start(bf16[6192,128]{1,0:T(8,128)(2,1)S(1)} %hold.7), channel_id=1, source_target_pairs={{0,4},{1,5},{2,6},{3,7},{4,0},{5,1},{6,2},{7,3},{8,12},{9,13},{10,... | collective-permute-start | bytes 4755464 | tf_op jit(solution)/shard_map/ppermute | solution.py:431
  27.2 35.9 %collective-permute-start.3 = (bf16[6192,128]{1,0:T(8,128)(2,1)S(1)}, bf16[6192,128]{1,0:T(8,128)(2,1)S(1)}, u32[]{:S(2)}, u32[]{:S(2)}) collective-permute-start(bf16[6192,128]{1,0:T(8,128)(2,1)S(1)} %hold.6), channel_id=1, source_target_pairs={{0,12},{1,13},{2,14},{3,15},{4,8},{5,9},{6,10},{7,11},{8,4},{9,5},... | collective-permute-start | bytes 4755464 | tf_op jit(solution)/shard_map/ppermute | solution.py:431
  29.5 34.9 %collective-permute-start.1 = (bf16[6192,128]{1,0:T(8,128)(2,1)S(1)}, bf16[6192,128]{1,0:T(8,128)(2,1)S(1)}, u32[]{:S(2)}, u32[]{:S(2)}) collective-permute-start(bf16[6192,128]{1,0:T(8,128)(2,1)S(1)} %hold.5.refs_2_), channel_id=1, source_target_pairs={{0,1},{1,0},{2,3},{3,2},{4,5},{5,4},{6,7},{7,6},{8,9},{9,8},{10,11... | collective-permute-start | bytes 4755464 | tf_op jit(solution)/shard_map/ppermute | solution.py:431
  56.4 25.3 %collective-permute-start.11 = (bf16[4128,128]{1,0:T(8,128)(2,1)S(1)}, bf16[4128,128]{1,0:T(8,128)(2,1)S(1)}, u32[]{:S(2)}, u32[]{:S(2)}) collective-permute-start(bf16[4128,128]{1,0:T(8,128)(2,1)S(1)} %sum_send_8.4.refs_3_), channel_id=1, source_target_pairs={{0,4},{1,5},{2,6},{3,7},{4,0},{5,1},{6,2},{7,3},{8,12},{9,13},{10,... | collective-permute-start | bytes 3170312 | tf_op jit(solution)/shard_map/ppermute | solution.py:441
  59.6 26.2 %collective-permute-start.10 = (bf16[4128,128]{1,0:T(8,128)(2,1)S(1)}, bf16[4128,128]{1,0:T(8,128)(2,1)S(1)}, u32[]{:S(2)}, u32[]{:S(2)}) collective-permute-start(bf16[4128,128]{1,0:T(8,128)(2,1)S(1)} %sum_send_8.5.refs_3_), channel_id=1, source_target_pairs={{0,12},{1,13},{2,14},{3,15},{4,8},{5,9},{6,10},{7,11},{8,4},{9,5},... | collective-permute-start | bytes 3170312 | tf_op jit(solution)/shard_map/ppermute | solution.py:441
  64.3 22.4 %collective-permute-start.9 = (bf16[4128,128]{1,0:T(8,128)(2,1)S(1)}, bf16[4128,128]{1,0:T(8,128)(2,1)S(1)}, u32[]{:S(2)}, u32[]{:S(2)}) collective-permute-start(bf16[4128,128]{1,0:T(8,128)(2,1)S(1)} %sum_send_8.6.refs_3_), channel_id=1, source_target_pairs={{0,1},{1,0},{2,3},{3,2},{4,5},{5,4},{6,7},{7,6},{8,9},{9,8},{10,11... | collective-permute-start | bytes 3170312 | tf_op jit(solution)/shard_map/ppermute | solution.py:441
  65.6 22.8 %collective-permute-start.8 = (bf16[4128,128]{1,0:T(8,128)(2,1)S(1)}, bf16[4128,128]{1,0:T(8,128)(2,1)S(1)}, u32[]{:S(2)}, u32[]{:S(2)}) collective-permute-start(bf16[4128,128]{1,0:T(8,128)(2,1)S(1)} %sum_send_8.7.refs_3_), channel_id=1, source_target_pairs={{0,3},{1,2},{2,1},{3,0},{4,7},{5,6},{6,5},{7,4},{8,11},{9,10},{10,... | collective-permute-start | bytes 3170312 | tf_op jit(solution)/shard_map/ppermute | solution.py:441
  82.5 14.9 %collective-permute-start.15 = (bf16[2064,128]{1,0:T(8,128)(2,1)S(1)}, bf16[2064,128]{1,0:T(8,128)(2,1)S(1)}, u32[]{:S(2)}, u32[]{:S(2)}) collective-permute-start(bf16[2064,128]{1,0:T(8,128)(2,1)S(1)} %sum_send_4.4.refs_2_), channel_id=1, source_target_pairs={{0,12},{1,13},{2,14},{3,15},{4,8},{5,9},{6,10},{7,11},{8,4},{9,5},... | collective-permute-start | bytes 1585160 | tf_op jit(solution)/shard_map/ppermute | solution.py:441
  86.6 11.2 %collective-permute-start.14 = (bf16[2064,128]{1,0:T(8,128)(2,1)S(1)}, bf16[2064,128]{1,0:T(8,128)(2,1)S(1)}, u32[]{:S(2)}, u32[]{:S(2)}) collective-permute-start(bf16[2064,128]{1,0:T(8,128)(2,1)S(1)} %sum_send_4.5.refs_2_), channel_id=1, source_target_pairs={{0,1},{1,0},{2,3},{3,2},{4,5},{5,4},{6,7},{7,6},{8,9},{9,8},{10,11... | collective-permute-start | bytes 1585160 | tf_op jit(solution)/shard_map/ppermute | solution.py:441
  87.5 12.4 %collective-permute-start.13 = (bf16[2064,128]{1,0:T(8,128)(2,1)S(1)}, bf16[2064,128]{1,0:T(8,128)(2,1)S(1)}, u32[]{:S(2)}, u32[]{:S(2)}) collective-permute-start(bf16[2064,128]{1,0:T(8,128)(2,1)S(1)} %sum_send_4.6.refs_2_), channel_id=1, source_target_pairs={{0,3},{1,2},{2,1},{3,0},{4,7},{5,6},{6,5},{7,4},{8,11},{9,10},{10,... | collective-permute-start | bytes 1585160 | tf_op jit(solution)/shard_map/ppermute | solution.py:441
  89.2 11.1 %collective-permute-start.12 = (bf16[2064,128]{1,0:T(8,128)(2,1)S(1)}, bf16[2064,128]{1,0:T(8,128)(2,1)S(1)}, u32[]{:S(2)}, u32[]{:S(2)}) collective-permute-start(bf16[2064,128]{1,0:T(8,128)(2,1)S(1)} %sum_send_4.7.refs_2_), channel_id=1, source_target_pairs={{0,4},{1,5},{2,6},{3,7},{4,0},{5,1},{6,2},{7,3},{8,12},{9,13},{10,... | collective-permute-start | bytes 1585160 | tf_op jit(solution)/shard_map/ppermute | solution.py:441
  97.7 6.9 %collective-permute-start.18 = (bf16[1040,128]{1,0:T(8,128)(2,1)S(1)}, bf16[1040,128]{1,0:T(8,128)(2,1)S(1)}, u32[]{:S(2)}, u32[]{:S(2)}) collective-permute-start(bf16[1040,128]{1,0:T(8,128)(2,1)S(1)} %sum_send_2.4.refs_2_), channel_id=1, source_target_pairs={{0,1},{1,0},{2,3},{3,2},{4,5},{5,4},{6,7},{7,6},{8,9},{9,8},{10,11... | collective-permute-start | bytes 798728 | tf_op jit(solution)/shard_map/ppermute | solution.py:441
  98.2 11.1 %collective-permute-start.17 = (bf16[1040,128]{1,0:T(8,128)(2,1)S(1)}, bf16[1040,128]{1,0:T(8,128)(2,1)S(1)}, u32[]{:S(2)}, u32[]{:S(2)}) collective-permute-start(bf16[1040,128]{1,0:T(8,128)(2,1)S(1)} %sum_send_2.5.refs_2_), channel_id=1, source_target_pairs={{0,3},{1,2},{2,1},{3,0},{4,7},{5,6},{6,5},{7,4},{8,11},{9,10},{10,... | collective-permute-start | bytes 798728 | tf_op jit(solution)/shard_map/ppermute | solution.py:441
  100.2 10.4 %collective-permute-start.20 = (bf16[1040,128]{1,0:T(8,128)(2,1)S(1)}, bf16[1040,128]{1,0:T(8,128)(2,1)S(1)}, u32[]{:S(2)}, u32[]{:S(2)}) collective-permute-start(bf16[1040,128]{1,0:T(8,128)(2,1)S(1)} %sum_send_2.6.refs_2_), channel_id=1, source_target_pairs={{0,4},{1,5},{2,6},{3,7},{4,0},{5,1},{6,2},{7,3},{8,12},{9,13},{10,... | collective-permute-start | bytes 798728 | tf_op jit(solution)/shard_map/ppermute | solution.py:441
  104.9 5.5 %collective-permute-start.21 = (bf16[528,128]{1,0:T(8,128)(2,1)S(1)}, bf16[528,128]{1,0:T(8,128)(2,1)S(1)}, u32[]{:S(2)}, u32[]{:S(2)}) collective-permute-start(bf16[528,128]{1,0:T(8,128)(2,1)S(1)} %get-tuple-element.31), channel_id=1, source_target_pairs={{0,16},{16,0},{32,48},{48,32},{64,80},{80,64},{96,112},{112,96},{1... | collective-permute-start | bytes 405512 | tf_op jit(solution)/shard_map/ppermute | solution.py:450
  107.8 9.2 %collective-permute-start.16 = (bf16[1040,128]{1,0:T(8,128)(2,1)S(1)}, bf16[1040,128]{1,0:T(8,128)(2,1)S(1)}, u32[]{:S(2)}, u32[]{:S(2)}) collective-permute-start(bf16[1040,128]{1,0:T(8,128)(2,1)S(1)} %sum_send_2.7.refs_2_), channel_id=1, source_target_pairs={{0,12},{1,13},{2,14},{3,15},{4,8},{5,9},{6,10},{7,11},{8,4},{9,5},... | collective-permute-start | bytes 798728 | tf_op jit(solution)/shard_map/ppermute | solution.py:441
  109.6 4.2 %collective-permute-start.19 = (bf16[528,128]{1,0:T(8,128)(2,1)S(1)}, bf16[528,128]{1,0:T(8,128)(2,1)S(1)}, u32[]{:S(2)}, u32[]{:S(2)}) collective-permute-start(bf16[528,128]{1,0:T(8,128)(2,1)S(1)} %get-tuple-element.30), channel_id=1, source_target_pairs={{0,16},{16,0},{32,48},{48,32},{64,80},{80,64},{96,112},{112,96},{1... | collective-permute-start | bytes 405512 | tf_op jit(solution)/shard_map/ppermute | solution.py:450
  110.6 13.6 %copy-start = (f32[64,1024]{1,0:T(8,128)S(1)}, f32[64,1024]{1,0:T(8,128)}, u32[]{:S(2)}) copy-start(f32[64,1024]{1,0:T(8,128)} %master.3) | copy-start | bytes 786436
  110.6 13.6 %copy-start.1 = (f32[64,1024]{1,0:T(8,128)S(1)}, f32[64,1024]{1,0:T(8,128)}, u32[]{:S(2)}) copy-start(f32[64,1024]{1,0:T(8,128)} %moment.3) | copy-start | bytes 786436
  110.6 13.6 %copy-start.2 = (f32[64,1024]{1,0:T(8,128)S(1)}, f32[64,1024]{1,0:T(8,128)}, u32[]{:S(2)}) copy-start(f32[64,1024]{1,0:T(8,128)} %second.3) | copy-start | bytes 786436
  111.0 7.2 %collective-permute-start.23 = (bf16[528,128]{1,0:T(8,128)(2,1)S(1)}, bf16[528,128]{1,0:T(8,128)(2,1)S(1)}, u32[]{:S(2)}, u32[]{:S(2)}) collective-permute-start(bf16[528,128]{1,0:T(8,128)(2,1)S(1)} %get-tuple-element.35), channel_id=1, source_target_pairs={{0,16},{16,0},{32,48},{48,32},{64,80},{80,64},{96,112},{112,96},{1... | collective-permute-start | bytes 405512 | tf_op jit(solution)/shard_map/ppermute | solution.py:450
  112.5 10.5 %collective-permute-start.24 = (bf16[528,128]{1,0:T(8,128)(2,1)S(1)}, bf16[528,128]{1,0:T(8,128)(2,1)S(1)}, u32[]{:S(2)}, u32[]{:S(2)}) collective-permute-start(bf16[528,128]{1,0:T(8,128)(2,1)S(1)} %core_sum.4._), channel_id=1, source_target_pairs={{0,32},{16,48},{32,64},{48,80},{64,96},{80,112},{96,0},{112,16},{1... | collective-permute-start | bytes 405512 | tf_op jit(solution)/shard_map/ppermute | solution.py:453
  114.0 9.0 %collective-permute-start.25 = (bf16[528,128]{1,0:T(8,128)(2,1)S(1)}, bf16[528,128]{1,0:T(8,128)(2,1)S(1)}, u32[]{:S(2)}, u32[]{:S(2)}) collective-permute-start(bf16[528,128]{1,0:T(8,128)(2,1)S(1)} %core_sum.5._), channel_id=1, source_target_pairs={{0,64},{16,80},{32,96},{48,112},{64,0},{80,16},{96,32},{112,48},{1... | collective-permute-start | bytes 405512 | tf_op jit(solution)/shard_map/ppermute | solution.py:453
  117.3 3.9 %collective-permute-start.22 = (bf16[528,128]{1,0:T(8,128)(2,1)S(1)}, bf16[528,128]{1,0:T(8,128)(2,1)S(1)}, u32[]{:S(2)}, u32[]{:S(2)}) collective-permute-start(bf16[528,128]{1,0:T(8,128)(2,1)S(1)} %get-tuple-element.34), channel_id=1, source_target_pairs={{0,16},{16,0},{32,48},{48,32},{64,80},{80,64},{96,112},{112,96},{1... | collective-permute-start | bytes 405512 | tf_op jit(solution)/shard_map/ppermute | solution.py:450
  118.4 5.8 %collective-permute-start.26 = (bf16[528,128]{1,0:T(8,128)(2,1)S(1)}, bf16[528,128]{1,0:T(8,128)(2,1)S(1)}, u32[]{:S(2)}, u32[]{:S(2)}) collective-permute-start(bf16[528,128]{1,0:T(8,128)(2,1)S(1)} %core_sum.6._), channel_id=1, source_target_pairs={{0,96},{16,112},{32,0},{48,16},{64,32},{80,48},{96,64},{112,80},{1... | collective-permute-start | bytes 405512 | tf_op jit(solution)/shard_map/ppermute | solution.py:453
  124.6 7.8 %collective-permute-start.28 = (bf16[64,1024]{1,0:T(8,128)(2,1)S(1)}, bf16[64,1024]{1,0:T(8,128)(2,1)S(1)}, u32[]{:S(2)}, u32[]{:S(2)}) collective-permute-start(bf16[64,1024]{1,0:T(8,128)(2,1)S(1)} %get-tuple-element.40.refs_0_), channel_id=1, source_target_pairs={{0,64},{16,80},{32,96},{48,112},{64,0},{80,16},{96,32},{112,48},{1... | collective-permute-start | bytes 393224 | tf_op jit(solution)/shard_map/ppermute | solution.py:455
  127.1 6.8 %collective-permute-start.27 = (bf16[64,1024]{1,0:T(8,128)(2,1)S(1)}, bf16[64,1024]{1,0:T(8,128)(2,1)S(1)}, u32[]{:S(2)}, u32[]{:S(2)}) collective-permute-start(bf16[64,1024]{1,0:T(8,128)(2,1)S(1)} %get-tuple-element.40.refs_0_), channel_id=1, source_target_pairs={{0,32},{16,48},{32,64},{48,80},{64,96},{80,112},{96,0},{112,16},{1... | collective-permute-start | bytes 393224 | tf_op jit(solution)/shard_map/ppermute | solution.py:455
  128.7 6.4 %collective-permute-start.29 = (bf16[64,1024]{1,0:T(8,128)(2,1)S(1)}, bf16[64,1024]{1,0:T(8,128)(2,1)S(1)}, u32[]{:S(2)}, u32[]{:S(2)}) collective-permute-start(bf16[64,1024]{1,0:T(8,128)(2,1)S(1)} %get-tuple-element.40.refs_0_), channel_id=1, source_target_pairs={{0,96},{16,112},{32,0},{48,16},{64,32},{80,48},{96,64},{112,80},{1... | collective-permute-start | bytes 393224 | tf_op jit(solution)/shard_map/ppermute | solution.py:455
  129.8 6.2 %collective-permute-start.30 = (bf16[64,1024]{1,0:T(8,128)(2,1)S(1)}, bf16[64,1024]{1,0:T(8,128)(2,1)S(1)}, u32[]{:S(2)}, u32[]{:S(2)}) collective-permute-start(bf16[64,1024]{1,0:T(8,128)(2,1)S(1)} %get-tuple-element.40.refs_0_), channel_id=1, source_target_pairs={{0,16},{16,0},{32,48},{48,32},{64,80},{80,64},{96,112},{112,96},{1... | collective-permute-start | bytes 393224 | tf_op jit(solution)/shard_map/ppermute | solution.py:458
  132.4 3.6 %collective-permute-start.32 = (bf16[64,1024]{1,0:T(8,128)(2,1)S(1)}, bf16[64,1024]{1,0:T(8,128)(2,1)S(1)}, u32[]{:S(2)}, u32[]{:S(2)}) collective-permute-start(bf16[64,1024]{1,0:T(8,128)(2,1)S(1)} %collective-permute-done.28.refs_2_), channel_id=1, source_target_pairs={{0,16},{16,0},{32,48},{48,32},{64,80},{80,64},{96,112},{112,96},{1... | collective-permute-start | bytes 393224 | tf_op jit(solution)/shard_map/ppermute | solution.py:458
  133.9 2.2 %collective-permute-start.31 = (bf16[64,1024]{1,0:T(8,128)(2,1)S(1)}, bf16[64,1024]{1,0:T(8,128)(2,1)S(1)}, u32[]{:S(2)}, u32[]{:S(2)}) collective-permute-start(bf16[64,1024]{1,0:T(8,128)(2,1)S(1)} %collective-permute-done.27.refs_1_), channel_id=1, source_target_pairs={{0,16},{16,0},{32,48},{48,32},{64,80},{80,64},{96,112},{112,96},{1... | collective-permute-start | bytes 393224 | tf_op jit(solution)/shard_map/ppermute | solution.py:458
  135.1 1.8 %collective-permute-start.33 = (bf16[64,1024]{1,0:T(8,128)(2,1)S(1)}, bf16[64,1024]{1,0:T(8,128)(2,1)S(1)}, u32[]{:S(2)}, u32[]{:S(2)}) collective-permute-start(bf16[64,1024]{1,0:T(8,128)(2,1)S(1)} %hold.9.refs_3_), channel_id=1, source_target_pairs={{0,16},{16,0},{32,48},{48,32},{64,80},{80,64},{96,112},{112,96},{1... | collective-permute-start | bytes 393224 | tf_op jit(solution)/shard_map/ppermute | solution.py:458
